TPU v7x, 256 devices: a whole 4x4x8 slice. The times are simulated.
256 devices in a mesh: dp: 4 (over z_hi), field: 64 (over z_lo, y, x, core).
Axes of the slice: x: 4, y: 4, z: 8 (z_hi: 4, z_lo: 2; z = z_hi * 2 + z_lo), core: 2. Of those that a mesh axis runs over, the one named last changes fastest.
Arguments:
- inputs: bfloat16 [12, 512, 64, 1024], P('dp', 'field'), may hold values from -6 to 6
- cotangent: bfloat16 [12, 512, 64, 1024], P('dp', 'field'), may hold values from -6 to 6
- spec_weight: float32 [1024, 2, 64, 64], P('field'), may hold values from -0.75 to 0.75
- point_weight: bfloat16 [64, 64], replicated, may hold values from -0.75 to 0.75
Outputs:
- input_grad: bfloat16 [12, 512, 64, 1024], P('dp', 'field')
- spec_grad: float32 [1024, 2, 64, 64], P('field')
- point_grad: float32 [64, 64], replicated
All inputs are finite; a program needn't handle non-finite values.
Results may differ from a plain program's by a relative error of at most 0.018.
Values may be sent and summed in bfloat16 or wider, within the bound.
No kernel may reach another device: no remote copies, remote signals or barrier semaphores. Data moves between devices by JAX's collectives and lax.ppermute only.
A program may use at most 64 MiB of HBM per device.

v0:
```python
import math

import jax
import jax.numpy as jnp
from jax import lax
from jax.sharding import PartitionSpec as P

DEPTH = 512
DURATION = 1024
DMODES = 32
TMODES = 32


def time_table(count_t, modes):
    times = jnp.arange(count_t, dtype=jnp.int32)
    orders = jnp.arange(modes, dtype=jnp.int32)
    phase = jnp.mod(times[:, None] * orders[None, :], count_t).astype(jnp.float32) * (
        2.0 * math.pi / count_t
    )
    return jnp.concatenate([jnp.cos(phase), -jnp.sin(phase)], axis=1).astype(jnp.bfloat16)


def depth_table(positions, count_x, modes):
    orders = jnp.arange(modes, dtype=jnp.int32)
    freqs = jnp.where(orders < modes // 2, orders, orders - modes)
    phase = jnp.mod(freqs[:, None] * positions[None, :], count_x).astype(jnp.float32) * (
        2.0 * math.pi / count_x
    )
    return (jnp.cos(phase), jnp.sin(phase))


def precise(form, left, right):
    return jnp.einsum(form, left, right, precision=lax.Precision.HIGHEST)


def forward_depth(rows, cosines, sine_vals, modes):
    real_part = rows[..., :modes]
    imag_part = rows[..., modes:]
    spec_real = precise("kx,bxcm->kmbc", cosines, real_part) + precise(
        "kx,bxcm->kmbc", sine_vals, imag_part
    )
    spec_imag = precise("kx,bxcm->kmbc", cosines, imag_part) - precise(
        "kx,bxcm->kmbc", sine_vals, real_part
    )
    stacked = jnp.stack([spec_real, spec_imag], axis=2)
    return stacked.reshape(cosines.shape[0] * modes, 2, rows.shape[0], rows.shape[2])


def inverse_depth(spectrum, cosines, sine_vals, modes):
    shaped = spectrum.reshape(cosines.shape[0], modes, 2, spectrum.shape[2], spectrum.shape[3])
    spec_real = shaped[:, :, 0]
    spec_imag = shaped[:, :, 1]
    row_real = precise("kx,kmbc->bxcm", cosines, spec_real) - precise(
        "kx,kmbc->bxcm", sine_vals, spec_imag
    )
    row_imag = precise("kx,kmbc->bxcm", sine_vals, spec_real) + precise(
        "kx,kmbc->bxcm", cosines, spec_imag
    )
    return jnp.concatenate([row_real, row_imag], axis=3)


def mix(spectrum, weights):
    s_real, s_imag = (spectrum[:, 0], spectrum[:, 1])
    w_real, w_imag = (weights[:, 0], weights[:, 1])
    out_real = precise("pbc,pco->pbo", s_real, w_real) - precise("pbc,pco->pbo", s_imag, w_imag)
    out_imag = precise("pbc,pco->pbo", s_real, w_imag) + precise("pbc,pco->pbo", s_imag, w_real)
    return jnp.stack([out_real, out_imag], axis=1)


def mix_adjoint(dspec, weights):
    d_real, d_imag = (dspec[:, 0], dspec[:, 1])
    w_real, w_imag = (weights[:, 0], weights[:, 1])
    out_real = precise("pbo,pco->pbc", d_real, w_real) + precise("pbo,pco->pbc", d_imag, w_imag)
    out_imag = precise("pbo,pco->pbc", d_imag, w_real) - precise("pbo,pco->pbc", d_real, w_imag)
    return jnp.stack([out_real, out_imag], axis=1)


def weight_term(spectrum, dspec):
    s_real, s_imag = (spectrum[:, 0], spectrum[:, 1])
    d_real, d_imag = (dspec[:, 0], dspec[:, 1])
    g_real = precise("pbc,pbo->pco", s_real, d_real) + precise("pbc,pbo->pco", s_imag, d_imag)
    g_imag = precise("pbc,pbo->pco", s_real, d_imag) - precise("pbc,pbo->pco", s_imag, d_real)
    return jnp.stack([g_real, g_imag], axis=1)


def local(inputs, cotangent, spec_weight, point_weight):
    samples, slab, channels, duration = inputs.shape
    table = time_table(duration, TMODES)
    scale = 1.0 / math.sqrt(DEPTH * DURATION)
    inv_scale = 1.0 / math.sqrt(DMODES * TMODES)
    local_pos = lax.axis_index("field") * slab + jnp.arange(slab, dtype=jnp.int32)
    local_cos, local_sin = depth_table(local_pos, DEPTH, DMODES)

    def to_owner(rows):
        partial_value = forward_depth(rows, local_cos, local_sin, TMODES)
        return lax.psum_scatter(partial_value, "field", scatter_dimension=0, tiled=True)

    def from_owner(owned):
        whole = lax.all_gather(owned, "field", axis=0, tiled=True)
        return inverse_depth(whole, local_cos, local_sin, TMODES).astype(jnp.bfloat16)

    coeffs = jnp.einsum("bxct,tj->bxcj", inputs, table, preferred_element_type=jnp.float32) * scale
    spectrum = to_owner(coeffs)
    mixed = mix(spectrum, spec_weight)
    spec_rows = from_owner(mixed)
    spatial = (
        jnp.einsum("bxcj,tj->bxct", spec_rows, table, preferred_element_type=jnp.float32)
        * inv_scale
    )
    pre = spatial + jnp.einsum(
        "bxct,co->bxot", inputs, point_weight, preferred_element_type=jnp.float32
    )
    slope = jax.vjp(jax.nn.gelu, pre)[1](cotangent.astype(jnp.float32))[0]
    dpre = slope.astype(jnp.bfloat16)
    point_local = jnp.einsum("bxct,bxot->co", inputs, dpre, preferred_element_type=jnp.float32)
    drows = jnp.einsum("bxot,tj->bxoj", dpre, table, preferred_element_type=jnp.float32) * inv_scale
    dmixed = to_owner(drows)
    spec_local = weight_term(spectrum, dmixed)
    dspec = mix_adjoint(dmixed, spec_weight)
    dcoeffs = from_owner(dspec)
    grad_in = (
        jnp.einsum("bxcj,tj->bxct", dcoeffs, table, preferred_element_type=jnp.float32) * scale
    )
    grad_in = grad_in + jnp.einsum(
        "bxot,co->bxct", dpre, point_weight, preferred_element_type=jnp.float32
    )
    input_grad = grad_in.astype(jnp.bfloat16)
    point_total = lax.psum(point_local, ("dp", "field"))
    spec_total = lax.psum(spec_local.astype(jnp.bfloat16), "dp").astype(jnp.float32)
    batch = lax.axis_size("dp") * samples
    spec_grad = spec_total / math.sqrt(batch * DEPTH)
    point_grad = point_total / math.sqrt(batch * DEPTH * DURATION)
    return (input_grad, spec_grad, point_grad)


def solution(mesh):
    in_specs = (
        P("dp", "field", None, None),
        P("dp", "field", None, None),
        P("field", None, None, None),
        P(),
    )
    out_specs = (P("dp", "field", None, None), P("field", None, None, None), P())
    return jax.shard_map(local, mesh=mesh, in_specs=in_specs, out_specs=out_specs, check_vma=False)
```

profile of v0, /device:TPU:32, one launch (start us, length us, event | category | flops | bytes accessed | tf_op | source)
XLA Modules:
  0.0 1492.8 jit_solution(18409350041912385997)
XLA Ops:
  13.1 2.6 fusion.74
  20.9 4.4 copy.80
  27.3 560.8 %all-reduce.8.cloned.1.call-done = f32[1024,2,3,64]{3,1,2,0:T(2,128)} async-done(((f32[1024,2,3,64]{3,1,2,0:T(2,128)}), f32[1024,2,3,64]{3,1,2,0:T(2,128)}) %all-reduce.8.cloned.1.call-update) | async-done | bytes 1572880
  596.0 108.5 %all-gather.3.cloned.1.call-done = f32[1024,2,3,64]{3,2,0,1:T(4,128)} async-done(((f32[16,2,3,64]{3,2,0,1:T(4,128)}), f32[1024,2,3,64]{3,2,0,1:T(4,128)}) %all-gather.3.cloned.1.call-update) | async-done | bytes 1572880 | tf_op jit(solution)/shard_map/all_gather | solution.py:99
  704.5 2.9 fusion.188
  707.5 1.8 fusion.12
  709.3 1.8 fusion.13
  711.2 1.8 fusion.35
  713.1 1.8 fusion.34
  716.9 6.1 fusion.2
  733.1 4.1 copy.95
  737.5 559.1 %all-reduce.10.cloned.1.call-done = f32[1024,2,3,64]{3,1,2,0:T(2,128)} async-done(((f32[1024,2,3,64]{3,1,2,0:T(2,128)}), f32[1024,2,3,64]{3,1,2,0:T(2,128)}) %all-reduce.10.cloned.1.call-update) | async-done | bytes 1572880
  1297.5 2.0 fusion.45
  1300.5 2.0 fusion.47
  1306.6 2.0 fusion.36
  1308.5 2.0 fusion.37
  1311.2 2.8 convolution_bitcast_fusion
  1314.0 79.8 %psum.15 = f32[64,64]{0,1:T(8,128)S(1)} all-reduce(f32[64,64]{0,1:T(8,128)S(1)} %convolution_bitcast_fusion), channel_id=1, replica_groups=mesh['dp'=4,'field'=64] {'dp','field'}, use_global_device_ids=true, to_apply=%region_3.4 | all-reduce | flops 4096 | bytes 32768 | tf_op jit(solution)/shard_map/psum | solution.py:128
  1396.8 74.0 %all-gather.5.cloned.1.call-done = f32[1024,2,3,64]{3,2,0,1:T(4,128)} async-done(((f32[16,2,3,64]{3,2,0,1:T(4,128)}), f32[1024,2,3,64]{3,2,0,1:T(4,128)}) %all-gather.5.cloned.1.call-update) | async-done | bytes 1572880 | tf_op jit(solution)/shard_map/all_gather | solution.py:99
  1470.8 2.9 fusion.187
  1473.8 1.8 fusion.16
  1477.5 1.8 fusion.33
  1479.3 1.8 fusion.32
  1483.2 2.6 fusion.10
  (76 shorter events, 45.9 us)
Async XLA Ops:
  7.2 1.9 copy-start
  7.2 580.9 %all-reduce.8.cloned.1.call-start = ((), (), s32[]{:S(2)}) async-start(), calls=%async_computation.3 | async-start | bytes 6291456
  7.8 0.6 copy-start.4
  7.8 3.0 copy-start.6
  11.5 4.1 copy-start.3
  25.4 0.7 copy-start.10
  25.4 679.1 %all-gather.3.cloned.1.call-start = ((), (), s32[]{:S(2)}) async-start(), calls=%async_computation | async-start | bytes 4259840 | tf_op jit(solution)/shard_map/all_gather | solution.py:99
  596.0 700.6 %all-reduce.10.cloned.1.call-start = ((), (), s32[]{:S(2)}) async-start(), calls=%async_computation.4 | async-start | bytes 6291456
  709.3 5.7 copy-start.5
  709.3 5.7 copy-start.7
  715.0 1.0 copy-start.8
  715.0 1.9 copy-start.9
  723.0 3.3 copy-start.1
  737.3 657.3 %all-reduce.6.cloned.1.call-start = ((), (), s32[]{:S(2)}) async-start(), calls=%async_computation.2 | async-start | bytes 1048576 | tf_op jit(solution)/shard_map/psum | solution.py:129
  1306.5 164.3 %all-gather.5.cloned.1.call-start = ((), (), s32[]{:S(2)}) async-start(), calls=%async_computation.1 | async-start | bytes 4259840 | tf_op jit(solution)/shard_map/all_gather | solution.py:99
  1481.3 1.9 copy-start.2
Sparse Core Ops, SparseCore 0:
  25.5 562.5 all-reduce.7
  596.1 108.3 all-gather.2
  737.4 559.1 all-reduce.9
  1306.6 54.6 all-reduce.5
  1363.6 107.1 all-gather.4
where the time goes:
time: 1500 us; the launch traced here: 1490 us
  waiting for transfers between devices  1300 us (87%)
  blocking collectives  79.8 us (5%)
  matrix products  63.4 us (4%)
  local copies, waits for them, and re-layouts  26.8 us (2%)
  between operations  15.3 us (1%)
    unnamed x7, waiting for transfers between devices  1120 us
    all_gather x2, waiting for transfers between devices, from_owner(): whole = lax.all_gather(owned, 'field', axis=0, tiled=True)  182 us
    psum x1, blocking collectives, local(): point_total = lax.psum(point_local, ('dp', 'field'))  79.8 us
    dot_general x28, matrix products, precise(): return jnp.einsum(form, left, right, precision=lax.Precision.HIGHEST)  46.5 us
  transfers between devices with their start and end apart: 5, of which 4 were waited for; matrix products, arithmetic and copies ran while one was open for 1% of the time, Pallas kernels for 0%

commit v1 on v0

v1 whole, which is shorter than its diff:
```python
import math

import jax
import jax.numpy as jnp
import ml_dtypes
import numpy as np
from jax import lax
from jax.experimental import pallas as pl
from jax.experimental.pallas import tpu as pltpu
from jax.sharding import Mesh
from jax.sharding import PartitionSpec as P

DEPTH = 512
DURATION = 1024
CHANNELS = 64
DMODES = 32
TMODES = 32
BATCH = 12

FIELD = ("z", "y", "x", "core")
BF16 = jnp.bfloat16
F32 = jnp.float32
SCALE = 1.0 / math.sqrt(DEPTH * DURATION)
INV_SCALE = 1.0 / math.sqrt(DMODES * TMODES)
NT = (((1,), (1,)), ((), ()))
TN = (((0,), (0,)), ((), ()))
VMEM_LIMIT = 48 * 1024 * 1024


def time_rows():
    q = np.arange(TMODES)
    m = (q % 2) * 16 + q // 2
    phase = ((m[:, None] * np.arange(DURATION)[None, :]) % DURATION) * (2.0 * np.pi / DURATION)
    return np.concatenate([np.cos(phase), -np.sin(phase)], axis=0).astype(ml_dtypes.bfloat16)


def depth_rows():
    orders = np.arange(DMODES)
    freqs = np.where(orders < DMODES // 2, orders, orders - DMODES)
    phase = ((freqs[:, None] * np.arange(DEPTH)[None, :]) % DEPTH) * (2.0 * np.pi / DEPTH)
    halves = []
    for half in range(2):
        part = phase[half * 16 : half * 16 + 16]
        both = np.concatenate([np.cos(part), np.sin(part)], axis=0)
        high = both.astype(ml_dtypes.bfloat16)
        low = (both - high.astype(np.float64)).astype(ml_dtypes.bfloat16)
        halves.append(np.concatenate([high, low], axis=0))
    return np.stack(halves)


def lanes(shape):
    return lax.broadcasted_iota(jnp.int32, shape, len(shape) - 1)


def swap(v):
    return pltpu.roll(v, 64, 1)


def turn(v, first):
    return swap(v) * jnp.where(lanes(v.shape) < 64, first, -first).astype(F32)


def dot(a, b, dims=(((1,), (0,)), ((), ()))):
    return lax.dot_general(a, b, dims, preferred_element_type=F32)


def emit_rows(r, scratch, store):
    for xl in range(8):
        cols = slice(xl * 64, xl * 64 + 64)
        block = jnp.concatenate([r[:32, cols], r[32:, cols]], axis=1)
        scratch[pl.ds(xl, 32, stride=8), :] = block
    store(scratch[...].reshape(32, 8, 128).astype(BF16))


def load_rows(recv, scratch):
    both = recv[:32, 0].astype(F32) + recv[32:, 0].astype(F32)
    scratch[...] = both.reshape(256, 128)


def mode_block(scratch, xl):
    g = scratch[pl.ds(xl, 32, stride=8), :]
    return jnp.concatenate([g[:, :64], g[:, 64:]], axis=0)


def weight_kernel(w_ref, o_ref):
    o_ref[...] = jnp.concatenate([w_ref[:, 0], w_ref[:, 1]], axis=2).astype(BF16)


def coeff_kernel(in_ref, tab_ref, o_ref, scratch):
    r = dot(tab_ref[...], in_ref[0].reshape(512, DURATION), NT) * SCALE

    def store(v):
        o_ref[:32, 0] = v
        o_ref[32:, 0] = v

    emit_rows(r, scratch, store)


def to_modes(recv, table):
    out = []
    for b in range(3):
        rows = recv[:, b].astype(F32).reshape(DEPTH, 128).astype(BF16)
        both = dot(table, rows)
        both = both[:32] + both[32:]
        out.append(both[:16] + turn(both[16:], 1.0))
    return jnp.concatenate(out, axis=0)


def from_modes(modes, table, factor, o_ref):
    turned = turn(modes, -1.0)
    for b in range(3):
        rows = slice(b * 16, b * 16 + 16)
        pair = jnp.concatenate([modes[rows], turned[rows]], axis=0)
        pair = jnp.concatenate([pair, pair], axis=0).astype(BF16)
        back = dot(table, pair, TN)
        if factor != 1.0:
            back = back * factor
        o_ref[:, b] = back.reshape(64, 8, 128).astype(BF16)


def own_pair(kp):
    row = lax.broadcasted_iota(jnp.int32, (48, 128), 0) % 16
    return row == 2 * kp + lanes((48, 128)) // 64


def mix_kernel(recv_ref, tab_ref, w_ref, o_ref, spec_ref):
    table = tab_ref[lax.axis_index("z")]
    spec = to_modes(recv_ref, table)
    spec_ref[...] = spec
    low = lanes((48, 128)) < 64
    other = swap(spec)
    real = jnp.where(low, spec, other)
    imag = jnp.where(low, other, spec)
    cols = []
    for kp in range(8):
        own = own_pair(kp)
        cols.append(
            jnp.concatenate([jnp.where(own, real, 0.0), jnp.where(own, imag, 0.0)], axis=0).astype(BF16)
        )
    prod = dot(jnp.concatenate(cols, axis=1), w_ref[...].reshape(1024, 128))
    mixed = prod[:48] + turn(prod[48:], -1.0)
    from_modes(mixed, table, 1.0, o_ref)


def adjoint_kernel(recv_ref, tab_ref, w_ref, spec_ref, o_ref, fact_ref, scratch):
    table = tab_ref[lax.axis_index("z")]
    dmix = to_modes(recv_ref, table)
    both = jnp.concatenate([dmix, turn(dmix, 1.0)], axis=0).astype(BF16)
    prod = dot(both, w_ref[...].reshape(1024, 128), NT)
    real = jnp.zeros((48, 128), F32)
    imag = jnp.zeros((48, 128), F32)
    for kp in range(8):
        own = own_pair(kp)
        cols = slice(kp * 128, kp * 128 + 128)
        real = real + jnp.where(own, prod[:48, cols], 0.0)
        imag = imag + jnp.where(own, prod[48:, cols], 0.0)
    real = real + swap(real)
    imag = imag + swap(imag)
    dspec = jnp.where(lanes((48, 128)) < 64, real, imag)
    from_modes(dspec, table, SCALE, o_ref)
    scratch[...] = jnp.zeros_like(scratch)
    for b in range(3):
        scratch[pl.ds(b, 16, stride=16), :] = spec_ref[b * 16 : b * 16 + 16, :]
        scratch[pl.ds(8 + b, 16, stride=16), :] = dmix[b * 16 : b * 16 + 16]
    point = jnp.sum(recv_ref[:, 3].astype(F32), axis=0)
    point = split_pair(point + swap(point))[:4]
    for k in range(16):
        scratch[k * 16 + 12 : k * 16 + 16, :] = point
    fact = scratch[...].reshape(16, 16, 128).astype(BF16)
    for dp in range(4):
        fact_ref[dp * 16 : dp * 16 + 16] = fact


def split_pair(v):
    high = v.astype(BF16).astype(F32)
    return jnp.where(lanes(v.shape) < 64, high, v - high)


def field_kernel(in_ref, cot_ref, recv_ref, tab_ref, w_ref, dpre_ref, o_ref, rows, scratch, point):
    b = pl.program_id(0)

    @pl.when(b == 0)
    def _():
        point[...] = jnp.zeros_like(point)

    load_rows(recv_ref, rows)
    mix_t = w_ref[...].astype(F32).T.astype(BF16)
    root = math.sqrt(2.0 / math.pi)
    for xl in range(8):
        g = (mode_block(rows, xl).T * INV_SCALE).astype(BF16)
        for chunk in range(4):
            ts = slice(chunk * 256, chunk * 256 + 256)
            pre = dot(g, tab_ref[:, ts]) + dot(mix_t, in_ref[0, xl, :, ts])
            sq = pre * pre
            th = jnp.tanh(pre * (root + (root * 0.044715) * sq))
            slope = 0.5 + 0.5 * th + (0.5 * pre) * (1.0 - th * th) * (
                root + (3.0 * root * 0.044715) * sq
            )
            dpre_ref[0, xl, :, ts] = (slope * cot_ref[0, xl, :, ts].astype(F32)).astype(BF16)
        point[...] += dot(in_ref[0, xl], dpre_ref[0, xl], NT)
    r = dot(tab_ref[...], dpre_ref[0].reshape(512, DURATION), NT) * INV_SCALE

    def store(v):
        o_ref[:32, b] = v
        o_ref[32:, b] = v

    emit_rows(r, scratch, store)

    @pl.when(b == 2)
    def _():
        total = point[...]
        pair = split_pair(jnp.concatenate([total, total], axis=1))
        for q in range(32):
            piece = pair[(q // 2) * 4 : (q // 2) * 4 + 4]
            piece = jnp.concatenate([piece, jnp.zeros_like(piece)], axis=0).astype(BF16)
            o_ref[q, 3] = piece
            o_ref[32 + q, 3] = piece


def grad_kernel(dpre_ref, recv_ref, tab_ref, w_ref, o_ref, rows):
    load_rows(recv_ref, rows)
    mixing = w_ref[...]
    for xl in range(8):
        g = mode_block(rows, xl).T.astype(BF16)
        for chunk in range(4):
            ts = slice(chunk * 256, chunk * 256 + 256)
            total = dot(g, tab_ref[:, ts]) + dot(mixing, dpre_ref[0, xl, :, ts])
            o_ref[0, xl, :, ts] = total.astype(BF16)


def weight_grad_kernel(fact_ref, spec_ref, point_ref, scratch):
    for m in range(16):
        parts = [fact_ref[dp * 16 + m].astype(F32) for dp in range(4)]
        s = jnp.concatenate([p[:8] for p in parts], axis=0)
        d = jnp.concatenate([p[8:] for p in parts], axis=0)
        left = jnp.concatenate([s[:, :64], s[:, 64:]], axis=0).astype(BF16)
        right = jnp.concatenate([d, turn(d, 1.0)], axis=0).astype(BF16)
        g = dot(left, right, TN) * (1.0 / math.sqrt(BATCH * DEPTH))
        spec_ref[m, 0] = g[:, :64]
        spec_ref[m, 1] = g[:, 64:]
        total = d[4:8] + d[12:16] + d[20:24] + d[28:32]
        scratch[m * 4 : m * 4 + 4, :] = total
    point = scratch[...]
    point = (point + swap(point)) * (1.0 / math.sqrt(BATCH * DEPTH * DURATION))
    point_ref[...] = point[:, :64]


def whole(shape):
    return pl.BlockSpec(shape, lambda *_: (0,) * len(shape))


def call(kernel, out_shape, grid, in_specs, out_specs, scratch=()):
    return pl.pallas_call(
        kernel,
        out_shape=out_shape,
        grid=grid,
        in_specs=in_specs,
        out_specs=out_specs,
        scratch_shapes=list(scratch),
        compiler_params=pltpu.CompilerParams(vmem_limit_bytes=VMEM_LIMIT),
    )


def shape(*dims, dtype=BF16):
    return jax.ShapeDtypeStruct(dims, dtype)


def exchange(v, axes):
    return lax.all_to_all(v, axes, 0, 0, tiled=True)


def local(inputs, cotangent, spec_weight, point_weight):
    tab = jnp.asarray(time_rows())
    depth = jnp.asarray(depth_rows())
    field_block = pl.BlockSpec((1, 8, 64, DURATION), lambda b: (b, 0, 0, 0))
    recv_block = pl.BlockSpec((64, 1, 8, 128), lambda b: (0, b, 0, 0))
    tab_block = whole((64, DURATION))
    mix_block = whole((64, 64))
    message = (64, 3, 8, 128)

    w_send = call(
        weight_kernel, shape(16, 64, 128), (1,), [whole((16, 2, 64, 64))], whole((16, 64, 128))
    )(spec_weight)
    weights = exchange(w_send, ("y", "x"))
    coeffs = call(
        coeff_kernel,
        shape(*message),
        (3,),
        [field_block, tab_block],
        recv_block,
        [pltpu.VMEM((256, 128), F32)],
    )(inputs, tab)
    got = exchange(coeffs, FIELD)
    rows, spectrum = call(
        mix_kernel,
        (shape(*message), shape(48, 128, dtype=F32)),
        (1,),
        [whole(message), whole((2, 64, DEPTH)), whole((16, 64, 128))],
        (whole(message), whole((48, 128))),
    )(got, depth, weights)
    got = exchange(rows, FIELD)
    dpre, drows = call(
        field_kernel,
        (shape(3, 8, 64, DURATION), shape(64, 4, 8, 128)),
        (3,),
        [field_block, field_block, recv_block, tab_block, mix_block],
        (field_block, whole((64, 4, 8, 128))),
        [pltpu.VMEM((256, 128), F32), pltpu.VMEM((256, 128), F32), pltpu.VMEM((64, 64), F32)],
    )(inputs, cotangent, got, tab, point_weight)
    got = exchange(drows, FIELD)
    drows, factors = call(
        adjoint_kernel,
        (shape(*message), shape(64, 16, 128)),
        (1,),
        [whole((64, 4, 8, 128)), whole((2, 64, DEPTH)), whole((16, 64, 128)), whole((48, 128))],
        (whole(message), whole((64, 16, 128))),
        [pltpu.VMEM((256, 128), F32)],
    )(got, depth, weights, spectrum)
    got = exchange(drows, FIELD)
    factors = exchange(factors, ("dp", "y", "x"))
    input_grad = call(
        grad_kernel,
        shape(3, 8, 64, DURATION),
        (3,),
        [field_block, recv_block, tab_block, mix_block],
        field_block,
        [pltpu.VMEM((256, 128), F32)],
    )(dpre, got, tab, point_weight)
    spec_grad, point_grad = call(
        weight_grad_kernel,
        (shape(16, 2, 64, 64, dtype=F32), shape(64, 64, dtype=F32)),
        (1,),
        [whole((64, 16, 128))],
        (whole((16, 2, 64, 64)), whole((64, 64))),
        [pltpu.VMEM((64, 128), F32)],
    )(factors)
    return (input_grad, spec_grad, point_grad)


def solution(mesh):
    fine = Mesh(mesh.devices.reshape(4, 2, 4, 4, 2), ("dp",) + FIELD)
    fields = P("dp", FIELD, None, None)
    weights = P(FIELD, None, None, None)
    return jax.shard_map(
        local,
        mesh=fine,
        in_specs=(fields, fields, weights, P()),
        out_specs=(fields, weights, P()),
        check_vma=False,
    )
```

time: 1500 us -> 127 us (0.08)
  waiting for transfers between devices: 1300 us -> 11.9 us
  matrix products: 63.4 us -> 0 us
  Pallas kernels: 0 us -> 21.5 us
  local copies, waits for them, and re-layouts: 26.8 us -> 5.87 us
    unnamed x7 -> x0, waiting for transfers between devices: 1120 us -> none
    all_gather x2 -> x0, waiting for transfers between devices: 182 us -> none  [from_owner(): whole = lax.all_gather(owned, 'field', axis=0, tiled=True)]
    psum x1 -> x0, blocking collectives: 79.8 us -> none  [local(): point_total = lax.psum(point_local, ('dp', 'field'))]
    all_to_all x0 -> x4, blocking collectives: none -> 72.3 us  [exchange(): return lax.all_to_all(v, axes, 0, 0, tiled=True)]
    dot_general x35 -> x0, matrix products: 63.4 us -> none  [the longest x28 46.5 us: precise(): return jnp.einsum(form, left, right, precision=lax.Precision.HIGHEST)]
    pallas_call x0 -> x7, Pallas kernels: none -> 21.5 us  [the longest x1 11.8 us: local(): call(field_kernel, (shape(3, 8, 64, DURATION), shape(64, 4, 8, 128)), (3,...]
  transfers between devices with their start and end apart: 5 -> 2, of which waited for: 4 -> 2; matrix products, arithmetic and copies ran while one was open for 1% -> 0% of each run, Pallas kernels for 0% -> 3%
where the time goes in v1:
time: 127 us; the launch traced here: 125 us
  blocking collectives  72.3 us (57%)
  Pallas kernels  21.5 us (17%)
  starting transfers between devices  12.4 us (10%)
  waiting for transfers between devices  11.9 us (9%)
  local copies, waits for them, and re-layouts  5.87 us (5%)
    all_to_all x4, blocking collectives, exchange(): return lax.all_to_all(v, axes, 0, 0, tiled=True)  72.3 us
    all_to_all x2, starting transfers between devices, exchange(): return lax.all_to_all(v, axes, 0, 0, tiled=True)  12.4 us
    all_to_all x2, waiting for transfers between devices, exchange(): return lax.all_to_all(v, axes, 0, 0, tiled=True)  11.9 us
    pallas_call x1, Pallas kernels, local(): call(field_kernel, (shape(3, 8, 64, DURATION), shape(64, 4, 8, 128)), (3,...  11.8 us
    unnamed x20, local copies, waits for them, and re-layouts  5.87 us
    pallas_call x1, Pallas kernels, local(): call(grad_kernel, shape(3, 8, 64, DURATION), (3,), [field_block, recv_blo...  3.62 us
  transfers between devices with their start and end apart: 2, of which 2 were waited for; matrix products, arithmetic and copies ran while one was open for 0% of the time, Pallas kernels for 3%

profile of v1, /device:TPU:32, one launch (start us, length us, event | category | flops | bytes accessed | tf_op | source)
XLA Modules:
  0.0 124.7 jit_solution(10113388071637201787)
XLA Ops:
  0.6 0.0 copy-start.4
  0.6 1.2 copy-done.4
  1.9 0.8 shard_map.86
  2.7 7.0 %all-to-all-start.1 = ((bf16[16,64,128]{2,1,0:T(8,128)(2,1)}), bf16[16,64,128]{2,1,0:T(8,128)(2,1)S(1)}, u32[]{:S(2)}, u32[]{:S(2)}) async-start(bf16[16,64,128]{2,1,0:T(8,128)(2,1)} %shard_map.86), calls=%async_computation.1 | async-start | bytes 524288 | tf_op jit(solution)/shard_map/all_to_all | solution.py:269
  9.7 0.0 copy-start
  9.8 1.9 %copy-done = bf16[3,8,64,1024]{3,2,1,0:T(8,128)(2,1)S(1)} copy-done((bf16[3,8,64,1024]{3,2,1,0:T(8,128)(2,1)S(1)}, bf16[3,8,64,1024]{3,2,1,0:T(8,128)(2,1)}, u32[]{:S(2)}) %copy-start) | copy-done | bytes 3145752
  11.6 0.9 copy-done.1
  12.5 1.7 %shard_map.85 = bf16[64,3,8,128]{3,2,1,0:T(8,128)(2,1)S(1)} custom-call(bf16[3,8,64,1024]{3,2,1,0:T(8,128)(2,1)S(1)} %copy-done, bf16[64,1024]{1,0:T(8,128)(2,1)S(1)} %copy-done.1), custom_call_target="tpu_custom_call" | custom-call | tf_op jit(solution)/shard_map/pallas_call | solution.py:285
  14.3 4.2 %all-to-all-done.1.w_ref = bf16[16,64,128]{2,1,0:T(8,128)(2,1)S(1)} async-done(((bf16[16,64,128]{2,1,0:T(8,128)(2,1)}), bf16[16,64,128]{2,1,0:T(8,128)(2,1)S(1)}, u32[]{:S(2)}, u32[]{:S(2)}) %all-to-all-start.1) | async-done | bytes 262176 | tf_op jit(solution)/shard_map/all_to_all | solution.py:269
  18.4 15.3 %all_to_all.30.recv_ref = bf16[64,3,8,128]{3,2,1,0:T(8,128)(2,1)S(1)} all-to-all(bf16[64,3,8,128]{3,2,1,0:T(8,128)(2,1)S(1)} %shard_map.85), channel_id=1, replica_groups=mesh['dp'=4,'z'=2,'y'=4,'x'=4,'core'=2] {'z','y','x','core'}, dimensions={0} | all-to-all | bytes 786432 | tf_op jit(solution)/shard_map/all_to_all | solution.py:269
  33.7 0.0 copy-done.6
  33.7 0.9 shard_map.87
  34.6 15.4 %all_to_all.31.recv_ref = bf16[64,3,8,128]{3,2,1,0:T(8,128)(2,1)S(1)} all-to-all(bf16[64,3,8,128]{3,2,1,0:T(8,128)(2,1)S(1)} %get-tuple-element.11), channel_id=1, replica_groups=mesh['dp'=4,'z'=2,'y'=4,'x'=4,'core'=2] {'z','y','x','core'}, dimensions={0} | all-to-all | bytes 786432 | tf_op jit(solution)/shard_map/all_to_all | solution.py:269
  50.0 11.8 %shard_map.88 = (bf16[3,8,64,1024]{3,2,1,0:T(8,128)(2,1)S(1)}, bf16[64,4,8,128]{3,2,1,0:T(8,128)(2,1)S(1)}) custom-call(bf16[3,8,64,1024]{3,2,1,0:T(8,128)(2,1)} %in_ref.3, bf16[3,8,64,1024]{3,2,1,0:T(8,128)(2,1)} %cot_ref.1, bf16[64,3,8,128]{3,2,1,0:T(8,128)(2,1)S(1)} %all_to_all.31.recv_ref, bf16[64,1024]{1,0:T(8,128)(2,1)S(1)} %copy-done.2, ...), custom_call_target="tpu_custom_call" | custom-call | tf_op jit(solution)/shard_map/pallas_call | solution.py:302
  61.8 16.7 %all_to_all.32.recv_ref = bf16[64,4,8,128]{3,2,1,0:T(8,128)(2,1)S(1)} all-to-all(bf16[64,4,8,128]{3,2,1,0:T(8,128)(2,1)S(1)} %get-tuple-element.13), channel_id=1, replica_groups=mesh['dp'=4,'z'=2,'y'=4,'x'=4,'core'=2] {'z','y','x','core'}, dimensions={0} | all-to-all | bytes 1048576 | tf_op jit(solution)/shard_map/all_to_all | solution.py:269
  78.5 1.0 shard_map.89
  79.5 0.0 copy-start.8
  79.5 24.9 %all_to_all.33.fact_ref = bf16[64,16,128]{2,1,0:T(8,128)(2,1)} all-to-all(bf16[64,16,128]{2,1,0:T(8,128)(2,1)S(1)} %get-tuple-element.16), channel_id=1, replica_groups=mesh['dp'=4,'z'=2,'y'=4,'x'=4,'core'=2] {'dp','y','x'}, dimensions={0} | all-to-all | bytes 524288 | tf_op jit(solution)/shard_map/all_to_all | solution.py:269
  104.4 5.4 %all-to-all-start.4 = ((bf16[64,3,8,128]{3,2,1,0:T(8,128)(2,1)}), bf16[64,3,8,128]{3,2,1,0:T(8,128)(2,1)S(1)}, u32[]{:S(2)}, u32[]{:S(2)}) async-start(bf16[64,3,8,128]{3,2,1,0:T(8,128)(2,1)} %copy-done.8), calls=%async_computation.4 | async-start | bytes 786432 | tf_op jit(solution)/shard_map/all_to_all | solution.py:269
  109.8 0.9 copy-done.5
  110.7 1.8 %shard_map.91 = (f32[16,2,64,64]{3,2,1,0:T(8,128)}, f32[64,64]{1,0:T(8,128)}) custom-call(bf16[64,16,128]{2,1,0:T(8,128)(2,1)S(1)} %copy-done.5), custom_call_target="tpu_custom_call" | custom-call | tf_op jit(solution)/shard_map/pallas_call | solution.py:329
  112.5 7.7 %all-to-all-done.4.recv_ref = bf16[64,3,8,128]{3,2,1,0:T(8,128)(2,1)S(1)} async-done(((bf16[64,3,8,128]{3,2,1,0:T(8,128)(2,1)}), bf16[64,3,8,128]{3,2,1,0:T(8,128)(2,1)S(1)}, u32[]{:S(2)}, u32[]{:S(2)}) %all-to-all-start.4) | async-done | bytes 393248 | tf_op jit(solution)/shard_map/all_to_all | solution.py:269
  120.2 0.9 copy-done.3
  121.1 3.6 %shard_map.90 = bf16[3,8,64,1024]{3,2,1,0:T(8,128)(2,1)} custom-call(bf16[3,8,64,1024]{3,2,1,0:T(8,128)(2,1)S(1)} %get-tuple-element.12.dpre_ref, bf16[64,3,8,128]{3,2,1,0:T(8,128)(2,1)S(1)} %all-to-all-done.4.recv_ref, bf16[64,1024]{1,0:T(8,128)(2,1)S(1)} %copy-done.3, bf16[64,64]{1,0:T(8,128)(2,1)S(1)} %copy-done.9), custom_call_target="tpu_custom_call" | custom-call | tf_op jit(solution)/shard_map/pallas_call | solution.py:321
  (11 shorter events, 0.0 us)
Async XLA Ops:
  0.6 1.2 copy-start.4
  1.9 31.9 %copy-start.6 = (bf16[2,64,512]{2,1,0:T(8,128)(2,1)S(1)}, bf16[2,64,512]{2,1,0:T(8,128)(2,1)}, u32[]{:S(2)}) copy-start(bf16[2,64,512]{2,1,0:T(8,128)(2,1)} %constant.5.clone.tab_ref) | copy-start | bytes 393220
  2.7 15.7 %all-to-all-start.1 = ((bf16[16,64,128]{2,1,0:T(8,128)(2,1)}), bf16[16,64,128]{2,1,0:T(8,128)(2,1)S(1)}, u32[]{:S(2)}, u32[]{:S(2)}) async-start(bf16[16,64,128]{2,1,0:T(8,128)(2,1)} %shard_map.86), calls=%async_computation.1 | async-start | bytes 524288 | tf_op jit(solution)/shard_map/all_to_all | solution.py:269
  9.7 1.9 %copy-start = (bf16[3,8,64,1024]{3,2,1,0:T(8,128)(2,1)S(1)}, bf16[3,8,64,1024]{3,2,1,0:T(8,128)(2,1)}, u32[]{:S(2)}) copy-start(bf16[3,8,64,1024]{3,2,1,0:T(8,128)(2,1)} %in_ref.3) | copy-start | bytes 9437188
  11.6 0.9 copy-start.1
  12.5 37.5 %copy-start.2 = (bf16[64,1024]{1,0:T(8,128)(2,1)S(1)}, bf16[64,1024]{1,0:T(8,128)(2,1)}, u32[]{:S(2)}) copy-start(bf16[64,1024]{1,0:T(8,128)(2,1)} %constant.4.clone.tab_ref) | copy-start | bytes 393220
  12.5 37.5 %copy-start.9 = (bf16[64,64]{1,0:T(8,128)(2,1)S(1)}, bf16[64,64]{1,0:T(8,128)(2,1)}, u32[]{:S(2)}) copy-start(bf16[64,64]{1,0:T(8,128)(2,1)} %w_ref.5) | copy-start | bytes 24580
  50.0 28.5 %copy-start.7 = (bf16[2,64,512]{2,1,0:T(8,128)(2,1)S(1)}, bf16[2,64,512]{2,1,0:T(8,128)(2,1)}, u32[]{:S(2)}) copy-start(bf16[2,64,512]{2,1,0:T(8,128)(2,1)} %constant.5.clone.tab_ref) | copy-start | bytes 393220
  79.5 24.9 %copy-start.8 = (bf16[64,3,8,128]{3,2,1,0:T(8,128)(2,1)}, bf16[64,3,8,128]{3,2,1,0:T(8,128)(2,1)S(1)}, u32[]{:S(2)}) copy-start(bf16[64,3,8,128]{3,2,1,0:T(8,128)(2,1)S(1)} %get-tuple-element.15) | copy-start | bytes 1179652
  104.4 15.8 %all-to-all-start.4 = ((bf16[64,3,8,128]{3,2,1,0:T(8,128)(2,1)}), bf16[64,3,8,128]{3,2,1,0:T(8,128)(2,1)S(1)}, u32[]{:S(2)}, u32[]{:S(2)}) async-start(bf16[64,3,8,128]{3,2,1,0:T(8,128)(2,1)} %copy-done.8), calls=%async_computation.4 | async-start | bytes 786432 | tf_op jit(solution)/shard_map/all_to_all | solution.py:269
  109.8 1.0 copy-start.5
  120.2 0.9 copy-start.3

commit v2 on v1

v2 whole, which is shorter than its diff:
```python
import math

import jax
import jax.numpy as jnp
import ml_dtypes
import numpy as np
from jax import lax
from jax.experimental import pallas as pl
from jax.experimental.pallas import tpu as pltpu
from jax.sharding import Mesh
from jax.sharding import PartitionSpec as P

DEPTH = 512
DURATION = 1024
CHANNELS = 64
DMODES = 32
TMODES = 32
BATCH = 12

CHIP = ("z", "y", "x")
FIELD = CHIP + ("core",)
BF16 = jnp.bfloat16
F32 = jnp.float32
SCALE = 1.0 / math.sqrt(DEPTH * DURATION)
INV_SCALE = 1.0 / math.sqrt(DMODES * TMODES)
NN = (((1,), (0,)), ((), ()))
NT = (((1,), (1,)), ((), ()))
VMEM_LIMIT = 48 * 1024 * 1024
PAIRS = 48
ROWS = 56


def time_rows():
    out = []
    for core in range(2):
        m = np.concatenate([core * 16 + np.arange(16), (1 - core) * 16 + np.arange(16)])
        phase = ((m[:, None] * np.arange(DURATION)[None, :]) % DURATION) * (2.0 * np.pi / DURATION)
        out.append(np.concatenate([np.cos(phase), -np.sin(phase)], axis=0))
    return np.stack(out).astype(ml_dtypes.bfloat16)


def depth_rows():
    orders = np.arange(DMODES)
    freqs = np.where(orders < DMODES // 2, orders, orders - DMODES)
    forward, inverse = [], []
    for f in range(64):
        x = np.concatenate([f * 8 + np.arange(8), (f ^ 1) * 8 + np.arange(8)])
        phase = ((freqs[:, None] * x[None, :]) % DEPTH) * (2.0 * np.pi / DEPTH)
        both = np.concatenate([np.cos(phase), np.sin(phase)], axis=0)
        high = both.astype(ml_dtypes.bfloat16)
        low = (both - high.astype(np.float64)).astype(ml_dtypes.bfloat16)
        forward.append(np.concatenate([high, low], axis=1))
        inverse.append(np.concatenate([high, low], axis=0).T)
    return np.stack(forward), np.stack(inverse)


def lanes(shape):
    return lax.broadcasted_iota(jnp.int32, shape, len(shape) - 1)


def swap(v):
    return pltpu.roll(v, 64, 1)


def turn(v, first):
    return swap(v) * jnp.where(lanes(v.shape) < 64, first, -first).astype(F32)


def split_pair(v):
    high = v.astype(BF16).astype(F32)
    return jnp.where(lanes(v.shape) < 64, high, v - high)


def dot(a, b, dims=NN):
    return lax.dot_general(a, b, dims, preferred_element_type=F32)


def emit_rows(r, scratch):
    for xl in range(8):
        cols = slice(xl * 64, xl * 64 + 64)
        block = jnp.concatenate([r[:32, cols], r[32:, cols]], axis=1)
        scratch[pl.ds(xl, 32, stride=8), :] = block
    return scratch[...].reshape(32, 8, 128).astype(BF16)


def load_rows(own_ref, other_ref, scratch):
    scratch[:128] = own_ref[:, 0].astype(F32).reshape(128, 128)
    scratch[128:] = other_ref[:, 0].astype(F32).reshape(128, 128)


def mode_block(scratch, xl):
    g = scratch[pl.ds(xl, 32, stride=8), :]
    return jnp.concatenate([g[:, :64], g[:, 64:]], axis=0)


def own_pair(kp, rows):
    row = lax.broadcasted_iota(jnp.int32, (rows, 128), 0)
    first = row - lanes((rows, 128)) // 64 * 3 - 6 * kp
    return (first >= 0) & (first < 3)


def weight_kernel(w_ref, o_ref):
    o_ref[...] = jnp.concatenate([w_ref[:, 0], w_ref[:, 1]], axis=2).astype(BF16)


def coeff_kernel(in_ref, tab_ref, own_ref, send_ref, scratch):
    table = tab_ref[lax.axis_index("core")]
    rows = emit_rows(dot(table, in_ref[0].reshape(512, DURATION), NT) * SCALE, scratch)
    own_ref[:, 0] = rows[:16]
    send_ref[:, 0] = rows[16:]


def spread_kernel(f_ref, own_ref, other_ref, tab_ref, o_ref, scratch, *point, rows):
    del f_ref
    table = tab_ref[0]
    both = jnp.concatenate([own_ref[:, :3].astype(F32), other_ref[:, :3].astype(F32)], axis=2).astype(BF16)
    both = both.reshape(PAIRS, 16, 128)
    for group in range(4):
        data = jnp.concatenate([both[group * 12 + i] for i in range(12)], axis=1)
        modes = dot(table, jnp.concatenate([data, data], axis=0))
        for i in range(12):
            cols = slice(i * 128, i * 128 + 128)
            part = modes[:32, cols] + turn(modes[32:, cols], 1.0)
            scratch[pl.ds(group * 12 + i, 32, stride=rows), :] = part
    if point:
        (pairs,) = point
        total = own_ref[:8, 3].astype(F32).reshape(64, 128) + other_ref[:8, 3].astype(F32).reshape(64, 128)
        pairs[...] = split_pair(total + swap(total))
        for i in range(2):
            scratch[pl.ds(PAIRS + i, 32, stride=rows), :] = pairs[pl.ds(i, 32, stride=2), :]
        for i in range(2, 8):
            scratch[pl.ds(PAIRS + i, 32, stride=rows), :] = jnp.zeros((32, 128), F32)
    o_ref[...] = scratch[...].reshape(32, rows, 128).astype(BF16)


def mix_kernel(recv_ref, w_ref, o_ref, spec_ref):
    spec = jnp.sum(recv_ref[...].astype(F32), axis=0)
    spec_ref[...] = spec
    low = lanes(spec.shape) < 64
    other = swap(spec)
    real = jnp.where(low, spec, other)
    imag = jnp.where(low, other, spec)
    cols = []
    for kp in range(8):
        own = own_pair(kp, PAIRS)
        cols.append(
            jnp.concatenate([jnp.where(own, real, 0.0), jnp.where(own, imag, 0.0)], axis=0).astype(BF16)
        )
    prod = dot(jnp.concatenate(cols, axis=1), w_ref[...].reshape(1024, 128))
    mixed = (prod[:PAIRS] + turn(prod[PAIRS:], -1.0)).astype(BF16)
    o_ref[...] = jnp.broadcast_to(mixed[None], (32, PAIRS, 128))


def adjoint_kernel(recv_ref, w_ref, o_ref, dmix_ref):
    total = jnp.sum(recv_ref[...].astype(F32), axis=0)
    dmix = total[:PAIRS]
    dmix_ref[...] = dmix
    both = jnp.concatenate([dmix, turn(dmix, 1.0)], axis=0).astype(BF16)
    prod = dot(both, w_ref[...].reshape(1024, 128), NT)
    real = jnp.zeros((PAIRS, 128), F32)
    imag = jnp.zeros((PAIRS, 128), F32)
    for kp in range(8):
        own = own_pair(kp, PAIRS)
        cols = slice(kp * 128, kp * 128 + 128)
        real = real + jnp.where(own, prod[:PAIRS, cols], 0.0)
        imag = imag + jnp.where(own, prod[PAIRS:, cols], 0.0)
    real = real + swap(real)
    imag = imag + swap(imag)
    dspec = jnp.where(lanes(real.shape) < 64, real, imag) * SCALE
    point = total[PAIRS:]
    point = split_pair(point + swap(point))
    message = jnp.concatenate([dspec, point], axis=0).astype(BF16)
    o_ref[...] = jnp.broadcast_to(message[None], (32, ROWS, 128))


def gather_kernel(f_ref, recv_ref, tab_ref, *rest, rows):
    del f_ref
    if rows == ROWS:
        spec_ref, dmix_ref, own_ref, send_ref, fact_ref, scratch, fact = rest
    else:
        own_ref, send_ref, scratch = rest
    table = tab_ref[0]
    scratch[...] = recv_ref[...].astype(F32).reshape(32 * rows, 128)
    for group in range(4):
        cols = []
        for i in range(12):
            modes = scratch[pl.ds(group * 12 + i, 32, stride=rows), :]
            pair = jnp.concatenate([modes, turn(modes, -1.0)], axis=0)
            cols.append(jnp.concatenate([pair, pair], axis=0).astype(BF16))
        back = dot(table, jnp.concatenate(cols, axis=1))
        for i in range(12):
            m, b = divmod(group * 12 + i, 3)
            part = back[:, i * 128 : i * 128 + 128].astype(BF16)
            own_ref[m, b] = part[:8]
            send_ref[m, b] = part[8:]
    if rows == ROWS:
        fact[...] = jnp.zeros_like(fact)
        fact[:PAIRS] = spec_ref[...]
        fact[64 : 64 + PAIRS] = dmix_ref[...]
        for i in range(2):
            fact[pl.ds(128 + i, 32, stride=2), :] = scratch[pl.ds(PAIRS + i, 32, stride=rows), :]
        whole_fact = fact[...].astype(BF16)
        fact_ref[...] = jnp.broadcast_to(whole_fact[None], (4, 192, 128))


def field_kernel(
    in_ref, cot_ref, got_ref, other_ref, tab_ref, w_ref, dpre_ref, own_ref, send_ref, rows, scratch, point
):
    b = pl.program_id(0)

    @pl.when(b == 0)
    def _():
        point[...] = jnp.zeros_like(point)

    load_rows(got_ref, other_ref, rows)
    table = tab_ref.at[lax.axis_index("core")]
    mix_t = w_ref[...].astype(F32).T.astype(BF16)
    root = math.sqrt(2.0 / math.pi)
    for xl in range(8):
        g = (mode_block(rows, xl).T * INV_SCALE).astype(BF16)
        for chunk in range(4):
            ts = slice(chunk * 256, chunk * 256 + 256)
            pre = dot(g, table[:, ts]) + dot(mix_t, in_ref[0, xl, :, ts])
            sq = pre * pre
            th = jnp.tanh(pre * (root + (root * 0.044715) * sq))
            slope = 0.5 + 0.5 * th + (0.5 * pre) * (1.0 - th * th) * (
                root + (3.0 * root * 0.044715) * sq
            )
            dpre_ref[0, xl, :, ts] = (slope * cot_ref[0, xl, :, ts].astype(F32)).astype(BF16)
        point[...] += dot(in_ref[0, xl], dpre_ref[0, xl], NT)
    r = dot(table[...], dpre_ref[0].reshape(512, DURATION), NT) * INV_SCALE
    out = emit_rows(r, scratch)
    own_ref[:, b] = out[:16]
    send_ref[:, b] = out[16:]

    @pl.when(b == 2)
    def _():
        total = point[...]
        pair = split_pair(jnp.concatenate([total, total], axis=1))
        pair = jnp.concatenate([pair, jnp.zeros_like(pair)], axis=0).reshape(16, 8, 128).astype(BF16)
        own_ref[:, 3] = pair
        send_ref[:, 3] = pair


def grad_kernel(dpre_ref, got_ref, other_ref, tab_ref, w_ref, o_ref, rows):
    load_rows(got_ref, other_ref, rows)
    table = tab_ref.at[lax.axis_index("core")]
    mixing = w_ref[...]
    for xl in range(8):
        g = mode_block(rows, xl).T.astype(BF16)
        for chunk in range(4):
            ts = slice(chunk * 256, chunk * 256 + 256)
            total = dot(g, table[:, ts]) + dot(mixing, dpre_ref[0, xl, :, ts])
            o_ref[0, xl, :, ts] = total.astype(BF16)


def weight_grad_kernel(fact_ref, spec_ref, point_ref):
    fact = fact_ref[...].astype(F32)
    turned = fact[:, :64].reshape(256, 128).T
    real = turned[:64]
    imag = turned[64:]
    left = jnp.concatenate([real, imag], axis=1)
    row = lanes((64, 512)) % 64
    d = fact[:, 64:128].reshape(256, 128)
    right = jnp.concatenate([d, turn(d, 1.0)], axis=0).astype(BF16)
    parts = [
        jnp.where((row >= 3 * m) & (row < 3 * m + 3), left, 0.0).astype(BF16) for m in range(16)
    ]
    g = dot(jnp.concatenate(parts, axis=0), right) * (1.0 / math.sqrt(BATCH * DEPTH))
    g = g.reshape(16, 64, 128)
    spec_ref[:, 0] = g[:, :, :64]
    spec_ref[:, 1] = g[:, :, 64:]
    point = fact[0, 128:] + fact[1, 128:] + fact[2, 128:] + fact[3, 128:]
    point = (point + swap(point)) * (1.0 / math.sqrt(BATCH * DEPTH * DURATION))
    point_ref[...] = point[:, :64]


def whole(shape):
    return pl.BlockSpec(shape, lambda *_: (0,) * len(shape))


def call(kernel, out_shape, grid, in_specs, out_specs, scratch=(), prefetch=0):
    return pl.pallas_call(
        kernel,
        out_shape=out_shape,
        grid_spec=pltpu.PrefetchScalarGridSpec(
            num_scalar_prefetch=prefetch,
            grid=grid,
            in_specs=in_specs,
            out_specs=out_specs,
            scratch_shapes=list(scratch),
        ),
        compiler_params=pltpu.CompilerParams(vmem_limit_bytes=VMEM_LIMIT),
    )


def shape(*dims, dtype=BF16):
    return jax.ShapeDtypeStruct(dims, dtype)


def exchange(v, axes):
    return lax.all_to_all(v, axes, 0, 0, tiled=True)


def to_other_core(v):
    return lax.ppermute(v, "core", [(0, 1), (1, 0)])


def local(inputs, cotangent, spec_weight, point_weight):
    tab = jnp.asarray(time_rows())
    forward, inverse = (jnp.asarray(v) for v in depth_rows())
    place = lax.axis_index(FIELD).reshape(1)
    field_block = pl.BlockSpec((1, 8, 64, DURATION), lambda b: (b, 0, 0, 0))
    part_block = pl.BlockSpec((16, 1, 8, 128), lambda b: (0, b, 0, 0))
    tab_block = whole((2, 64, DURATION))
    mix_block = whole((64, 64))
    forward_block = pl.BlockSpec((1, 64, 32), lambda i, f: (f[0], 0, 0))
    inverse_block = pl.BlockSpec((1, 16, 128), lambda i, f: (f[0], 0, 0))
    part = shape(16, 3, 8, 128)
    part4 = shape(16, 4, 8, 128)

    def spread(own, other, rows):
        scratch = [pltpu.VMEM((32 * rows, 128), F32)]
        if rows == ROWS:
            scratch.append(pltpu.VMEM((64, 128), F32))
        return call(
            lambda *refs: spread_kernel(*refs, rows=rows),
            shape(32, rows, 128),
            (1,),
            [whole(own.shape), whole(own.shape), forward_block],
            whole((32, rows, 128)),
            scratch,
            prefetch=1,
        )(place, own, other, forward)

    weights = call(
        weight_kernel, shape(16, 64, 128), (1,), [whole((16, 2, 64, 64))], whole((16, 64, 128))
    )(spec_weight)
    own, send = call(
        coeff_kernel,
        (part, part),
        (3,),
        [field_block, tab_block],
        (part_block, part_block),
        [pltpu.VMEM((256, 128), F32)],
    )(inputs, tab)
    got = exchange(spread(own, to_other_core(send), PAIRS), CHIP)
    mixed, spectrum = call(
        mix_kernel,
        (shape(32, PAIRS, 128), shape(PAIRS, 128, dtype=F32)),
        (1,),
        [whole((32, PAIRS, 128)), whole((16, 64, 128))],
        (whole((32, PAIRS, 128)), whole((PAIRS, 128))),
    )(got, weights)
    got = exchange(mixed, CHIP)
    own, send = call(
        lambda *refs: gather_kernel(*refs, rows=PAIRS),
        (part, part),
        (1,),
        [whole((32, PAIRS, 128)), inverse_block],
        (whole(part.shape), whole(part.shape)),
        [pltpu.VMEM((32 * PAIRS, 128), F32)],
        prefetch=1,
    )(place, got, inverse)
    dpre, own, send = call(
        field_kernel,
        (shape(3, 8, 64, DURATION), part4, part4),
        (3,),
        [field_block, field_block, part_block, part_block, tab_block, mix_block],
        (field_block, whole(part4.shape), whole(part4.shape)),
        [pltpu.VMEM((256, 128), F32), pltpu.VMEM((256, 128), F32), pltpu.VMEM((64, 64), F32)],
    )(inputs, cotangent, own, to_other_core(send), tab, point_weight)
    got = exchange(spread(own, to_other_core(send), ROWS), CHIP)
    dmodes, dmixed = call(
        adjoint_kernel,
        (shape(32, ROWS, 128), shape(PAIRS, 128, dtype=F32)),
        (1,),
        [whole((32, ROWS, 128)), whole((16, 64, 128))],
        (whole((32, ROWS, 128)), whole((PAIRS, 128))),
    )(got, weights)
    got = exchange(dmodes, CHIP)
    own, send, factors = call(
        lambda *refs: gather_kernel(*refs, rows=ROWS),
        (part, part, shape(4, 192, 128)),
        (1,),
        [whole((32, ROWS, 128)), inverse_block, whole((PAIRS, 128)), whole((PAIRS, 128))],
        (whole(part.shape), whole(part.shape), whole((4, 192, 128))),
        [pltpu.VMEM((32 * ROWS, 128), F32), pltpu.VMEM((192, 128), F32)],
        prefetch=1,
    )(place, got, inverse, spectrum, dmixed)
    factors = exchange(factors, "dp")
    input_grad = call(
        grad_kernel,
        shape(3, 8, 64, DURATION),
        (3,),
        [field_block, part_block, part_block, tab_block, mix_block],
        field_block,
        [pltpu.VMEM((256, 128), F32)],
    )(dpre, own, to_other_core(send), tab, point_weight)
    spec_grad, point_grad = call(
        weight_grad_kernel,
        (shape(16, 2, 64, 64, dtype=F32), shape(64, 64, dtype=F32)),
        (1,),
        [whole((4, 192, 128))],
        (whole((16, 2, 64, 64)), whole((64, 64))),
    )(factors)
    return (input_grad, spec_grad, point_grad)


def solution(mesh):
    fine = Mesh(mesh.devices.reshape(4, 2, 4, 4, 2), ("dp",) + FIELD)
    fields = P("dp", FIELD, None, None)
    weights = P(FIELD, None, None, None)
    return jax.shard_map(
        local,
        mesh=fine,
        in_specs=(fields, fields, weights, P()),
        out_specs=(fields, weights, P()),
        check_vma=False,
    )
```

time: 127 us -> 107 us (0.84)
  blocking collectives: 72.3 us -> 42.6 us
  waiting for transfers between devices: 11.9 us -> 17.6 us
  starting transfers between devices: 12.4 us -> 16.4 us
    all_to_all x4 -> x3, blocking collectives: 72.3 us -> 42.6 us  [exchange(): return lax.all_to_all(v, axes, 0, 0, tiled=True)]
    ppermute x0 -> x4, waiting for transfers between devices: none -> 5.06 us  [to_other_core(): return lax.ppermute(v, 'core', [(0, 1), (1, 0)])]
    all_to_all x2, starting transfers between devices: 12.4 us -> 16.1 us  [exchange(): return lax.all_to_all(v, axes, 0, 0, tiled=True)]
    pallas_call x5 -> x9, Pallas kernels: 19 us -> 20.9 us  [the longest x1 11.7 us: local(): call(field_kernel, (shape(3, 8, 64, DURATION), part4, part4), (3,), [fiel...]
    unnamed x20 -> x22, local copies, waits for them, and re-layouts: 5.87 us -> 5.48 us
  transfers between devices with their start and end apart: 2 -> 6, of which waited for: 2 -> 6; matrix products, arithmetic and copies ran while one was open for 0% -> 0% of each run, Pallas kernels for 3% -> 4%
where the time goes in v2:
time: 107 us; the launch traced here: 106 us
  blocking collectives  42.6 us (40%)
  Pallas kernels  22.6 us (21%)
  waiting for transfers between devices  17.6 us (16%)
  starting transfers between devices  16.4 us (15%)
  local copies, waits for them, and re-layouts  5.48 us (5%)
    all_to_all x3, blocking collectives, exchange(): return lax.all_to_all(v, axes, 0, 0, tiled=True)  42.6 us
    all_to_all x2, starting transfers between devices, exchange(): return lax.all_to_all(v, axes, 0, 0, tiled=True)  16.1 us
    all_to_all x2, waiting for transfers between devices, exchange(): return lax.all_to_all(v, axes, 0, 0, tiled=True)  12.6 us
    pallas_call x1, Pallas kernels, local(): call(field_kernel, (shape(3, 8, 64, DURATION), part4, part4), (3,), [fiel...  11.7 us
    unnamed x22, local copies, waits for them, and re-layouts  5.48 us
    ppermute x4, waiting for transfers between devices, to_other_core(): return lax.ppermute(v, 'core', [(0, 1), (1, 0)])  5.06 us
    pallas_call x1, Pallas kernels, local(): call(grad_kernel, shape(3, 8, 64, DURATION), (3,), [field_block, part_blo...  3.6 us
  transfers between devices with their start and end apart: 6, of which 6 were waited for; matrix products, arithmetic and copies ran while one was open for 0% of the time, Pallas kernels for 4%

profile of v2, /device:TPU:32, one launch (start us, length us, event | category | flops | bytes accessed | tf_op | source)
XLA Modules:
  0.0 105.6 jit_solution(13127925578156957197)
XLA Ops:
  0.6 1.9 %copy-done = bf16[3,8,64,1024]{3,2,1,0:T(8,128)(2,1)S(1)} copy-done((bf16[3,8,64,1024]{3,2,1,0:T(8,128)(2,1)S(1)}, bf16[3,8,64,1024]{3,2,1,0:T(8,128)(2,1)}, u32[]{:S(2)}) %copy-start) | copy-done | bytes 3145752
  2.5 0.9 copy-done.4
  3.5 1.7 %shard_map.94 = (bf16[16,3,8,128]{3,2,1,0:T(8,128)(2,1)S(1)}, bf16[16,3,8,128]{3,2,1,0:T(8,128)(2,1)S(1)}) custom-call(bf16[3,8,64,1024]{3,2,1,0:T(8,128)(2,1)S(1)} %copy-done, bf16[2,64,1024]{2,1,0:T(8,128)(2,1)S(1)} %copy-done.4), custom_call_target="tpu_custom_call" | custom-call | tf_op jit(solution)/shard_map/pallas_call | solution.py:339
  5.3 1.3 %collective-permute-done.refs_2_ = bf16[16,3,8,128]{3,2,1,0:T(8,128)(2,1)S(1)} collective-permute-done((bf16[16,3,8,128]{3,2,1,0:T(8,128)(2,1)S(1)}, bf16[16,3,8,128]{3,2,1,0:T(8,128)(2,1)S(1)}, u32[]{:S(2)}, u32[]{:S(2)}) %collective-permute-start) | collective-permute-done | bytes 98336 | tf_op jit(solution)/shard_map/ppermute | solution.py:306
  6.6 1.3 %shard_map.95 = bf16[32,48,128]{2,1,0:T(8,128)(2,1)} custom-call(s32[1]{0:T(128)} %bitcast.refs_0_, bf16[16,3,8,128]{3,2,1,0:T(8,128)(2,1)S(1)} %get-tuple-element.19.refs_1_, bf16[16,3,8,128]{3,2,1,0:T(8,128)(2,1)S(1)} %collective-permute-done.refs_2_, bf16[64,64,32]{2,1,0:T(8,128)(2,1)S(1)} %copy-done.1), custom_call_target="tpu_custom_call" | custom-call | tf_op jit(solution)/shard_map/pallas_call | solution.py:326
  7.9 8.6 %all-to-all-start = ((bf16[32,48,128]{2,1,0:T(8,128)(2,1)}), bf16[32,48,128]{2,1,0:T(8,128)(2,1)S(1)}, u32[]{:S(2)}, u32[]{:S(2)}) async-start(bf16[32,48,128]{2,1,0:T(8,128)(2,1)} %shard_map.95), calls=%async_computation | async-start | bytes 786432 | tf_op jit(solution)/shard_map/all_to_all | solution.py:302
  16.6 9.5 %all-to-all-done.recv_ref = bf16[32,48,128]{2,1,0:T(8,128)(2,1)S(1)} async-done(((bf16[32,48,128]{2,1,0:T(8,128)(2,1)}), bf16[32,48,128]{2,1,0:T(8,128)(2,1)S(1)}, u32[]{:S(2)}, u32[]{:S(2)}) %all-to-all-start) | async-done | bytes 393248 | tf_op jit(solution)/shard_map/all_to_all | solution.py:302
  26.5 13.6 %all_to_all.25.refs_1_ = bf16[32,48,128]{2,1,0:T(8,128)(2,1)S(1)} all-to-all(bf16[32,48,128]{2,1,0:T(8,128)(2,1)S(1)} %get-tuple-element.21), channel_id=1, replica_groups=mesh['dp'=4,'z'=2,'y'=4,'x'=4,'core'=2] {'z','y','x'}, dimensions={0} | all-to-all | bytes 786432 | tf_op jit(solution)/shard_map/all_to_all | solution.py:302
  40.1 0.5 shard_map.98
  40.6 1.3 %collective-permute-done.1.other_ref = bf16[16,3,8,128]{3,2,1,0:T(8,128)(2,1)S(1)} collective-permute-done((bf16[16,3,8,128]{3,2,1,0:T(8,128)(2,1)S(1)}, bf16[16,3,8,128]{3,2,1,0:T(8,128)(2,1)S(1)}, u32[]{:S(2)}, u32[]{:S(2)}) %collective-permute-start.1) | collective-permute-done | bytes 98336 | tf_op jit(solution)/shard_map/ppermute | solution.py:306
  41.9 11.7 %shard_map.99 = (bf16[3,8,64,1024]{3,2,1,0:T(8,128)(2,1)S(1)}, bf16[16,4,8,128]{3,2,1,0:T(8,128)(2,1)S(1)}, bf16[16,4,8,128]{3,2,1,0:T(8,128)(2,1)S(1)}) custom-call(bf16[3,8,64,1024]{3,2,1,0:T(8,128)(2,1)} %in_ref.3, bf16[3,8,64,1024]{3,2,1,0:T(8,128)(2,1)} %cot_ref.1, bf16[16,3,8,128]{3,2,1,0:T(8,128)(2,1)S(1)} %get-tuple-element.22.got_ref, ...), custom_call_target="tpu_custom_call" | custom-call | tf_op jit(solution)/shard_map/pallas_call | solution.py:365
  53.6 1.7 %copy-done.2 = bf16[3,8,64,1024]{3,2,1,0:T(8,128)(2,1)} copy-done((bf16[3,8,64,1024]{3,2,1,0:T(8,128)(2,1)}, bf16[3,8,64,1024]{3,2,1,0:T(8,128)(2,1)S(1)}, u32[]{:S(2)}) %copy-start.2) | copy-done | bytes 3145752
  55.4 1.2 %collective-permute-done.2.refs_2_ = bf16[16,4,8,128]{3,2,1,0:T(8,128)(2,1)S(1)} collective-permute-done((bf16[16,4,8,128]{3,2,1,0:T(8,128)(2,1)S(1)}, bf16[16,4,8,128]{3,2,1,0:T(8,128)(2,1)S(1)}, u32[]{:S(2)}, u32[]{:S(2)}) %collective-permute-start.2) | collective-permute-done | bytes 131104 | tf_op jit(solution)/shard_map/ppermute | solution.py:306
  56.6 0.5 shard_map.100
  57.1 15.0 %all_to_all.26.recv_ref = bf16[32,56,128]{2,1,0:T(8,128)(2,1)S(1)} all-to-all(bf16[32,56,128]{2,1,0:T(8,128)(2,1)S(1)} %shard_map.100), channel_id=1, replica_groups=mesh['dp'=4,'z'=2,'y'=4,'x'=4,'core'=2] {'z','y','x'}, dimensions={0} | all-to-all | bytes 917504 | tf_op jit(solution)/shard_map/all_to_all | solution.py:302
  72.1 0.4 shard_map.101
  72.5 14.0 %all_to_all.27.refs_1_ = bf16[32,56,128]{2,1,0:T(8,128)(2,1)S(1)} all-to-all(bf16[32,56,128]{2,1,0:T(8,128)(2,1)S(1)} %get-tuple-element.27), channel_id=1, replica_groups=mesh['dp'=4,'z'=2,'y'=4,'x'=4,'core'=2] {'z','y','x'}, dimensions={0} | all-to-all | bytes 917504 | tf_op jit(solution)/shard_map/all_to_all | solution.py:302
  86.6 1.0 shard_map.102
  87.6 7.6 %all-to-all-start.4 = ((bf16[4,192,128]{2,1,0:T(8,128)(2,1)}), bf16[4,192,128]{2,1,0:T(8,128)(2,1)S(1)}, u32[]{:S(2)}, u32[]{:S(2)}) async-start(bf16[4,192,128]{2,1,0:T(8,128)(2,1)} %get-tuple-element.32), calls=%async_computation.4 | async-start | bytes 393216 | tf_op jit(solution)/shard_map/all_to_all | solution.py:302
  95.1 1.3 %collective-permute-done.3.other_ref = bf16[16,3,8,128]{3,2,1,0:T(8,128)(2,1)S(1)} collective-permute-done((bf16[16,3,8,128]{3,2,1,0:T(8,128)(2,1)S(1)}, bf16[16,3,8,128]{3,2,1,0:T(8,128)(2,1)S(1)}, u32[]{:S(2)}, u32[]{:S(2)}) %collective-permute-start.3) | collective-permute-done | bytes 98336 | tf_op jit(solution)/shard_map/ppermute | solution.py:306
  96.4 0.9 copy-done.6
  97.4 3.6 %shard_map.103 = bf16[3,8,64,1024]{3,2,1,0:T(8,128)(2,1)} custom-call(bf16[3,8,64,1024]{3,2,1,0:T(8,128)(2,1)S(1)} %copy-done.3, bf16[16,3,8,128]{3,2,1,0:T(8,128)(2,1)S(1)} %get-tuple-element.30.got_ref, bf16[16,3,8,128]{3,2,1,0:T(8,128)(2,1)S(1)} %collective-permute-done.3.other_ref, bf16[2,64,1024]{2,1,0:T(8,128)(2,1)S(1)} %copy-done.6, ...), custom_call_target="tpu_custom_call" | custom-call | tf_op jit(solution)/shard_map/pallas_call | solution.py:392
  101.0 3.1 %all-to-all-done.4.fact_ref = bf16[4,192,128]{2,1,0:T(8,128)(2,1)S(1)} async-done(((bf16[4,192,128]{2,1,0:T(8,128)(2,1)}), bf16[4,192,128]{2,1,0:T(8,128)(2,1)S(1)}, u32[]{:S(2)}, u32[]{:S(2)}) %all-to-all-start.4) | async-done | bytes 196640 | tf_op jit(solution)/shard_map/all_to_all | solution.py:302
  104.1 1.6 %shard_map.104 = (f32[16,2,64,64]{3,2,1,0:T(8,128)}, f32[64,64]{1,0:T(8,128)}) custom-call(bf16[4,192,128]{2,1,0:T(8,128)(2,1)S(1)} %all-to-all-done.4.fact_ref), custom_call_target="tpu_custom_call" | custom-call | tf_op jit(solution)/shard_map/pallas_call | solution.py:400
  (24 shorter events, 0.9 us)
Async XLA Ops:
  0.6 1.9 %copy-start = (bf16[3,8,64,1024]{3,2,1,0:T(8,128)(2,1)S(1)}, bf16[3,8,64,1024]{3,2,1,0:T(8,128)(2,1)}, u32[]{:S(2)}) copy-start(bf16[3,8,64,1024]{3,2,1,0:T(8,128)(2,1)} %in_ref.3) | copy-start | bytes 9437188
  2.5 0.9 copy-start.4
  3.5 3.1 %copy-start.1 = (bf16[64,64,32]{2,1,0:T(8,128)(2,1)S(1)}, bf16[64,64,32]{2,1,0:T(8,128)(2,1)}, u32[]{:S(2)}) copy-start(bf16[64,64,32]{2,1,0:T(8,128)(2,1)} %constant.28.clone.refs_3_) | copy-start | bytes 786436
  3.5 13.0 %copy-start.7 = (f32[16,2,64,64]{3,2,1,0:T(8,128)S(1)}, f32[16,2,64,64]{3,2,1,0:T(8,128)}, u32[]{:S(2)}) copy-start(f32[16,2,64,64]{3,2,1,0:T(8,128)} %w_ref.3) | copy-start | bytes 1572868
  5.2 34.9 %copy-start.8 = (bf16[64,16,128]{2,1,0:T(8,128)(2,1)S(1)}, bf16[64,16,128]{2,1,0:T(8,128)(2,1)}, u32[]{:S(2)}) copy-start(bf16[64,16,128]{2,1,0:T(8,128)(2,1)} %constant.29.clone.refs_2_) | copy-start | bytes 786436
  5.2 36.7 %copy-start.5 = (bf16[2,64,1024]{2,1,0:T(8,128)(2,1)S(1)}, bf16[2,64,1024]{2,1,0:T(8,128)(2,1)}, u32[]{:S(2)}) copy-start(bf16[2,64,1024]{2,1,0:T(8,128)(2,1)} %constant.27.clone.tab_ref) | copy-start | bytes 786436
  5.2 36.7 %copy-start.10 = (bf16[64,64]{1,0:T(8,128)(2,1)S(1)}, bf16[64,64]{1,0:T(8,128)(2,1)}, u32[]{:S(2)}) copy-start(bf16[64,64]{1,0:T(8,128)(2,1)} %w_ref.5) | copy-start | bytes 24580
  5.2 1.4 %collective-permute-start = (bf16[16,3,8,128]{3,2,1,0:T(8,128)(2,1)S(1)}, bf16[16,3,8,128]{3,2,1,0:T(8,128)(2,1)S(1)}, u32[]{:S(2)}, u32[]{:S(2)}) collective-permute-start(bf16[16,3,8,128]{3,2,1,0:T(8,128)(2,1)S(1)} %get-tuple-element.20), channel_id=1, source_target_pairs={{0,1},{1,0},{2,3},{3,2},{4,5},{5,4},{6,7},{7,6},{8,9},{9,8},{10,11... | collective-permute-start | bytes 294920 | tf_op jit(solution)/shard_map/ppermute | solution.py:306
  7.9 18.2 %all-to-all-start = ((bf16[32,48,128]{2,1,0:T(8,128)(2,1)}), bf16[32,48,128]{2,1,0:T(8,128)(2,1)S(1)}, u32[]{:S(2)}, u32[]{:S(2)}) async-start(bf16[32,48,128]{2,1,0:T(8,128)(2,1)} %shard_map.95), calls=%async_computation | async-start | bytes 786432 | tf_op jit(solution)/shard_map/all_to_all | solution.py:302
  40.5 1.4 %collective-permute-start.1 = (bf16[16,3,8,128]{3,2,1,0:T(8,128)(2,1)S(1)}, bf16[16,3,8,128]{3,2,1,0:T(8,128)(2,1)S(1)}, u32[]{:S(2)}, u32[]{:S(2)}) collective-permute-start(bf16[16,3,8,128]{3,2,1,0:T(8,128)(2,1)S(1)} %get-tuple-element.23), channel_id=1, source_target_pairs={{0,1},{1,0},{2,3},{3,2},{4,5},{5,4},{6,7},{7,6},{8,9},{9,8},{10,11... | collective-permute-start | bytes 294920 | tf_op jit(solution)/shard_map/ppermute | solution.py:306
  53.6 1.7 %copy-start.2 = (bf16[3,8,64,1024]{3,2,1,0:T(8,128)(2,1)}, bf16[3,8,64,1024]{3,2,1,0:T(8,128)(2,1)S(1)}, u32[]{:S(2)}) copy-start(bf16[3,8,64,1024]{3,2,1,0:T(8,128)(2,1)S(1)} %get-tuple-element.24.dpre_ref) | copy-start | bytes 9437188
  55.3 31.3 %copy-start.9 = (bf16[64,16,128]{2,1,0:T(8,128)(2,1)S(1)}, bf16[64,16,128]{2,1,0:T(8,128)(2,1)}, u32[]{:S(2)}) copy-start(bf16[64,16,128]{2,1,0:T(8,128)(2,1)} %constant.29.clone.refs_2_) | copy-start | bytes 786436
  55.3 1.3 %collective-permute-start.2 = (bf16[16,4,8,128]{3,2,1,0:T(8,128)(2,1)S(1)}, bf16[16,4,8,128]{3,2,1,0:T(8,128)(2,1)S(1)}, u32[]{:S(2)}, u32[]{:S(2)}) collective-permute-start(bf16[16,4,8,128]{3,2,1,0:T(8,128)(2,1)S(1)} %get-tuple-element.26), channel_id=1, source_target_pairs={{0,1},{1,0},{2,3},{3,2},{4,5},{5,4},{6,7},{7,6},{8,9},{9,8},{10,11... | collective-permute-start | bytes 393224 | tf_op jit(solution)/shard_map/ppermute | solution.py:306
  57.1 39.3 %copy-start.3 = (bf16[3,8,64,1024]{3,2,1,0:T(8,128)(2,1)S(1)}, bf16[3,8,64,1024]{3,2,1,0:T(8,128)(2,1)}, u32[]{:S(2)}) copy-start(bf16[3,8,64,1024]{3,2,1,0:T(8,128)(2,1)} %copy-done.2) | copy-start | bytes 9437188
  87.6 16.5 %all-to-all-start.4 = ((bf16[4,192,128]{2,1,0:T(8,128)(2,1)}), bf16[4,192,128]{2,1,0:T(8,128)(2,1)S(1)}, u32[]{:S(2)}, u32[]{:S(2)}) async-start(bf16[4,192,128]{2,1,0:T(8,128)(2,1)} %get-tuple-element.32), calls=%async_computation.4 | async-start | bytes 393216 | tf_op jit(solution)/shard_map/all_to_all | solution.py:302
  95.1 1.3 %collective-permute-start.3 = (bf16[16,3,8,128]{3,2,1,0:T(8,128)(2,1)S(1)}, bf16[16,3,8,128]{3,2,1,0:T(8,128)(2,1)S(1)}, u32[]{:S(2)}, u32[]{:S(2)}) collective-permute-start(bf16[16,3,8,128]{3,2,1,0:T(8,128)(2,1)S(1)} %get-tuple-element.31), channel_id=1, source_target_pairs={{0,1},{1,0},{2,3},{3,2},{4,5},{5,4},{6,7},{7,6},{8,9},{9,8},{10,11... | collective-permute-start | bytes 294920 | tf_op jit(solution)/shard_map/ppermute | solution.py:306
  96.4 1.0 copy-start.6

commit v3 on v2

--- a/solution.py
+++ b/solution.py
@@ -25,18 +25,16 @@
 INV_SCALE = 1.0 / math.sqrt(DMODES * TMODES)
 NN = (((1,), (0,)), ((), ()))
 NT = (((1,), (1,)), ((), ()))
-VMEM_LIMIT = 48 * 1024 * 1024
+MIB = 1024 * 1024
+GROUPS = ((0, 3), (3, 3), (6, 2))
 PAIRS = 48
 ROWS = 56
 
 
 def time_rows():
-    out = []
-    for core in range(2):
-        m = np.concatenate([core * 16 + np.arange(16), (1 - core) * 16 + np.arange(16)])
-        phase = ((m[:, None] * np.arange(DURATION)[None, :]) % DURATION) * (2.0 * np.pi / DURATION)
-        out.append(np.concatenate([np.cos(phase), -np.sin(phase)], axis=0))
-    return np.stack(out).astype(ml_dtypes.bfloat16)
+    m = np.arange(TMODES)
+    phase = ((m[:, None] * np.arange(DURATION)[None, :]) % DURATION) * (2.0 * np.pi / DURATION)
+    return np.concatenate([np.cos(phase), -np.sin(phase)], axis=0).astype(ml_dtypes.bfloat16)
 
 
 def depth_rows():
@@ -80,17 +78,38 @@
         cols = slice(xl * 64, xl * 64 + 64)
         block = jnp.concatenate([r[:32, cols], r[32:, cols]], axis=1)
         scratch[pl.ds(xl, 32, stride=8), :] = block
-    return scratch[...].reshape(32, 8, 128).astype(BF16)
+    core = lax.axis_index("core")
+    return [
+        scratch[pl.ds(pl.multiple_of(c * 128, 128), 128), :].reshape(16, 8, 128).astype(BF16)
+        for c in (core, 1 - core)
+    ]
 
 
 def load_rows(own_ref, other_ref, scratch):
-    scratch[:128] = own_ref[:, 0].astype(F32).reshape(128, 128)
-    scratch[128:] = other_ref[:, 0].astype(F32).reshape(128, 128)
+    core = lax.axis_index("core")
+    for c, ref in ((core, own_ref), (1 - core, other_ref)):
+        scratch[pl.ds(pl.multiple_of(c * 128, 128), 128), :] = ref[:, 0].astype(F32).reshape(128, 128)
 
 
 def mode_block(scratch, xl):
     g = scratch[pl.ds(xl, 32, stride=8), :]
     return jnp.concatenate([g[:, :64], g[:, 64:]], axis=0)
+
+
+def left_of(blocks, mixing):
+    zero = jnp.zeros((64, 64), BF16)
+    rows = []
+    for i, g in enumerate(blocks):
+        rows.append(jnp.concatenate([g] + [mixing if k == i else zero for k in range(len(blocks))], axis=1))
+    return jnp.concatenate(rows, axis=0)
+
+
+def gelu_slope(pre, cot):
+    root = math.sqrt(2.0 / math.pi)
+    p = (root * 0.044715) * (pre * pre) + root
+    th = jnp.tanh(pre * p)
+    q = 3.0 * p - 2.0 * root
+    return ((1.0 + th) * (1.0 + (pre * q) * (1.0 - th))) * (0.5 * cot)
 
 
 def own_pair(kp, rows):
@@ -104,10 +123,8 @@
 
 
 def coeff_kernel(in_ref, tab_ref, own_ref, send_ref, scratch):
-    table = tab_ref[lax.axis_index("core")]
-    rows = emit_rows(dot(table, in_ref[0].reshape(512, DURATION), NT) * SCALE, scratch)
-    own_ref[:, 0] = rows[:16]
-    send_ref[:, 0] = rows[16:]
+    r = dot(tab_ref[...], in_ref[0].reshape(512, DURATION), NT) * SCALE
+    own_ref[:, 0], send_ref[:, 0] = emit_rows(r, scratch)
 
 
 def spread_kernel(f_ref, own_ref, other_ref, tab_ref, o_ref, scratch, *point, rows):
@@ -213,29 +230,32 @@
         point[...] = jnp.zeros_like(point)
 
     load_rows(got_ref, other_ref, rows)
-    table = tab_ref.at[lax.axis_index("core")]
     mix_t = w_ref[...].astype(F32).T.astype(BF16)
-    root = math.sqrt(2.0 / math.pi)
-    for xl in range(8):
-        g = (mode_block(rows, xl).T * INV_SCALE).astype(BF16)
+    total = point[...]
+    drows = []
+    for first, n in GROUPS:
+        blocks = [(mode_block(rows, first + i).T * INV_SCALE).astype(BF16) for i in range(n)]
+        left = left_of(blocks, mix_t)
         for chunk in range(4):
             ts = slice(chunk * 256, chunk * 256 + 256)
-            pre = dot(g, table[:, ts]) + dot(mix_t, in_ref[0, xl, :, ts])
-            sq = pre * pre
-            th = jnp.tanh(pre * (root + (root * 0.044715) * sq))
-            slope = 0.5 + 0.5 * th + (0.5 * pre) * (1.0 - th * th) * (
-                root + (3.0 * root * 0.044715) * sq
+            right = jnp.concatenate(
+                [tab_ref[:, ts]] + [in_ref[0, first + i, :, ts] for i in range(n)], axis=0
             )
-            dpre_ref[0, xl, :, ts] = (slope * cot_ref[0, xl, :, ts].astype(F32)).astype(BF16)
-        point[...] += dot(in_ref[0, xl], dpre_ref[0, xl], NT)
-    r = dot(table[...], dpre_ref[0].reshape(512, DURATION), NT) * INV_SCALE
-    out = emit_rows(r, scratch)
-    own_ref[:, b] = out[:16]
-    send_ref[:, b] = out[16:]
+            pre = dot(left, right)
+            for i in range(n):
+                slope = gelu_slope(pre[i * 64 : i * 64 + 64], cot_ref[0, first + i, :, ts].astype(F32))
+                dpre_ref[0, first + i, :, ts] = slope.astype(BF16)
+        left = jnp.concatenate([tab_ref[...]] + [in_ref[0, first + i] for i in range(n)], axis=0)
+        r = dot(left, dpre_ref[0, first : first + n].reshape(n * 64, DURATION), NT)
+        drows.append(r[:64])
+        for i in range(n):
+            total = total + r[64 + i * 64 : 128 + i * 64, i * 64 : i * 64 + 64]
+    point[...] = total
+    out = emit_rows(jnp.concatenate(drows, axis=1) * INV_SCALE, scratch)
+    own_ref[:, b], send_ref[:, b] = out
 
     @pl.when(b == 2)
     def _():
-        total = point[...]
         pair = split_pair(jnp.concatenate([total, total], axis=1))
         pair = jnp.concatenate([pair, jnp.zeros_like(pair)], axis=0).reshape(16, 8, 128).astype(BF16)
         own_ref[:, 3] = pair
@@ -244,14 +264,17 @@
 
 def grad_kernel(dpre_ref, got_ref, other_ref, tab_ref, w_ref, o_ref, rows):
     load_rows(got_ref, other_ref, rows)
-    table = tab_ref.at[lax.axis_index("core")]
     mixing = w_ref[...]
-    for xl in range(8):
-        g = mode_block(rows, xl).T.astype(BF16)
+    for first, n in GROUPS:
+        left = left_of([mode_block(rows, first + i).T.astype(BF16) for i in range(n)], mixing)
         for chunk in range(4):
             ts = slice(chunk * 256, chunk * 256 + 256)
-            total = dot(g, table[:, ts]) + dot(mixing, dpre_ref[0, xl, :, ts])
-            o_ref[0, xl, :, ts] = total.astype(BF16)
+            right = jnp.concatenate(
+                [tab_ref[:, ts]] + [dpre_ref[0, first + i, :, ts] for i in range(n)], axis=0
+            )
+            grad = dot(left, right).astype(BF16)
+            for i in range(n):
+                o_ref[0, first + i, :, ts] = grad[i * 64 : i * 64 + 64]
 
 
 def weight_grad_kernel(fact_ref, spec_ref, point_ref):
@@ -279,7 +302,7 @@
     return pl.BlockSpec(shape, lambda *_: (0,) * len(shape))
 
 
-def call(kernel, out_shape, grid, in_specs, out_specs, scratch=(), prefetch=0):
+def call(kernel, out_shape, grid, in_specs, out_specs, scratch=(), prefetch=0, limit=8):
     return pl.pallas_call(
         kernel,
         out_shape=out_shape,
@@ -290,7 +313,7 @@
             out_specs=out_specs,
             scratch_shapes=list(scratch),
         ),
-        compiler_params=pltpu.CompilerParams(vmem_limit_bytes=VMEM_LIMIT),
+        compiler_params=pltpu.CompilerParams(vmem_limit_bytes=limit * MIB),
     )
 
 
@@ -312,7 +335,7 @@
     place = lax.axis_index(FIELD).reshape(1)
     field_block = pl.BlockSpec((1, 8, 64, DURATION), lambda b: (b, 0, 0, 0))
     part_block = pl.BlockSpec((16, 1, 8, 128), lambda b: (0, b, 0, 0))
-    tab_block = whole((2, 64, DURATION))
+    tab_block = whole((64, DURATION))
     mix_block = whole((64, 64))
     forward_block = pl.BlockSpec((1, 64, 32), lambda i, f: (f[0], 0, 0))
     inverse_block = pl.BlockSpec((1, 16, 128), lambda i, f: (f[0], 0, 0))
@@ -343,6 +366,7 @@
         [field_block, tab_block],
         (part_block, part_block),
         [pltpu.VMEM((256, 128), F32)],
+        limit=14,
     )(inputs, tab)
     got = exchange(spread(own, to_other_core(send), PAIRS), CHIP)
     mixed, spectrum = call(
@@ -369,6 +393,7 @@
         [field_block, field_block, part_block, part_block, tab_block, mix_block],
         (field_block, whole(part4.shape), whole(part4.shape)),
         [pltpu.VMEM((256, 128), F32), pltpu.VMEM((256, 128), F32), pltpu.VMEM((64, 64), F32)],
+        limit=14,
     )(inputs, cotangent, own, to_other_core(send), tab, point_weight)
     got = exchange(spread(own, to_other_core(send), ROWS), CHIP)
     dmodes, dmixed = call(
@@ -396,6 +421,7 @@
         [field_block, part_block, part_block, tab_block, mix_block],
         field_block,
         [pltpu.VMEM((256, 128), F32)],
+        limit=14,
     )(dpre, own, to_other_core(send), tab, point_weight)
     spec_grad, point_grad = call(
         weight_grad_kernel,

time: 107 us -> 108 us (level)
  local copies, waits for them, and re-layouts: 5.48 us -> 12.6 us
  Pallas kernels: 22.6 us -> 17.9 us
    unnamed x22 -> x34, local copies, waits for them, and re-layouts: 5.48 us -> 12.6 us
    pallas_call x1, Pallas kernels: 11.7 us -> 6.33 us  [local(): call(field_kernel, (shape(3, 8, 64, DURATION), part4, part4), (3,), [fiel...]
  transfers between devices with their start and end apart: 6 -> 6, of which waited for: 6 -> 6; matrix products, arithmetic and copies ran while one was open for 0% -> 0% of each run, Pallas kernels for 4% -> 3%
where the time goes in v3:
time: 108 us; the launch traced here: 107 us
  blocking collectives  42.4 us (39%)
  Pallas kernels  17.9 us (17%)
  waiting for transfers between devices  17.2 us (16%)
  starting transfers between devices  16.4 us (15%)
  local copies, waits for them, and re-layouts  12.6 us (12%)
    all_to_all x3, blocking collectives, exchange(): return lax.all_to_all(v, axes, 0, 0, tiled=True)  42.4 us
    all_to_all x2, starting transfers between devices, exchange(): return lax.all_to_all(v, axes, 0, 0, tiled=True)  16.2 us
    unnamed x34, local copies, waits for them, and re-layouts  12.6 us
    all_to_all x2, waiting for transfers between devices, exchange(): return lax.all_to_all(v, axes, 0, 0, tiled=True)  11.7 us
    pallas_call x1, Pallas kernels, local(): call(field_kernel, (shape(3, 8, 64, DURATION), part4, part4), (3,), [fiel...  6.33 us
    ppermute x4, waiting for transfers between devices, to_other_core(): return lax.ppermute(v, 'core', [(0, 1), (1, 0)])  5.5 us
    pallas_call x1, Pallas kernels, local(): call(grad_kernel, shape(3, 8, 64, DURATION), (3,), [field_block, part_blo...  3.18 us
    pallas_call x1, Pallas kernels, local(): call(coeff_kernel, (part, part), (3,), [field_block, tab_block], (part_bl...  2.33 us
  transfers between devices with their start and end apart: 6, of which 6 were waited for; matrix products, arithmetic and copies ran while one was open for 0% of the time, Pallas kernels for 3%

profile of v3, /device:TPU:32, one launch (start us, length us, event | category | flops | bytes accessed | tf_op | source)
XLA Modules:
  0.0 107.3 jit_solution(3252312819691344360)
XLA Ops:
  0.6 1.9 %copy-done = bf16[3,8,64,1024]{3,2,1,0:T(8,128)(2,1)S(1)} copy-done((bf16[3,8,64,1024]{3,2,1,0:T(8,128)(2,1)S(1)}, bf16[3,8,64,1024]{3,2,1,0:T(8,128)(2,1)}, u32[]{:S(2)}) %copy-start) | copy-done | bytes 3145752
  2.5 0.9 copy-done.7
  3.4 2.3 %shard_map.94 = (bf16[16,3,8,128]{3,2,1,0:T(8,128)(2,1)S(1)}, bf16[16,3,8,128]{3,2,1,0:T(8,128)(2,1)}) custom-call(bf16[3,8,64,1024]{3,2,1,0:T(8,128)(2,1)S(1)} %copy-done, bf16[64,1024]{1,0:T(8,128)(2,1)S(1)} %copy-done.7), custom_call_target="tpu_custom_call" | custom-call | tf_op jit(solution)/shard_map/pallas_call | solution.py:362
  5.8 1.5 %collective-permute-done.refs_2_ = bf16[16,3,8,128]{3,2,1,0:T(8,128)(2,1)S(1)} collective-permute-done((bf16[16,3,8,128]{3,2,1,0:T(8,128)(2,1)}, bf16[16,3,8,128]{3,2,1,0:T(8,128)(2,1)S(1)}, u32[]{:S(2)}, u32[]{:S(2)}) %collective-permute-start) | collective-permute-done | bytes 98336 | tf_op jit(solution)/shard_map/ppermute | solution.py:329
  7.3 1.2 %copy-done.2 = bf16[64,64,32]{2,1,0:T(8,128)(2,1)S(1)} copy-done((bf16[64,64,32]{2,1,0:T(8,128)(2,1)S(1)}, bf16[64,64,32]{2,1,0:T(8,128)(2,1)}, u32[]{:S(2)}) %copy-start.2) | copy-done | bytes 262168
  8.5 1.3 %shard_map.95 = bf16[32,48,128]{2,1,0:T(8,128)(2,1)} custom-call(s32[1]{0:T(128)} %bitcast.refs_0_, bf16[16,3,8,128]{3,2,1,0:T(8,128)(2,1)S(1)} %get-tuple-element.19.refs_1_, bf16[16,3,8,128]{3,2,1,0:T(8,128)(2,1)S(1)} %collective-permute-done.refs_2_, bf16[64,64,32]{2,1,0:T(8,128)(2,1)S(1)} %copy-done.2), custom_call_target="tpu_custom_call" | custom-call | tf_op jit(solution)/shard_map/pallas_call | solution.py:349
  9.8 8.6 %all-to-all-start = ((bf16[32,48,128]{2,1,0:T(8,128)(2,1)}), bf16[32,48,128]{2,1,0:T(8,128)(2,1)}, u32[]{:S(2)}, u32[]{:S(2)}) async-start(bf16[32,48,128]{2,1,0:T(8,128)(2,1)} %shard_map.95), calls=%async_computation | async-start | bytes 786432 | tf_op jit(solution)/shard_map/all_to_all | solution.py:325
  18.4 1.2 %copy-done.9 = f32[16,2,64,64]{3,2,1,0:T(8,128)S(1)} copy-done((f32[16,2,64,64]{3,2,1,0:T(8,128)S(1)}, f32[16,2,64,64]{3,2,1,0:T(8,128)}, u32[]{:S(2)}) %copy-start.9) | copy-done | bytes 524312
  19.8 8.3 %all-to-all-done.recv_ref = bf16[32,48,128]{2,1,0:T(8,128)(2,1)} async-done(((bf16[32,48,128]{2,1,0:T(8,128)(2,1)}), bf16[32,48,128]{2,1,0:T(8,128)(2,1)}, u32[]{:S(2)}, u32[]{:S(2)}) %all-to-all-start) | async-done | bytes 393248 | tf_op jit(solution)/shard_map/all_to_all | solution.py:325
  28.1 1.4 %shard_map.97 = (bf16[32,48,128]{2,1,0:T(8,128)(2,1)S(1)}, f32[48,128]{1,0:T(8,128)S(1)}) custom-call(bf16[32,48,128]{2,1,0:T(8,128)(2,1)} %all-to-all-done.recv_ref, bf16[16,64,128]{2,1,0:T(8,128)(2,1)S(1)} %shard_map.96.w_ref), custom_call_target="tpu_custom_call" | custom-call | tf_op jit(solution)/shard_map/pallas_call | solution.py:372
  29.5 13.6 %all_to_all.25.refs_1_ = bf16[32,48,128]{2,1,0:T(8,128)(2,1)S(1)} all-to-all(bf16[32,48,128]{2,1,0:T(8,128)(2,1)S(1)} %get-tuple-element.21), channel_id=1, replica_groups=mesh['dp'=4,'z'=2,'y'=4,'x'=4,'core'=2] {'z','y','x'}, dimensions={0} | all-to-all | bytes 786432 | tf_op jit(solution)/shard_map/all_to_all | solution.py:325
  43.1 0.9 copy-done.10
  44.6 1.3 %collective-permute-done.1.other_ref = bf16[16,3,8,128]{3,2,1,0:T(8,128)(2,1)S(1)} collective-permute-done((bf16[16,3,8,128]{3,2,1,0:T(8,128)(2,1)S(1)}, bf16[16,3,8,128]{3,2,1,0:T(8,128)(2,1)S(1)}, u32[]{:S(2)}, u32[]{:S(2)}) %collective-permute-start.1) | collective-permute-done | bytes 98336 | tf_op jit(solution)/shard_map/ppermute | solution.py:329
  45.9 1.9 %copy-done.4 = bf16[3,8,64,1024]{3,2,1,0:T(8,128)(2,1)S(1)} copy-done((bf16[3,8,64,1024]{3,2,1,0:T(8,128)(2,1)S(1)}, bf16[3,8,64,1024]{3,2,1,0:T(8,128)(2,1)}, u32[]{:S(2)}) %copy-start.4) | copy-done | bytes 3145752
  47.8 6.3 %shard_map.99 = (bf16[3,8,64,1024]{3,2,1,0:T(8,128)(2,1)S(1)}, bf16[16,4,8,128]{3,2,1,0:T(8,128)(2,1)S(1)}, bf16[16,4,8,128]{3,2,1,0:T(8,128)(2,1)S(1)}) custom-call(bf16[3,8,64,1024]{3,2,1,0:T(8,128)(2,1)S(1)} %copy-done.1, bf16[3,8,64,1024]{3,2,1,0:T(8,128)(2,1)S(1)} %copy-done.4, bf16[16,3,8,128]{3,2,1,0:T(8,128)(2,1)S(1)} %get-tuple-element.22.got_ref, ...), custom_call_target="tpu_custom_call" | custom-call | tf_op jit(solution)/shard_map/pallas_call | solution.py:389
  54.1 1.7 %copy-done.5 = bf16[3,8,64,1024]{3,2,1,0:T(8,128)(2,1)} copy-done((bf16[3,8,64,1024]{3,2,1,0:T(8,128)(2,1)}, bf16[3,8,64,1024]{3,2,1,0:T(8,128)(2,1)S(1)}, u32[]{:S(2)}) %copy-start.5) | copy-done | bytes 3145752
  55.9 1.2 %collective-permute-done.2.refs_2_ = bf16[16,4,8,128]{3,2,1,0:T(8,128)(2,1)S(1)} collective-permute-done((bf16[16,4,8,128]{3,2,1,0:T(8,128)(2,1)S(1)}, bf16[16,4,8,128]{3,2,1,0:T(8,128)(2,1)S(1)}, u32[]{:S(2)}, u32[]{:S(2)}) %collective-permute-start.2) | collective-permute-done | bytes 131104 | tf_op jit(solution)/shard_map/ppermute | solution.py:329
  57.6 14.8 %all_to_all.26.recv_ref = bf16[32,56,128]{2,1,0:T(8,128)(2,1)S(1)} all-to-all(bf16[32,56,128]{2,1,0:T(8,128)(2,1)S(1)} %shard_map.100), channel_id=1, replica_groups=mesh['dp'=4,'z'=2,'y'=4,'x'=4,'core'=2] {'z','y','x'}, dimensions={0} | all-to-all | bytes 917504 | tf_op jit(solution)/shard_map/all_to_all | solution.py:325
  72.8 14.0 %all_to_all.27.refs_1_ = bf16[32,56,128]{2,1,0:T(8,128)(2,1)S(1)} all-to-all(bf16[32,56,128]{2,1,0:T(8,128)(2,1)S(1)} %get-tuple-element.27), channel_id=1, replica_groups=mesh['dp'=4,'z'=2,'y'=4,'x'=4,'core'=2] {'z','y','x'}, dimensions={0} | all-to-all | bytes 917504 | tf_op jit(solution)/shard_map/all_to_all | solution.py:325
  89.2 7.6 %all-to-all-start.4 = ((bf16[4,192,128]{2,1,0:T(8,128)(2,1)}), bf16[4,192,128]{2,1,0:T(8,128)(2,1)S(1)}, u32[]{:S(2)}, u32[]{:S(2)}) async-start(bf16[4,192,128]{2,1,0:T(8,128)(2,1)} %copy-done.12), calls=%async_computation.4 | async-start | bytes 393216 | tf_op jit(solution)/shard_map/all_to_all | solution.py:325
  96.8 1.5 %collective-permute-done.3.other_ref = bf16[16,3,8,128]{3,2,1,0:T(8,128)(2,1)S(1)} collective-permute-done((bf16[16,3,8,128]{3,2,1,0:T(8,128)(2,1)}, bf16[16,3,8,128]{3,2,1,0:T(8,128)(2,1)S(1)}, u32[]{:S(2)}, u32[]{:S(2)}) %collective-permute-start.3) | collective-permute-done | bytes 98336 | tf_op jit(solution)/shard_map/ppermute | solution.py:329
  99.2 3.2 %shard_map.103 = bf16[3,8,64,1024]{3,2,1,0:T(8,128)(2,1)} custom-call(bf16[3,8,64,1024]{3,2,1,0:T(8,128)(2,1)S(1)} %copy-done.6, bf16[16,3,8,128]{3,2,1,0:T(8,128)(2,1)S(1)} %copy-done.14, bf16[16,3,8,128]{3,2,1,0:T(8,128)(2,1)S(1)} %collective-permute-done.3.other_ref, bf16[64,1024]{1,0:T(8,128)(2,1)S(1)} %copy-done.8, bf16[64,64]{1,0:T(8,128)(2,1)S(1)} %copy-done.15), custom_call_target="tpu_custom_call" | custom-call | tf_op jit(solution)/shard_map/pallas_call | solution.py:417
  102.4 3.4 %all-to-all-done.4.fact_ref = bf16[4,192,128]{2,1,0:T(8,128)(2,1)S(1)} async-done(((bf16[4,192,128]{2,1,0:T(8,128)(2,1)}), bf16[4,192,128]{2,1,0:T(8,128)(2,1)S(1)}, u32[]{:S(2)}, u32[]{:S(2)}) %all-to-all-start.4) | async-done | bytes 196640 | tf_op jit(solution)/shard_map/all_to_all | solution.py:325
  105.7 1.6 %shard_map.104 = (f32[16,2,64,64]{3,2,1,0:T(8,128)}, f32[64,64]{1,0:T(8,128)}) custom-call(bf16[4,192,128]{2,1,0:T(8,128)(2,1)S(1)} %all-to-all-done.4.fact_ref), custom_call_target="tpu_custom_call" | custom-call | tf_op jit(solution)/shard_map/pallas_call | solution.py:426
  (36 shorter events, 5.0 us)
Async XLA Ops:
  0.6 1.9 %copy-start = (bf16[3,8,64,1024]{3,2,1,0:T(8,128)(2,1)S(1)}, bf16[3,8,64,1024]{3,2,1,0:T(8,128)(2,1)}, u32[]{:S(2)}) copy-start(bf16[3,8,64,1024]{3,2,1,0:T(8,128)(2,1)} %in_ref.3) | copy-start | bytes 9437188
  2.5 0.9 copy-start.7
  3.4 42.4 %copy-start.8 = (bf16[64,1024]{1,0:T(8,128)(2,1)S(1)}, bf16[64,1024]{1,0:T(8,128)(2,1)}, u32[]{:S(2)}) copy-start(bf16[64,1024]{1,0:T(8,128)(2,1)} %constant.27.clone.tab_ref) | copy-start | bytes 393220
  3.4 42.4 %copy-start.15 = (bf16[64,64]{1,0:T(8,128)(2,1)S(1)}, bf16[64,64]{1,0:T(8,128)(2,1)}, u32[]{:S(2)}) copy-start(bf16[64,64]{1,0:T(8,128)(2,1)} %w_ref.5) | copy-start | bytes 24580
  5.8 40.1 %copy-start.1 = (bf16[3,8,64,1024]{3,2,1,0:T(8,128)(2,1)S(1)}, bf16[3,8,64,1024]{3,2,1,0:T(8,128)(2,1)}, u32[]{:S(2)}) copy-start(bf16[3,8,64,1024]{3,2,1,0:T(8,128)(2,1)} %in_ref.3) | copy-start | bytes 9437188
  5.8 1.5 %collective-permute-start = (bf16[16,3,8,128]{3,2,1,0:T(8,128)(2,1)}, bf16[16,3,8,128]{3,2,1,0:T(8,128)(2,1)S(1)}, u32[]{:S(2)}, u32[]{:S(2)}) collective-permute-start(bf16[16,3,8,128]{3,2,1,0:T(8,128)(2,1)} %get-tuple-element.20), channel_id=1, source_target_pairs={{0,1},{1,0},{2,3},{3,2},{4,5},{5,4},{6,7},{7,6},{8,9},{9,8},{10,11... | collective-permute-start | bytes 294920 | tf_op jit(solution)/shard_map/ppermute | solution.py:329
  7.3 1.2 %copy-start.2 = (bf16[64,64,32]{2,1,0:T(8,128)(2,1)S(1)}, bf16[64,64,32]{2,1,0:T(8,128)(2,1)}, u32[]{:S(2)}) copy-start(bf16[64,64,32]{2,1,0:T(8,128)(2,1)} %constant.28.clone.refs_3_) | copy-start | bytes 786436
  9.8 18.3 %all-to-all-start = ((bf16[32,48,128]{2,1,0:T(8,128)(2,1)}), bf16[32,48,128]{2,1,0:T(8,128)(2,1)}, u32[]{:S(2)}, u32[]{:S(2)}) async-start(bf16[32,48,128]{2,1,0:T(8,128)(2,1)} %shard_map.95), calls=%async_computation | async-start | bytes 786432 | tf_op jit(solution)/shard_map/all_to_all | solution.py:325
  18.4 1.2 %copy-start.9 = (f32[16,2,64,64]{3,2,1,0:T(8,128)S(1)}, f32[16,2,64,64]{3,2,1,0:T(8,128)}, u32[]{:S(2)}) copy-start(f32[16,2,64,64]{3,2,1,0:T(8,128)} %w_ref.3) | copy-start | bytes 1572868
  43.1 1.0 copy-start.10
  44.5 1.4 %collective-permute-start.1 = (bf16[16,3,8,128]{3,2,1,0:T(8,128)(2,1)S(1)}, bf16[16,3,8,128]{3,2,1,0:T(8,128)(2,1)S(1)}, u32[]{:S(2)}, u32[]{:S(2)}) collective-permute-start(bf16[16,3,8,128]{3,2,1,0:T(8,128)(2,1)S(1)} %get-tuple-element.23), channel_id=1, source_target_pairs={{0,1},{1,0},{2,3},{3,2},{4,5},{5,4},{6,7},{7,6},{8,9},{9,8},{10,11... | collective-permute-start | bytes 294920 | tf_op jit(solution)/shard_map/ppermute | solution.py:329
  45.9 1.9 %copy-start.4 = (bf16[3,8,64,1024]{3,2,1,0:T(8,128)(2,1)S(1)}, bf16[3,8,64,1024]{3,2,1,0:T(8,128)(2,1)}, u32[]{:S(2)}) copy-start(bf16[3,8,64,1024]{3,2,1,0:T(8,128)(2,1)} %cot_ref.1) | copy-start | bytes 9437188
  47.8 9.4 %copy-start.3 = (bf16[64,64,32]{2,1,0:T(8,128)(2,1)S(1)}, bf16[64,64,32]{2,1,0:T(8,128)(2,1)}, u32[]{:S(2)}) copy-start(bf16[64,64,32]{2,1,0:T(8,128)(2,1)} %constant.28.clone.refs_3_) | copy-start | bytes 786436
  54.1 1.7 %copy-start.5 = (bf16[3,8,64,1024]{3,2,1,0:T(8,128)(2,1)}, bf16[3,8,64,1024]{3,2,1,0:T(8,128)(2,1)S(1)}, u32[]{:S(2)}) copy-start(bf16[3,8,64,1024]{3,2,1,0:T(8,128)(2,1)S(1)} %get-tuple-element.24.dpre_ref) | copy-start | bytes 9437188
  55.8 31.0 %copy-start.11 = (bf16[64,16,128]{2,1,0:T(8,128)(2,1)S(1)}, bf16[64,16,128]{2,1,0:T(8,128)(2,1)}, u32[]{:S(2)}) copy-start(bf16[64,16,128]{2,1,0:T(8,128)(2,1)} %constant.29.clone.refs_2_) | copy-start | bytes 786436
  55.8 42.5 %copy-start.6 = (bf16[3,8,64,1024]{3,2,1,0:T(8,128)(2,1)S(1)}, bf16[3,8,64,1024]{3,2,1,0:T(8,128)(2,1)}, u32[]{:S(2)}) copy-start(bf16[3,8,64,1024]{3,2,1,0:T(8,128)(2,1)} %copy-done.5) | copy-start | bytes 9437188
  55.8 1.3 %collective-permute-start.2 = (bf16[16,4,8,128]{3,2,1,0:T(8,128)(2,1)S(1)}, bf16[16,4,8,128]{3,2,1,0:T(8,128)(2,1)S(1)}, u32[]{:S(2)}, u32[]{:S(2)}) collective-permute-start(bf16[16,4,8,128]{3,2,1,0:T(8,128)(2,1)S(1)} %get-tuple-element.26), channel_id=1, source_target_pairs={{0,1},{1,0},{2,3},{3,2},{4,5},{5,4},{6,7},{7,6},{8,9},{9,8},{10,11... | collective-permute-start | bytes 393224 | tf_op jit(solution)/shard_map/ppermute | solution.py:329
  87.2 0.7 copy-start.12
  87.9 0.6 copy-start.13
  88.6 0.6 copy-start.16
  89.2 16.5 %all-to-all-start.4 = ((bf16[4,192,128]{2,1,0:T(8,128)(2,1)}), bf16[4,192,128]{2,1,0:T(8,128)(2,1)S(1)}, u32[]{:S(2)}, u32[]{:S(2)}) async-start(bf16[4,192,128]{2,1,0:T(8,128)(2,1)} %copy-done.12), calls=%async_computation.4 | async-start | bytes 393216 | tf_op jit(solution)/shard_map/all_to_all | solution.py:325
  96.8 1.5 %collective-permute-start.3 = (bf16[16,3,8,128]{3,2,1,0:T(8,128)(2,1)}, bf16[16,3,8,128]{3,2,1,0:T(8,128)(2,1)S(1)}, u32[]{:S(2)}, u32[]{:S(2)}) collective-permute-start(bf16[16,3,8,128]{3,2,1,0:T(8,128)(2,1)} %copy-done.16), channel_id=1, source_target_pairs={{0,1},{1,0},{2,3},{3,2},{4,5},{5,4},{6,7},{7,6},{8,9},{9,8},{10,11... | collective-permute-start | bytes 294920 | tf_op jit(solution)/shard_map/ppermute | solution.py:329
  98.3 0.9 copy-start.14

commit v4 on v3

v4 whole, which is shorter than its diff:
```python
import functools
import math

import jax
import jax.numpy as jnp
import ml_dtypes
import numpy as np
from jax import lax
from jax.experimental import pallas as pl
from jax.experimental.pallas import tpu as pltpu
from jax.sharding import Mesh
from jax.sharding import PartitionSpec as P

DEPTH = 512
DURATION = 1024
CHANNELS = 64
DMODES = 32
TMODES = 32
BATCH = 12

CHIP = ("z", "y", "x")
FIELD = CHIP + ("core",)
BF16 = jnp.bfloat16
F32 = jnp.float32
SCALE = 1.0 / math.sqrt(DEPTH * DURATION)
INV_SCALE = 1.0 / math.sqrt(DMODES * TMODES)
NN = (((1,), (0,)), ((), ()))
NT = (((1,), (1,)), ((), ()))
MIB = 1024 * 1024
FIELDS = 24
GROUPS = 8
PAIRS = 48
ROWS = 56


def time_rows():
    m = np.arange(TMODES)
    phase = ((m[:, None] * np.arange(DURATION)[None, :]) % DURATION) * (2.0 * np.pi / DURATION)
    return np.concatenate([np.cos(phase), -np.sin(phase)], axis=0).astype(ml_dtypes.bfloat16)


def depth_table(k, x, sine):
    freq = jnp.where(k < DMODES // 2, k, k - DMODES)
    phase = ((freq * x - jnp.where(sine, DEPTH // 4, 0) + DEPTH // 2) & (DEPTH - 1)) - DEPTH // 2
    return jnp.cos(phase.astype(F32) * (2.0 * math.pi / DEPTH))


def high_or_low(v, low):
    high = v.astype(BF16).astype(F32)
    return jnp.where(low, v - high, high).astype(BF16)


def position(i):
    return 8 * (lax.axis_index(FIELD) ^ (i >> 3)) + (i & 7)


def forward_table():
    row = lax.broadcasted_iota(jnp.int32, (64, 32), 0)
    col = lax.broadcasted_iota(jnp.int32, (64, 32), 1)
    return high_or_low(depth_table(row & 31, position(col & 15), row >= 32), col >= 16)


def inverse_table():
    row = lax.broadcasted_iota(jnp.int32, (16, 128), 0)
    col = lax.broadcasted_iota(jnp.int32, (16, 128), 1)
    return high_or_low(depth_table(col & 31, position(row), (col & 32) != 0), col >= 64)


def lanes(shape):
    return lax.broadcasted_iota(jnp.int32, shape, len(shape) - 1)


def swap(v):
    return pltpu.roll(v, 64, 1)


def turn(v, first):
    return swap(v) * jnp.where(lanes(v.shape) < 64, first, -first).astype(F32)


def split_pair(v):
    high = v.astype(BF16).astype(F32)
    return jnp.where(lanes(v.shape) < 64, high, v - high)


def dot(a, b, dims=NN):
    return lax.dot_general(a, b, dims, preferred_element_type=F32)


def store_rows(scratch, own_ref, send_ref):
    core = lax.axis_index("core")
    for b in range(3):
        for c, ref in ((core, own_ref), (1 - core, send_ref)):
            rows = scratch[pl.ds(pl.multiple_of(b * 256 + c * 128, 128), 128), :]
            ref[:, b] = rows.reshape(16, 8, 128).astype(BF16)


def load_rows(own_ref, other_ref, scratch):
    core = lax.axis_index("core")
    for b in range(3):
        for c, ref in ((core, own_ref), (1 - core, other_ref)):
            rows = ref[:, b].astype(F32).reshape(128, 128)
            scratch[pl.ds(pl.multiple_of(b * 256 + c * 128, 128), 128), :] = rows


def field_rows(field):
    b, xl = divmod(field, 8)
    return pl.ds(b * 256 + xl, 32, stride=8)


def mode_block(scratch, field):
    g = scratch[field_rows(field), :]
    return jnp.concatenate([g[:, :64], g[:, 64:]], axis=0).T


def left_of(blocks, mixing):
    zero = jnp.zeros((64, 64), BF16)
    rows = []
    for i, g in enumerate(blocks):
        rows.append(jnp.concatenate([g] + [mixing if k == i else zero for k in range(len(blocks))], axis=1))
    return jnp.concatenate(rows, axis=0)


def gelu_slope(pre, cot):
    root = math.sqrt(2.0 / math.pi)
    p = (root * 0.044715) * (pre * pre) + root
    th = jnp.tanh(pre * p)
    q = 3.0 * p - 2.0 * root
    return ((1.0 + th) * (1.0 + (pre * q) * (1.0 - th))) * (0.5 * cot)


def own_pair(kp, rows):
    row = lax.broadcasted_iota(jnp.int32, (rows, 128), 0)
    first = row - lanes((rows, 128)) // 64 * 3 - 6 * kp
    return (first >= 0) & (first < 3)


def coeff_kernel(
    in_ref, tab_ref, mix_ref, own_ref, send_ref, table, mixing, fields, scratch, sems
):
    copies = [
        pltpu.make_async_copy(tab_ref, table, sems.at[3]),
        pltpu.make_async_copy(mix_ref, mixing, sems.at[4]),
    ]
    for b in range(3):
        part = pl.ds(8 * b, 8)
        copies.append(pltpu.make_async_copy(in_ref.at[part], fields.at[part], sems.at[b]))
    for copy in copies:
        copy.start()
    copies[0].wait()
    for b in range(3):
        copies[2 + b].wait()
        coeffs = dot(table[...], fields[8 * b : 8 * b + 8].reshape(512, DURATION), NT) * SCALE
        for i in range(8):
            cols = slice(i * 64, i * 64 + 64)
            scratch[field_rows(8 * b + i), :] = jnp.concatenate([coeffs[:32, cols], coeffs[32:, cols]], axis=1)
    store_rows(scratch, own_ref, send_ref)
    copies[1].wait()


def weight_kernel(w_ref, o_ref, scratch, sem):
    copy = pltpu.make_async_copy(w_ref, scratch, sem)
    copy.start()
    copy.wait()
    o_ref[...] = jnp.concatenate([scratch[:, 0], scratch[:, 1]], axis=2).astype(BF16)


def spread_kernel(own_ref, other_ref, o_ref, scratch, *point, rows):
    table = forward_table()
    both = jnp.concatenate([own_ref[:, :3].astype(F32), other_ref[:, :3].astype(F32)], axis=2).astype(BF16)
    both = both.reshape(PAIRS, 16, 128)
    for group in range(4):
        data = jnp.concatenate([both[group * 12 + i] for i in range(12)], axis=1)
        modes = dot(table, jnp.concatenate([data, data], axis=0))
        for i in range(12):
            cols = slice(i * 128, i * 128 + 128)
            part = modes[:32, cols] + turn(modes[32:, cols], 1.0)
            scratch[pl.ds(group * 12 + i, 32, stride=rows), :] = part
    if point:
        (pairs,) = point
        total = own_ref[:8, 3].astype(F32).reshape(64, 128) + other_ref[:8, 3].astype(F32).reshape(64, 128)
        pairs[...] = split_pair(total + swap(total))
        for i in range(2):
            scratch[pl.ds(PAIRS + i, 32, stride=rows), :] = pairs[pl.ds(i, 32, stride=2), :]
        for i in range(2, 8):
            scratch[pl.ds(PAIRS + i, 32, stride=rows), :] = jnp.zeros((32, 128), F32)
    o_ref[...] = scratch[...].reshape(32, rows, 128).astype(BF16)


def mix_kernel(recv_ref, w_ref, o_ref, spec_ref):
    spec = jnp.sum(recv_ref[...].astype(F32), axis=0)
    spec_ref[...] = spec
    low = lanes(spec.shape) < 64
    other = swap(spec)
    real = jnp.where(low, spec, other)
    imag = jnp.where(low, other, spec)
    cols = []
    for kp in range(8):
        own = own_pair(kp, PAIRS)
        cols.append(
            jnp.concatenate([jnp.where(own, real, 0.0), jnp.where(own, imag, 0.0)], axis=0).astype(BF16)
        )
    prod = dot(jnp.concatenate(cols, axis=1), w_ref[...].reshape(1024, 128))
    mixed = (prod[:PAIRS] + turn(prod[PAIRS:], -1.0)).astype(BF16)
    o_ref[...] = jnp.broadcast_to(mixed[None], (32, PAIRS, 128))


def adjoint_kernel(recv_ref, w_ref, o_ref, dmix_ref):
    total = jnp.sum(recv_ref[...].astype(F32), axis=0)
    dmix = total[:PAIRS]
    dmix_ref[...] = dmix
    both = jnp.concatenate([dmix, turn(dmix, 1.0)], axis=0).astype(BF16)
    prod = dot(both, w_ref[...].reshape(1024, 128), NT)
    real = jnp.zeros((PAIRS, 128), F32)
    imag = jnp.zeros((PAIRS, 128), F32)
    for kp in range(8):
        own = own_pair(kp, PAIRS)
        cols = slice(kp * 128, kp * 128 + 128)
        real = real + jnp.where(own, prod[:PAIRS, cols], 0.0)
        imag = imag + jnp.where(own, prod[PAIRS:, cols], 0.0)
    real = real + swap(real)
    imag = imag + swap(imag)
    dspec = jnp.where(lanes(real.shape) < 64, real, imag) * SCALE
    point = total[PAIRS:]
    point = split_pair(point + swap(point))
    message = jnp.concatenate([dspec, point], axis=0).astype(BF16)
    o_ref[...] = jnp.broadcast_to(message[None], (32, ROWS, 128))


def gather_kernel(recv_ref, *rest, rows):
    if rows == ROWS:
        spec_ref, dmix_ref, own_ref, send_ref, fact_ref, scratch, fact = rest
    else:
        own_ref, send_ref, scratch = rest
    table = inverse_table()
    scratch[...] = recv_ref[...].astype(F32).reshape(32 * rows, 128)
    for group in range(4):
        cols = []
        for i in range(12):
            modes = scratch[pl.ds(group * 12 + i, 32, stride=rows), :]
            pair = jnp.concatenate([modes, turn(modes, -1.0)], axis=0)
            cols.append(jnp.concatenate([pair, pair], axis=0).astype(BF16))
        back = dot(table, jnp.concatenate(cols, axis=1))
        for i in range(12):
            m, b = divmod(group * 12 + i, 3)
            part = back[:, i * 128 : i * 128 + 128].astype(BF16)
            own_ref[m, b] = part[:8]
            send_ref[m, b] = part[8:]
    if rows == ROWS:
        fact[:PAIRS] = spec_ref[...]
        fact[PAIRS : 2 * PAIRS] = dmix_ref[...]
        for i in range(2):
            fact[pl.ds(2 * PAIRS + i, 32, stride=2), :] = scratch[pl.ds(PAIRS + i, 32, stride=rows), :]
        whole_fact = fact[...].astype(BF16)
        fact_ref[...] = jnp.broadcast_to(whole_fact[None], (4, 160, 128))


def field_kernel(
    in_ref, cot_ref, got_ref, other_ref, tab_ref, w_ref, dpre_ref, own_ref, send_ref, rows, scratch, dpre, sems
):
    load_rows(got_ref, other_ref, rows)
    mix_t = w_ref[...].astype(F32).T.astype(BF16)
    point = jnp.zeros((64, 64), F32)
    copies = []
    for g in range(GROUPS):
        fields = [3 * g + i for i in range(3)]
        left = left_of([(mode_block(rows, f) * INV_SCALE).astype(BF16) for f in fields], mix_t)
        for chunk in range(4):
            ts = slice(chunk * 256, chunk * 256 + 256)
            right = jnp.concatenate([tab_ref[:, ts]] + [in_ref[f, :, ts] for f in fields], axis=0)
            pre = dot(left, right)
            for i, f in enumerate(fields):
                slope = gelu_slope(pre[i * 64 : i * 64 + 64], cot_ref[f, :, ts].astype(F32))
                dpre[f, :, ts] = slope.astype(BF16)
        part = pl.ds(3 * g, 3)
        copies.append(pltpu.make_async_copy(dpre.at[part], dpre_ref.at[part], sems.at[g]))
        copies[g].start()
        left = jnp.concatenate([tab_ref[...]] + [in_ref[f] for f in fields], axis=0)
        r = dot(left, dpre[3 * g : 3 * g + 3].reshape(192, DURATION), NT)
        for i, f in enumerate(fields):
            cols = slice(i * 64, i * 64 + 64)
            point = point + r[64 + i * 64 : 128 + i * 64, cols]
            drows = jnp.concatenate([r[:32, cols], r[32:64, cols]], axis=1)
            scratch[field_rows(f), :] = drows * INV_SCALE
    store_rows(scratch, own_ref, send_ref)
    pair = split_pair(jnp.concatenate([point, point], axis=1))
    pair = jnp.concatenate([pair, jnp.zeros_like(pair)], axis=0).reshape(16, 8, 128).astype(BF16)
    own_ref[:, 3] = pair
    send_ref[:, 3] = pair
    for copy in copies:
        copy.wait()


def grad_kernel(
    dpre_ref, got_ref, other_ref, tab_ref, w_ref, o_ref, rows, dpre, grad, in_sems, out_sems
):
    ins, outs = [], []
    for g in range(GROUPS):
        part = pl.ds(3 * g, 3)
        ins.append(pltpu.make_async_copy(dpre_ref.at[part], dpre.at[part], in_sems.at[g]))
        outs.append(pltpu.make_async_copy(grad.at[part], o_ref.at[part], out_sems.at[g]))
        ins[g].start()
    load_rows(got_ref, other_ref, rows)
    mixing = w_ref[...]
    for g in range(GROUPS):
        fields = [3 * g + i for i in range(3)]
        left = left_of([mode_block(rows, f).astype(BF16) for f in fields], mixing)
        ins[g].wait()
        for chunk in range(4):
            ts = slice(chunk * 256, chunk * 256 + 256)
            right = jnp.concatenate([tab_ref[:, ts]] + [dpre[f, :, ts] for f in fields], axis=0)
            total = dot(left, right).astype(BF16)
            for i, f in enumerate(fields):
                grad[f, :, ts] = total[i * 64 : i * 64 + 64]
        outs[g].start()
    for copy in outs:
        copy.wait()


def weight_grad_kernel(fact_ref, spec_ref, point_ref):
    fact = fact_ref[...].astype(F32)
    place = lanes((1, 256)) & 127
    place = place - 24 * ((place * 171) >> 12)
    mode = (place * 43) >> 7
    empty = jnp.zeros((32, 128), F32)
    for half in range(2):
        rows = slice(half * 24, half * 24 + 24)
        s = jnp.concatenate([fact[:, rows].reshape(96, 128), empty], axis=0).T
        d = jnp.concatenate([fact[:, 48:96][:, rows].reshape(96, 128), empty], axis=0)
        left = jnp.concatenate([s[:64], s[64:]], axis=1)
        right = jnp.concatenate([d, turn(d, 1.0)], axis=0).astype(BF16)
        parts = [jnp.where(mode == m, left, 0.0).astype(BF16) for m in range(8)]
        g = dot(jnp.concatenate(parts, axis=0), right) * (1.0 / math.sqrt(BATCH * DEPTH))
        g = g.reshape(8, 64, 128)
        modes = slice(half * 8, half * 8 + 8)
        spec_ref[modes, 0] = g[:, :, :64]
        spec_ref[modes, 1] = g[:, :, 64:]
    point = fact[0, 96:] + fact[1, 96:] + fact[2, 96:] + fact[3, 96:]
    point = (point + swap(point)) * (1.0 / math.sqrt(BATCH * DEPTH * DURATION))
    point_ref[...] = point[:, :64]


FAST = pl.BlockSpec(memory_space=pltpu.VMEM)
SLOW = pl.BlockSpec(memory_space=pl.ANY)


def call(kernel, out_shape, in_specs, out_specs, scratch=(), limit=8):
    return pl.pallas_call(
        kernel,
        out_shape=out_shape,
        in_specs=in_specs,
        out_specs=out_specs,
        scratch_shapes=list(scratch),
        compiler_params=pltpu.CompilerParams(vmem_limit_bytes=limit * MIB),
    )


def shape(*dims, dtype=BF16):
    return jax.ShapeDtypeStruct(dims, dtype)


def exchange(v, axes):
    return lax.all_to_all(v, axes, 0, 0, tiled=True)


def to_other_core(v):
    return lax.ppermute(v, "core", [(0, 1), (1, 0)])


def spread(own, other, rows):
    scratch = [pltpu.VMEM((32 * rows, 128), F32)]
    if rows == ROWS:
        scratch.append(pltpu.VMEM((64, 128), F32))
    kernel = functools.partial(spread_kernel, rows=rows)
    return call(kernel, shape(32, rows, 128), [FAST] * 2, FAST, scratch)(own, other)


def local(inputs, cotangent, spec_weight, point_weight):
    tab = jnp.asarray(time_rows())
    fields = inputs.reshape(FIELDS, CHANNELS, DURATION)
    cots = cotangent.reshape(FIELDS, CHANNELS, DURATION)
    part = shape(16, 3, 8, 128)
    part4 = shape(16, 4, 8, 128)
    rows = pltpu.VMEM((FIELDS * 32, 128), F32)
    whole_field = pltpu.VMEM((FIELDS, CHANNELS, DURATION), BF16)
    sems = pltpu.SemaphoreType.DMA((GROUPS,))

    own, send, table, mixing, fields = call(
        coeff_kernel,
        (
            pltpu.VMEM((16, 3, 8, 128), BF16),
            pltpu.VMEM((16, 3, 8, 128), BF16),
            pltpu.VMEM((64, DURATION), BF16),
            pltpu.VMEM((CHANNELS, CHANNELS), BF16),
            pltpu.VMEM((FIELDS, CHANNELS, DURATION), BF16),
        ),
        [SLOW] * 3,
        (FAST,) * 5,
        [rows, pltpu.SemaphoreType.DMA((5,))],
        limit=56,
    )(*(pltpu.with_memory_space_constraint(v, pltpu.HBM) for v in (fields, tab, point_weight)))
    weights = call(
        weight_kernel,
        shape(16, 64, 128),
        [SLOW],
        FAST,
        [pltpu.VMEM((16, 2, CHANNELS, CHANNELS), F32), pltpu.SemaphoreType.DMA],
    )(pltpu.with_memory_space_constraint(spec_weight, pltpu.HBM))
    other, weights = lax.optimization_barrier((to_other_core(send), weights))
    got = exchange(spread(own, other, PAIRS), CHIP)
    mixed, spectrum = call(
        mix_kernel,
        (shape(32, PAIRS, 128), shape(PAIRS, 128, dtype=F32)),
        [FAST] * 2,
        (FAST,) * 2,
    )(got, weights)
    got = exchange(mixed, CHIP)
    own, send = call(
        functools.partial(gather_kernel, rows=PAIRS),
        (part, part),
        [FAST],
        (FAST, FAST),
        [pltpu.VMEM((32 * PAIRS, 128), F32)],
    )(got)
    dpre, own, send = call(
        field_kernel,
        (pltpu.HBM((FIELDS, CHANNELS, DURATION), BF16), part4, part4),
        [FAST] * 6,
        (SLOW, FAST, FAST),
        [rows, rows, whole_field, sems],
        limit=16,
    )(pltpu.with_memory_space_constraint(fields, pltpu.VMEM), cots, own, to_other_core(send), table, mixing)
    got = exchange(spread(own, to_other_core(send), ROWS), CHIP)
    dmodes, dmixed = call(
        adjoint_kernel,
        (shape(32, ROWS, 128), shape(PAIRS, 128, dtype=F32)),
        [FAST] * 2,
        (FAST, FAST),
    )(got, weights)
    got = exchange(dmodes, CHIP)
    own, send, factors = call(
        functools.partial(gather_kernel, rows=ROWS),
        (part, part, shape(4, 160, 128)),
        [FAST] * 3,
        (FAST,) * 3,
        [pltpu.VMEM((32 * ROWS, 128), F32), pltpu.VMEM((160, 128), F32)],
    )(got, spectrum, dmixed)
    factors = exchange(factors, "dp")
    input_grad = call(
        grad_kernel,
        pltpu.HBM((FIELDS, CHANNELS, DURATION), BF16),
        [SLOW] + [FAST] * 4,
        SLOW,
        [rows, whole_field, whole_field, sems, sems],
        limit=16,
    )(pltpu.with_memory_space_constraint(dpre, pltpu.HBM), own, to_other_core(send), table, mixing)
    spec_grad, point_grad = call(
        weight_grad_kernel,
        (shape(16, 2, 64, 64, dtype=F32), shape(64, 64, dtype=F32)),
        [FAST],
        (FAST, FAST),
    )(factors)
    return (input_grad.reshape(inputs.shape), spec_grad, point_grad)


def solution(mesh):
    fine = Mesh(mesh.devices.reshape(4, 2, 4, 4, 2), ("dp",) + FIELD)
    fields = P("dp", FIELD, None, None)
    weights = P(FIELD, None, None, None)
    return jax.shard_map(
        local,
        mesh=fine,
        in_specs=(fields, fields, weights, P()),
        out_specs=(fields, weights, P()),
        check_vma=False,
    )
```

time: 108 us -> 96.7 us (0.90)
  blocking collectives: 42.4 us -> 61.1 us
  local copies, waits for them, and re-layouts: 12.6 us -> 0.01 us
  waiting for transfers between devices: 17.2 us -> 7.55 us
  starting transfers between devices: 16.4 us -> 7.98 us
  Pallas kernels: 17.9 us -> 19 us
    all_to_all x3 -> x4, blocking collectives: 42.4 us -> 61.1 us  [exchange(): return lax.all_to_all(v, axes, 0, 0, tiled=True)]
    unnamed x34 -> x2, local copies, waits for them, and re-layouts: 12.6 us -> 0.01 us
    all_to_all x2 -> x1, starting transfers between devices: 16.2 us -> 7.57 us  [exchange(): return lax.all_to_all(v, axes, 0, 0, tiled=True)]
    all_to_all x2 -> x1, waiting for transfers between devices: 11.7 us -> 3.77 us  [exchange(): return lax.all_to_all(v, axes, 0, 0, tiled=True)]
    ppermute x4, waiting for transfers between devices: 5.5 us -> 3.78 us  [to_other_core(): return lax.ppermute(v, 'core', [(0, 1), (1, 0)])]
    pallas_call x9, Pallas kernels: 16 us -> 17.2 us  [the longest x1 5.44 us: local(): call(field_kernel, (pltpu.HBM((FIELDS, CHANNELS, DURATION), BF16), part4,...]
  transfers between devices with their start and end apart: 6 -> 5, of which waited for: 6 -> 4; matrix products, arithmetic and copies ran while one was open for 0% -> 0% of each run, Pallas kernels for 3% -> 6%
where the time goes in v4:
time: 96.7 us; the launch traced here: 96.4 us
  blocking collectives  61.1 us (63%)
  Pallas kernels  19 us (20%)
  starting transfers between devices  7.98 us (8%)
  waiting for transfers between devices  7.55 us (8%)
    all_to_all x4, blocking collectives, exchange(): return lax.all_to_all(v, axes, 0, 0, tiled=True)  61.1 us
    all_to_all x1, starting transfers between devices, exchange(): return lax.all_to_all(v, axes, 0, 0, tiled=True)  7.57 us
    pallas_call x1, Pallas kernels, local(): call(field_kernel, (pltpu.HBM((FIELDS, CHANNELS, DURATION), BF16), part4,...  5.44 us
    pallas_call x1, Pallas kernels, local(): call(grad_kernel, pltpu.HBM((FIELDS, CHANNELS, DURATION), BF16), [SLOW] +...  4.07 us
    ppermute x4, waiting for transfers between devices, to_other_core(): return lax.ppermute(v, 'core', [(0, 1), (1, 0)])  3.78 us
    all_to_all x1, waiting for transfers between devices, exchange(): return lax.all_to_all(v, axes, 0, 0, tiled=True)  3.77 us
    pallas_call x1, Pallas kernels, local(): call(coeff_kernel, (pltpu.VMEM((16, 3, 8, 128), BF16), pltpu.VMEM((16, 3,...  3.11 us
  transfers between devices with their start and end apart: 5, of which 4 were waited for; matrix products, arithmetic and copies ran while one was open for 0% of the time, Pallas kernels for 6%

profile of v4, /device:TPU:32, one launch (start us, length us, event | category | flops | bytes accessed | tf_op | source)
XLA Modules:
  0.0 96.4 jit_solution(2844119177977850953)
XLA Ops:
  0.6 3.1 %shard_map.76 = (bf16[16,3,8,128]{3,2,1,0:T(8,128)(2,1)S(1)}, bf16[16,3,8,128]{3,2,1,0:T(8,128)(2,1)S(1)}, bf16[64,1024]{1,0:T(8,128)(2,1)S(1)}, bf16[64,64]{1,0:T(8,128)(2,1)S(1)}, bf16[24,64,1024]{2,1,0:T(8,128)(2,1)S(1)}) custom-call(bf16[24,64,1024]{2,1,0:T(8,128)(2,1)} %bitcast.4, bf16[64,1024]{1,0:T(8,128)(2,1)} %constant.2.clone.tab_ref, ...), custom_call_target="tpu_custom_call" | custom-call | tf_op jit(solution)/shard_map/pallas_call | solution.py:388
  3.8 0.1 collective-permute-start
  3.9 1.4 %shard_map.77.w_ref = bf16[16,64,128]{2,1,0:T(8,128)(2,1)S(1)} custom-call(f32[16,2,64,64]{3,2,1,0:T(8,128)} %w_ref.1), custom_call_target="tpu_custom_call" | custom-call | tf_op jit(solution)/shard_map/pallas_call | solution.py:402
  5.2 0.0 collective-permute-done.other_ref
  5.3 0.7 shard_map.78
  5.9 18.3 %all_to_all.25.recv_ref = bf16[32,48,128]{2,1,0:T(8,128)(2,1)S(1)} all-to-all(bf16[32,48,128]{2,1,0:T(8,128)(2,1)S(1)} %shard_map.78), channel_id=1, replica_groups=mesh['dp'=4,'z'=2,'y'=4,'x'=4,'core'=2] {'z','y','x'}, dimensions={0} | all-to-all | bytes 786432 | tf_op jit(solution)/shard_map/all_to_all | solution.py:363
  24.2 0.4 shard_map.79
  24.6 13.7 %all_to_all.26.recv_ref = bf16[32,48,128]{2,1,0:T(8,128)(2,1)S(1)} all-to-all(bf16[32,48,128]{2,1,0:T(8,128)(2,1)S(1)} %get-tuple-element.29), channel_id=1, replica_groups=mesh['dp'=4,'z'=2,'y'=4,'x'=4,'core'=2] {'z','y','x'}, dimensions={0} | all-to-all | bytes 786432 | tf_op jit(solution)/shard_map/all_to_all | solution.py:363
  38.4 0.5 shard_map.80
  38.9 0.1 collective-permute-start.1
  39.0 1.3 %collective-permute-done.1.other_ref = bf16[16,3,8,128]{3,2,1,0:T(8,128)(2,1)S(1)} collective-permute-done((bf16[16,3,8,128]{3,2,1,0:T(8,128)(2,1)S(1)}, bf16[16,3,8,128]{3,2,1,0:T(8,128)(2,1)S(1)}, u32[]{:S(2)}, u32[]{:S(2)}) %collective-permute-start.1) | collective-permute-done | bytes 98336 | tf_op jit(solution)/shard_map/ppermute | solution.py:367
  40.3 5.4 %shard_map.81 = (bf16[24,64,1024]{2,1,0:T(8,128)(2,1)}, bf16[16,4,8,128]{3,2,1,0:T(8,128)(2,1)S(1)}, bf16[16,4,8,128]{3,2,1,0:T(8,128)(2,1)S(1)}) custom-call(bf16[24,64,1024]{2,1,0:T(8,128)(2,1)S(1)} %get-tuple-element.24.in_ref, bf16[24,64,1024]{2,1,0:T(8,128)(2,1)S(1)} %bitcast.3, bf16[16,3,8,128]{3,2,1,0:T(8,128)(2,1)S(1)} %get-tuple-element.30.got_ref, ...), custom_call_target="tpu_custom_call" | custom-call | tf_op jit(solution)/shard_map/pallas_call | solution.py:425
  45.7 0.2 collective-permute-start.2
  46.0 1.2 %collective-permute-done.2.other_ref = bf16[16,4,8,128]{3,2,1,0:T(8,128)(2,1)S(1)} collective-permute-done((bf16[16,4,8,128]{3,2,1,0:T(8,128)(2,1)S(1)}, bf16[16,4,8,128]{3,2,1,0:T(8,128)(2,1)S(1)}, u32[]{:S(2)}, u32[]{:S(2)}) %collective-permute-start.2) | collective-permute-done | bytes 131104 | tf_op jit(solution)/shard_map/ppermute | solution.py:367
  47.2 0.6 shard_map.82
  47.7 15.0 %all_to_all.27.recv_ref = bf16[32,56,128]{2,1,0:T(8,128)(2,1)S(1)} all-to-all(bf16[32,56,128]{2,1,0:T(8,128)(2,1)S(1)} %shard_map.82), channel_id=1, replica_groups=mesh['dp'=4,'z'=2,'y'=4,'x'=4,'core'=2] {'z','y','x'}, dimensions={0} | all-to-all | bytes 917504 | tf_op jit(solution)/shard_map/all_to_all | solution.py:363
  62.7 0.4 shard_map.83
  63.1 14.0 %all_to_all.28.recv_ref = bf16[32,56,128]{2,1,0:T(8,128)(2,1)S(1)} all-to-all(bf16[32,56,128]{2,1,0:T(8,128)(2,1)S(1)} %get-tuple-element.37), channel_id=1, replica_groups=mesh['dp'=4,'z'=2,'y'=4,'x'=4,'core'=2] {'z','y','x'}, dimensions={0} | all-to-all | bytes 917504 | tf_op jit(solution)/shard_map/all_to_all | solution.py:363
  77.2 1.0 %shard_map.84 = (bf16[16,3,8,128]{3,2,1,0:T(8,128)(2,1)S(1)}, bf16[16,3,8,128]{3,2,1,0:T(8,128)(2,1)S(1)}, bf16[4,160,128]{2,1,0:T(8,128)(2,1)}) custom-call(bf16[32,56,128]{2,1,0:T(8,128)(2,1)S(1)} %all_to_all.28.recv_ref, f32[48,128]{1,0:T(8,128)S(1)} %get-tuple-element.38.rest_0_, f32[48,128]{1,0:T(8,128)S(1)} %get-tuple-element.39.rest_1_), custom_call_target="tpu_custom_call" | custom-call | tf_op jit(solution)/shard_map/pallas_call | solution.py:441
  78.2 7.6 %all-to-all-start.4 = ((bf16[4,160,128]{2,1,0:T(8,128)(2,1)}), bf16[4,160,128]{2,1,0:T(8,128)(2,1)S(1)}, u32[]{:S(2)}, u32[]{:S(2)}) async-start(bf16[4,160,128]{2,1,0:T(8,128)(2,1)} %get-tuple-element.42), calls=%async_computation.4 | async-start | bytes 327680 | tf_op jit(solution)/shard_map/all_to_all | solution.py:363
  85.8 1.3 %collective-permute-done.3.other_ref = bf16[16,3,8,128]{3,2,1,0:T(8,128)(2,1)S(1)} collective-permute-done((bf16[16,3,8,128]{3,2,1,0:T(8,128)(2,1)S(1)}, bf16[16,3,8,128]{3,2,1,0:T(8,128)(2,1)S(1)}, u32[]{:S(2)}, u32[]{:S(2)}) %collective-permute-start.3) | collective-permute-done | bytes 98336 | tf_op jit(solution)/shard_map/ppermute | solution.py:367
  87.1 4.1 %shard_map.85 = bf16[24,64,1024]{2,1,0:T(8,128)(2,1)} custom-call(bf16[24,64,1024]{2,1,0:T(8,128)(2,1)} %get-tuple-element.34.dpre_ref, bf16[16,3,8,128]{3,2,1,0:T(8,128)(2,1)S(1)} %get-tuple-element.40.got_ref, bf16[16,3,8,128]{3,2,1,0:T(8,128)(2,1)S(1)} %collective-permute-done.3.other_ref, bf16[64,1024]{1,0:T(8,128)(2,1)S(1)} %get-tuple-element.32.tab_ref, ...), custom_call_target="tpu_custom_call" | custom-call | tf_op jit(solution)/shard_map/pallas_call | solution.py:449
  91.1 3.8 %all-to-all-done.4.fact_ref = bf16[4,160,128]{2,1,0:T(8,128)(2,1)S(1)} async-done(((bf16[4,160,128]{2,1,0:T(8,128)(2,1)}), bf16[4,160,128]{2,1,0:T(8,128)(2,1)S(1)}, u32[]{:S(2)}, u32[]{:S(2)}) %all-to-all-start.4) | async-done | bytes 163872 | tf_op jit(solution)/shard_map/all_to_all | solution.py:363
  94.9 1.5 %shard_map.86 = (f32[16,2,64,64]{3,2,1,0:T(8,128)}, f32[64,64]{1,0:T(8,128)}) custom-call(bf16[4,160,128]{2,1,0:T(8,128)(2,1)S(1)} %all-to-all-done.4.fact_ref), custom_call_target="tpu_custom_call" | custom-call | tf_op jit(solution)/shard_map/pallas_call | solution.py:457
  (3 shorter events, 0.0 us)
Async XLA Ops:
  0.6 39.6 %copy-start = (bf16[3,8,64,1024]{3,2,1,0:T(8,128)(2,1)S(1)}, bf16[3,8,64,1024]{3,2,1,0:T(8,128)(2,1)}, u32[]{:S(2)}) copy-start(bf16[3,8,64,1024]{3,2,1,0:T(8,128)(2,1)} %param.6) | copy-start | bytes 9437188
  3.8 1.5 %collective-permute-start = (bf16[16,3,8,128]{3,2,1,0:T(8,128)(2,1)S(1)}, bf16[16,3,8,128]{3,2,1,0:T(8,128)(2,1)S(1)}, u32[]{:S(2)}, u32[]{:S(2)}) collective-permute-start(bf16[16,3,8,128]{3,2,1,0:T(8,128)(2,1)S(1)} %get-tuple-element.26), channel_id=1, source_target_pairs={{0,1},{1,0},{2,3},{3,2},{4,5},{5,4},{6,7},{7,6},{8,9},{9,8},{10,11... | collective-permute-start | bytes 294920 | tf_op jit(solution)/shard_map/ppermute | solution.py:367
  38.9 1.4 %collective-permute-start.1 = (bf16[16,3,8,128]{3,2,1,0:T(8,128)(2,1)S(1)}, bf16[16,3,8,128]{3,2,1,0:T(8,128)(2,1)S(1)}, u32[]{:S(2)}, u32[]{:S(2)}) collective-permute-start(bf16[16,3,8,128]{3,2,1,0:T(8,128)(2,1)S(1)} %get-tuple-element.31), channel_id=1, source_target_pairs={{0,1},{1,0},{2,3},{3,2},{4,5},{5,4},{6,7},{7,6},{8,9},{9,8},{10,11... | collective-permute-start | bytes 294920 | tf_op jit(solution)/shard_map/ppermute | solution.py:367
  45.7 1.4 %collective-permute-start.2 = (bf16[16,4,8,128]{3,2,1,0:T(8,128)(2,1)S(1)}, bf16[16,4,8,128]{3,2,1,0:T(8,128)(2,1)S(1)}, u32[]{:S(2)}, u32[]{:S(2)}) collective-permute-start(bf16[16,4,8,128]{3,2,1,0:T(8,128)(2,1)S(1)} %get-tuple-element.36), channel_id=1, source_target_pairs={{0,1},{1,0},{2,3},{3,2},{4,5},{5,4},{6,7},{7,6},{8,9},{9,8},{10,11... | collective-permute-start | bytes 393224 | tf_op jit(solution)/shard_map/ppermute | solution.py:367
  78.2 16.7 %all-to-all-start.4 = ((bf16[4,160,128]{2,1,0:T(8,128)(2,1)}), bf16[4,160,128]{2,1,0:T(8,128)(2,1)S(1)}, u32[]{:S(2)}, u32[]{:S(2)}) async-start(bf16[4,160,128]{2,1,0:T(8,128)(2,1)} %get-tuple-element.42), calls=%async_computation.4 | async-start | bytes 327680 | tf_op jit(solution)/shard_map/all_to_all | solution.py:363
  85.8 1.3 %collective-permute-start.3 = (bf16[16,3,8,128]{3,2,1,0:T(8,128)(2,1)S(1)}, bf16[16,3,8,128]{3,2,1,0:T(8,128)(2,1)S(1)}, u32[]{:S(2)}, u32[]{:S(2)}) collective-permute-start(bf16[16,3,8,128]{3,2,1,0:T(8,128)(2,1)S(1)} %get-tuple-element.41), channel_id=1, source_target_pairs={{0,1},{1,0},{2,3},{3,2},{4,5},{5,4},{6,7},{7,6},{8,9},{9,8},{10,11... | collective-permute-start | bytes 294920 | tf_op jit(solution)/shard_map/ppermute | solution.py:367

commit v5 on v4

--- a/solution.py
+++ b/solution.py
@@ -158,11 +158,16 @@
     copies[1].wait()
 
 
-def weight_kernel(w_ref, o_ref, scratch, sem):
-    copy = pltpu.make_async_copy(w_ref, scratch, sem)
-    copy.start()
-    copy.wait()
-    o_ref[...] = jnp.concatenate([scratch[:, 0], scratch[:, 1]], axis=2).astype(BF16)
+def weight_kernel(w_ref, o_ref, scratch, sems):
+    copies = []
+    for part in range(4):
+        modes = pl.ds(4 * part, 4)
+        copies.append(pltpu.make_async_copy(w_ref.at[modes], scratch.at[modes], sems.at[part]))
+        copies[part].start()
+    for part in range(4):
+        copies[part].wait()
+        modes = slice(4 * part, 4 * part + 4)
+        o_ref[modes] = jnp.concatenate([scratch[modes, 0], scratch[modes, 1]], axis=2).astype(BF16)
 
 
 def spread_kernel(own_ref, other_ref, o_ref, scratch, *point, rows):
@@ -227,11 +232,16 @@
     o_ref[...] = jnp.broadcast_to(message[None], (32, ROWS, 128))
 
 
-def gather_kernel(recv_ref, *rest, rows):
-    if rows == ROWS:
-        spec_ref, dmix_ref, own_ref, send_ref, fact_ref, scratch, fact = rest
-    else:
-        own_ref, send_ref, scratch = rest
+def factor_kernel(recv_ref, spec_ref, dmix_ref, fact_ref, fact):
+    fact[:PAIRS] = spec_ref[...]
+    fact[PAIRS : 2 * PAIRS] = dmix_ref[...]
+    point = recv_ref[:, PAIRS:].astype(F32)
+    for k in range(32):
+        fact[2 * PAIRS + 2 * k : 2 * PAIRS + 2 * k + 2, :] = point[k, :2]
+    fact_ref[...] = jnp.broadcast_to(fact[...].astype(BF16)[None], (4, 160, 128))
+
+
+def gather_kernel(recv_ref, own_ref, send_ref, scratch, *, rows):
     table = inverse_table()
     scratch[...] = recv_ref[...].astype(F32).reshape(32 * rows, 128)
     for group in range(4):
@@ -246,13 +256,6 @@
             part = back[:, i * 128 : i * 128 + 128].astype(BF16)
             own_ref[m, b] = part[:8]
             send_ref[m, b] = part[8:]
-    if rows == ROWS:
-        fact[:PAIRS] = spec_ref[...]
-        fact[PAIRS : 2 * PAIRS] = dmix_ref[...]
-        for i in range(2):
-            fact[pl.ds(2 * PAIRS + i, 32, stride=2), :] = scratch[pl.ds(PAIRS + i, 32, stride=rows), :]
-        whole_fact = fact[...].astype(BF16)
-        fact_ref[...] = jnp.broadcast_to(whole_fact[None], (4, 160, 128))
 
 
 def field_kernel(
@@ -262,22 +265,34 @@
     mix_t = w_ref[...].astype(F32).T.astype(BF16)
     point = jnp.zeros((64, 64), F32)
     copies = []
-    for g in range(GROUPS):
-        fields = [3 * g + i for i in range(3)]
-        left = left_of([(mode_block(rows, f) * INV_SCALE).astype(BF16) for f in fields], mix_t)
+
+    def fields_of(g):
+        return [3 * g + i for i in range(3)]
+
+    def pre_of(g):
+        left = left_of([(mode_block(rows, f) * INV_SCALE).astype(BF16) for f in fields_of(g)], mix_t)
+        out = []
         for chunk in range(4):
             ts = slice(chunk * 256, chunk * 256 + 256)
-            right = jnp.concatenate([tab_ref[:, ts]] + [in_ref[f, :, ts] for f in fields], axis=0)
-            pre = dot(left, right)
-            for i, f in enumerate(fields):
-                slope = gelu_slope(pre[i * 64 : i * 64 + 64], cot_ref[f, :, ts].astype(F32))
+            right = jnp.concatenate([tab_ref[:, ts]] + [in_ref[f, :, ts] for f in fields_of(g)], axis=0)
+            out.append(dot(left, right))
+        return out
+
+    pre = pre_of(0)
+    for g in range(GROUPS):
+        following = pre_of(g + 1) if g + 1 < GROUPS else None
+        for chunk in range(4):
+            ts = slice(chunk * 256, chunk * 256 + 256)
+            for i, f in enumerate(fields_of(g)):
+                slope = gelu_slope(pre[chunk][i * 64 : i * 64 + 64], cot_ref[f, :, ts].astype(F32))
                 dpre[f, :, ts] = slope.astype(BF16)
+        pre = following
         part = pl.ds(3 * g, 3)
         copies.append(pltpu.make_async_copy(dpre.at[part], dpre_ref.at[part], sems.at[g]))
         copies[g].start()
-        left = jnp.concatenate([tab_ref[...]] + [in_ref[f] for f in fields], axis=0)
+        left = jnp.concatenate([tab_ref[...]] + [in_ref[f] for f in fields_of(g)], axis=0)
         r = dot(left, dpre[3 * g : 3 * g + 3].reshape(192, DURATION), NT)
-        for i, f in enumerate(fields):
+        for i, f in enumerate(fields_of(g)):
             cols = slice(i * 64, i * 64 + 64)
             point = point + r[64 + i * 64 : 128 + i * 64, cols]
             drows = jnp.concatenate([r[:32, cols], r[32:64, cols]], axis=1)
@@ -291,29 +306,29 @@
         copy.wait()
 
 
-def grad_kernel(
-    dpre_ref, got_ref, other_ref, tab_ref, w_ref, o_ref, rows, dpre, grad, in_sems, out_sems
-):
-    ins, outs = [], []
-    for g in range(GROUPS):
-        part = pl.ds(3 * g, 3)
-        ins.append(pltpu.make_async_copy(dpre_ref.at[part], dpre.at[part], in_sems.at[g]))
-        outs.append(pltpu.make_async_copy(grad.at[part], o_ref.at[part], out_sems.at[g]))
-        ins[g].start()
+def fetch_kernel(slow_ref, fast_ref, sem):
+    copy = pltpu.make_async_copy(slow_ref, fast_ref, sem)
+    copy.start()
+    copy.wait()
+
+
+def grad_kernel(dpre_ref, got_ref, other_ref, tab_ref, w_ref, o_ref, rows, grad, sems):
     load_rows(got_ref, other_ref, rows)
     mixing = w_ref[...]
+    copies = []
     for g in range(GROUPS):
         fields = [3 * g + i for i in range(3)]
         left = left_of([mode_block(rows, f).astype(BF16) for f in fields], mixing)
-        ins[g].wait()
         for chunk in range(4):
             ts = slice(chunk * 256, chunk * 256 + 256)
-            right = jnp.concatenate([tab_ref[:, ts]] + [dpre[f, :, ts] for f in fields], axis=0)
+            right = jnp.concatenate([tab_ref[:, ts]] + [dpre_ref[f, :, ts] for f in fields], axis=0)
             total = dot(left, right).astype(BF16)
             for i, f in enumerate(fields):
                 grad[f, :, ts] = total[i * 64 : i * 64 + 64]
-        outs[g].start()
-    for copy in outs:
+        part = pl.ds(3 * g, 3)
+        copies.append(pltpu.make_async_copy(grad.at[part], o_ref.at[part], sems.at[g]))
+        copies[g].start()
+    for copy in copies:
         copy.wait()
 
 
@@ -375,11 +390,20 @@
     return call(kernel, shape(32, rows, 128), [FAST] * 2, FAST, scratch)(own, other)
 
 
+def gather(got, rows):
+    return call(
+        functools.partial(gather_kernel, rows=rows),
+        (shape(16, 3, 8, 128),) * 2,
+        [FAST],
+        (FAST, FAST),
+        [pltpu.VMEM((32 * rows, 128), F32)],
+    )(got)
+
+
 def local(inputs, cotangent, spec_weight, point_weight):
     tab = jnp.asarray(time_rows())
     fields = inputs.reshape(FIELDS, CHANNELS, DURATION)
     cots = cotangent.reshape(FIELDS, CHANNELS, DURATION)
-    part = shape(16, 3, 8, 128)
     part4 = shape(16, 4, 8, 128)
     rows = pltpu.VMEM((FIELDS * 32, 128), F32)
     whole_field = pltpu.VMEM((FIELDS, CHANNELS, DURATION), BF16)
@@ -404,7 +428,7 @@
         shape(16, 64, 128),
         [SLOW],
         FAST,
-        [pltpu.VMEM((16, 2, CHANNELS, CHANNELS), F32), pltpu.SemaphoreType.DMA],
+        [pltpu.VMEM((16, 2, CHANNELS, CHANNELS), F32), pltpu.SemaphoreType.DMA((4,))],
     )(pltpu.with_memory_space_constraint(spec_weight, pltpu.HBM))
     other, weights = lax.optimization_barrier((to_other_core(send), weights))
     got = exchange(spread(own, other, PAIRS), CHIP)
@@ -415,13 +439,7 @@
         (FAST,) * 2,
     )(got, weights)
     got = exchange(mixed, CHIP)
-    own, send = call(
-        functools.partial(gather_kernel, rows=PAIRS),
-        (part, part),
-        [FAST],
-        (FAST, FAST),
-        [pltpu.VMEM((32 * PAIRS, 128), F32)],
-    )(got)
+    own, send = gather(got, PAIRS)
     dpre, own, send = call(
         field_kernel,
         (pltpu.HBM((FIELDS, CHANNELS, DURATION), BF16), part4, part4),
@@ -438,22 +456,32 @@
         (FAST, FAST),
     )(got, weights)
     got = exchange(dmodes, CHIP)
-    own, send, factors = call(
-        functools.partial(gather_kernel, rows=ROWS),
-        (part, part, shape(4, 160, 128)),
+    factors = call(
+        factor_kernel,
+        pltpu.HBM((4, 160, 128), BF16),
         [FAST] * 3,
-        (FAST,) * 3,
-        [pltpu.VMEM((32 * ROWS, 128), F32), pltpu.VMEM((160, 128), F32)],
+        FAST,
+        [pltpu.VMEM((160, 128), F32)],
     )(got, spectrum, dmixed)
     factors = exchange(factors, "dp")
+    own, send = gather(got, ROWS)
+    dpre = call(
+        fetch_kernel,
+        pltpu.VMEM((FIELDS, CHANNELS, DURATION), BF16),
+        [SLOW],
+        FAST,
+        [pltpu.SemaphoreType.DMA],
+        limit=1,
+    )(pltpu.with_memory_space_constraint(dpre, pltpu.HBM))
+    other, dpre = lax.optimization_barrier((to_other_core(send), dpre))
     input_grad = call(
         grad_kernel,
         pltpu.HBM((FIELDS, CHANNELS, DURATION), BF16),
-        [SLOW] + [FAST] * 4,
+        [FAST] * 5,
         SLOW,
-        [rows, whole_field, whole_field, sems, sems],
-        limit=16,
-    )(pltpu.with_memory_space_constraint(dpre, pltpu.HBM), own, to_other_core(send), table, mixing)
+        [rows, whole_field, sems],
+        limit=12,
+    )(pltpu.with_memory_space_constraint(dpre, pltpu.VMEM), own, other, table, mixing)
     spec_grad, point_grad = call(
         weight_grad_kernel,
         (shape(16, 2, 64, 64, dtype=F32), shape(64, 64, dtype=F32)),

time: 96.7 us -> 96 us (level)
    ppermute x4, waiting for transfers between devices: 3.78 us -> 2.48 us  [to_other_core(): return lax.ppermute(v, 'core', [(0, 1), (1, 0)])]
    pallas_call x3 -> x5, Pallas kernels: 5.61 us -> 5.69 us  [the longest x1 2.14 us: local(): call(grad_kernel, pltpu.HBM((FIELDS, CHANNELS, DURATION), BF16), [FAST] *...]
  transfers between devices with their start and end apart: 5 -> 5, of which waited for: 4 -> 3; matrix products, arithmetic and copies ran while one was open for 0% -> 0% of each run, Pallas kernels for 6% -> 6%
where the time goes in v5:
time: 96 us; the launch traced here: 95.7 us
  blocking collectives  61.1 us (64%)
  Pallas kernels  18.7 us (19%)
  starting transfers between devices  8.06 us (8%)
  waiting for transfers between devices  7.04 us (7%)
    all_to_all x4, blocking collectives, exchange(): return lax.all_to_all(v, axes, 0, 0, tiled=True)  61.1 us
    all_to_all x1, starting transfers between devices, exchange(): return lax.all_to_all(v, axes, 0, 0, tiled=True)  7.56 us
    pallas_call x1, Pallas kernels, local(): call(field_kernel, (pltpu.HBM((FIELDS, CHANNELS, DURATION), BF16), part4,...  5.11 us
    all_to_all x1, waiting for transfers between devices, exchange(): return lax.all_to_all(v, axes, 0, 0, tiled=True)  4.56 us
    pallas_call x1, Pallas kernels, local(): call(coeff_kernel, (pltpu.VMEM((16, 3, 8, 128), BF16), pltpu.VMEM((16, 3,...  3.11 us
    ppermute x4, waiting for transfers between devices, to_other_core(): return lax.ppermute(v, 'core', [(0, 1), (1, 0)])  2.48 us
    pallas_call x1, Pallas kernels, local(): call(grad_kernel, pltpu.HBM((FIELDS, CHANNELS, DURATION), BF16), [FAST] *...  2.14 us
  transfers between devices with their start and end apart: 5, of which 3 were waited for; matrix products, arithmetic and copies ran while one was open for 0% of the time, Pallas kernels for 6%

profile of v5, /device:TPU:32, one launch (start us, length us, event | category | flops | bytes accessed | tf_op | source)
XLA Modules:
  0.0 95.7 jit_solution(17630481885273085690)
XLA Ops:
  0.6 3.1 %shard_map.76 = (bf16[16,3,8,128]{3,2,1,0:T(8,128)(2,1)S(1)}, bf16[16,3,8,128]{3,2,1,0:T(8,128)(2,1)S(1)}, bf16[64,1024]{1,0:T(8,128)(2,1)S(1)}, bf16[64,64]{1,0:T(8,128)(2,1)S(1)}, bf16[24,64,1024]{2,1,0:T(8,128)(2,1)S(1)}) custom-call(bf16[24,64,1024]{2,1,0:T(8,128)(2,1)} %bitcast.4, bf16[64,1024]{1,0:T(8,128)(2,1)} %constant.2.clone.tab_ref, ...), custom_call_target="tpu_custom_call" | custom-call | tf_op jit(solution)/shard_map/pallas_call | solution.py:412
  3.8 0.1 collective-permute-start
  3.9 1.3 %shard_map.77.w_ref = bf16[16,64,128]{2,1,0:T(8,128)(2,1)S(1)} custom-call(f32[16,2,64,64]{3,2,1,0:T(8,128)} %w_ref.1), custom_call_target="tpu_custom_call" | custom-call | tf_op jit(solution)/shard_map/pallas_call | solution.py:426
  5.2 0.7 shard_map.78
  5.9 18.3 %all_to_all.25.recv_ref = bf16[32,48,128]{2,1,0:T(8,128)(2,1)S(1)} all-to-all(bf16[32,48,128]{2,1,0:T(8,128)(2,1)S(1)} %shard_map.78), channel_id=1, replica_groups=mesh['dp'=4,'z'=2,'y'=4,'x'=4,'core'=2] {'z','y','x'}, dimensions={0} | all-to-all | bytes 786432 | tf_op jit(solution)/shard_map/all_to_all | solution.py:378
  24.2 0.4 shard_map.79
  24.6 13.7 %all_to_all.26.recv_ref = bf16[32,48,128]{2,1,0:T(8,128)(2,1)S(1)} all-to-all(bf16[32,48,128]{2,1,0:T(8,128)(2,1)S(1)} %get-tuple-element.30), channel_id=1, replica_groups=mesh['dp'=4,'z'=2,'y'=4,'x'=4,'core'=2] {'z','y','x'}, dimensions={0} | all-to-all | bytes 786432 | tf_op jit(solution)/shard_map/all_to_all | solution.py:378
  38.3 0.5 shard_map.80
  38.9 1.3 %collective-permute-done.1.other_ref = bf16[16,3,8,128]{3,2,1,0:T(8,128)(2,1)S(1)} collective-permute-done((bf16[16,3,8,128]{3,2,1,0:T(8,128)(2,1)S(1)}, bf16[16,3,8,128]{3,2,1,0:T(8,128)(2,1)S(1)}, u32[]{:S(2)}, u32[]{:S(2)}) %collective-permute-start.1) | collective-permute-done | bytes 98336 | tf_op jit(solution)/shard_map/ppermute | solution.py:382
  40.2 5.1 %shard_map.81 = (bf16[24,64,1024]{2,1,0:T(8,128)(2,1)}, bf16[16,4,8,128]{3,2,1,0:T(8,128)(2,1)S(1)}, bf16[16,4,8,128]{3,2,1,0:T(8,128)(2,1)S(1)}) custom-call(bf16[24,64,1024]{2,1,0:T(8,128)(2,1)S(1)} %get-tuple-element.25.in_ref, bf16[24,64,1024]{2,1,0:T(8,128)(2,1)S(1)} %bitcast.3, bf16[16,3,8,128]{3,2,1,0:T(8,128)(2,1)S(1)} %get-tuple-element.31.got_ref, ...), custom_call_target="tpu_custom_call" | custom-call | tf_op jit(solution)/shard_map/pallas_call | solution.py:443
  45.3 0.2 collective-permute-start.2
  45.6 1.2 %collective-permute-done.2.other_ref = bf16[16,4,8,128]{3,2,1,0:T(8,128)(2,1)S(1)} collective-permute-done((bf16[16,4,8,128]{3,2,1,0:T(8,128)(2,1)S(1)}, bf16[16,4,8,128]{3,2,1,0:T(8,128)(2,1)S(1)}, u32[]{:S(2)}, u32[]{:S(2)}) %collective-permute-start.2) | collective-permute-done | bytes 131104 | tf_op jit(solution)/shard_map/ppermute | solution.py:382
  46.8 0.6 shard_map.82
  47.4 15.0 %all_to_all.27.recv_ref = bf16[32,56,128]{2,1,0:T(8,128)(2,1)S(1)} all-to-all(bf16[32,56,128]{2,1,0:T(8,128)(2,1)S(1)} %shard_map.82), channel_id=1, replica_groups=mesh['dp'=4,'z'=2,'y'=4,'x'=4,'core'=2] {'z','y','x'}, dimensions={0} | all-to-all | bytes 917504 | tf_op jit(solution)/shard_map/all_to_all | solution.py:378
  62.4 0.4 shard_map.83
  62.8 14.0 %all_to_all.28.recv_ref = bf16[32,56,128]{2,1,0:T(8,128)(2,1)S(1)} all-to-all(bf16[32,56,128]{2,1,0:T(8,128)(2,1)S(1)} %get-tuple-element.37), channel_id=1, replica_groups=mesh['dp'=4,'z'=2,'y'=4,'x'=4,'core'=2] {'z','y','x'}, dimensions={0} | all-to-all | bytes 917504 | tf_op jit(solution)/shard_map/all_to_all | solution.py:378
  76.8 0.7 shard_map.87
  77.5 7.6 %all-to-all-start.4 = ((bf16[4,160,128]{2,1,0:T(8,128)(2,1)}), bf16[4,160,128]{2,1,0:T(8,128)(2,1)S(1)}, u32[]{:S(2)}, u32[]{:S(2)}) async-start(bf16[4,160,128]{2,1,0:T(8,128)(2,1)} %shard_map.87), calls=%async_computation.4 | async-start | bytes 327680 | tf_op jit(solution)/shard_map/all_to_all | solution.py:378
  85.1 0.4 shard_map.84
  85.5 0.1 collective-permute-start.3
  85.6 1.9 %shard_map.85.dpre_ref = bf16[24,64,1024]{2,1,0:T(8,128)(2,1)S(1)} custom-call(bf16[24,64,1024]{2,1,0:T(8,128)(2,1)} %get-tuple-element.39.slow_ref), custom_call_target="tpu_custom_call" | custom-call | tf_op jit(solution)/shard_map/pallas_call | solution.py:468
  87.5 2.1 %shard_map.86 = bf16[24,64,1024]{2,1,0:T(8,128)(2,1)} custom-call(bf16[24,64,1024]{2,1,0:T(8,128)(2,1)S(1)} %shard_map.85.dpre_ref, bf16[16,3,8,128]{3,2,1,0:T(8,128)(2,1)S(1)} %get-tuple-element.41.got_ref, bf16[16,3,8,128]{3,2,1,0:T(8,128)(2,1)S(1)} %collective-permute-done.3.other_ref, bf16[64,1024]{1,0:T(8,128)(2,1)S(1)} %get-tuple-element.33.tab_ref, ...), custom_call_target="tpu_custom_call" | custom-call | tf_op jit(solution)/shard_map/pallas_call | solution.py:477
  89.6 4.6 %all-to-all-done.4.fact_ref = bf16[4,160,128]{2,1,0:T(8,128)(2,1)S(1)} async-done(((bf16[4,160,128]{2,1,0:T(8,128)(2,1)}), bf16[4,160,128]{2,1,0:T(8,128)(2,1)S(1)}, u32[]{:S(2)}, u32[]{:S(2)}) %all-to-all-start.4) | async-done | bytes 163872 | tf_op jit(solution)/shard_map/all_to_all | solution.py:378
  94.2 1.5 %shard_map.88 = (f32[16,2,64,64]{3,2,1,0:T(8,128)}, f32[64,64]{1,0:T(8,128)}) custom-call(bf16[4,160,128]{2,1,0:T(8,128)(2,1)S(1)} %all-to-all-done.4.fact_ref), custom_call_target="tpu_custom_call" | custom-call | tf_op jit(solution)/shard_map/pallas_call | solution.py:485
  (5 shorter events, 0.1 us)
Async XLA Ops:
  0.6 39.6 %copy-start = (bf16[3,8,64,1024]{3,2,1,0:T(8,128)(2,1)S(1)}, bf16[3,8,64,1024]{3,2,1,0:T(8,128)(2,1)}, u32[]{:S(2)}) copy-start(bf16[3,8,64,1024]{3,2,1,0:T(8,128)(2,1)} %param.6) | copy-start | bytes 9437188
  3.8 1.5 %collective-permute-start = (bf16[16,3,8,128]{3,2,1,0:T(8,128)(2,1)S(1)}, bf16[16,3,8,128]{3,2,1,0:T(8,128)(2,1)S(1)}, u32[]{:S(2)}, u32[]{:S(2)}) collective-permute-start(bf16[16,3,8,128]{3,2,1,0:T(8,128)(2,1)S(1)} %get-tuple-element.27), channel_id=1, source_target_pairs={{0,1},{1,0},{2,3},{3,2},{4,5},{5,4},{6,7},{7,6},{8,9},{9,8},{10,11... | collective-permute-start | bytes 294920 | tf_op jit(solution)/shard_map/ppermute | solution.py:382
  38.9 1.4 %collective-permute-start.1 = (bf16[16,3,8,128]{3,2,1,0:T(8,128)(2,1)S(1)}, bf16[16,3,8,128]{3,2,1,0:T(8,128)(2,1)S(1)}, u32[]{:S(2)}, u32[]{:S(2)}) collective-permute-start(bf16[16,3,8,128]{3,2,1,0:T(8,128)(2,1)S(1)} %get-tuple-element.32), channel_id=1, source_target_pairs={{0,1},{1,0},{2,3},{3,2},{4,5},{5,4},{6,7},{7,6},{8,9},{9,8},{10,11... | collective-permute-start | bytes 294920 | tf_op jit(solution)/shard_map/ppermute | solution.py:382
  45.3 1.4 %collective-permute-start.2 = (bf16[16,4,8,128]{3,2,1,0:T(8,128)(2,1)S(1)}, bf16[16,4,8,128]{3,2,1,0:T(8,128)(2,1)S(1)}, u32[]{:S(2)}, u32[]{:S(2)}) collective-permute-start(bf16[16,4,8,128]{3,2,1,0:T(8,128)(2,1)S(1)} %get-tuple-element.36), channel_id=1, source_target_pairs={{0,1},{1,0},{2,3},{3,2},{4,5},{5,4},{6,7},{7,6},{8,9},{9,8},{10,11... | collective-permute-start | bytes 393224 | tf_op jit(solution)/shard_map/ppermute | solution.py:382
  77.5 16.7 %all-to-all-start.4 = ((bf16[4,160,128]{2,1,0:T(8,128)(2,1)}), bf16[4,160,128]{2,1,0:T(8,128)(2,1)S(1)}, u32[]{:S(2)}, u32[]{:S(2)}) async-start(bf16[4,160,128]{2,1,0:T(8,128)(2,1)} %shard_map.87), calls=%async_computation.4 | async-start | bytes 327680 | tf_op jit(solution)/shard_map/all_to_all | solution.py:378
  85.5 2.0 %collective-permute-start.3 = (bf16[16,3,8,128]{3,2,1,0:T(8,128)(2,1)S(1)}, bf16[16,3,8,128]{3,2,1,0:T(8,128)(2,1)S(1)}, u32[]{:S(2)}, u32[]{:S(2)}) collective-permute-start(bf16[16,3,8,128]{3,2,1,0:T(8,128)(2,1)S(1)} %get-tuple-element.38), channel_id=1, source_target_pairs={{0,1},{1,0},{2,3},{3,2},{4,5},{5,4},{6,7},{7,6},{8,9},{9,8},{10,11... | collective-permute-start | bytes 294920 | tf_op jit(solution)/shard_map/ppermute | solution.py:382

commit v6 on v5

--- a/solution.py
+++ b/solution.py
@@ -29,6 +29,7 @@
 MIB = 1024 * 1024
 FIELDS = 24
 GROUPS = 8
+PARTS = ((0, 8), (8, 8), (16, 8))
 PAIRS = 48
 ROWS = 56
 
@@ -121,12 +122,12 @@
     return jnp.concatenate(rows, axis=0)
 
 
-def gelu_slope(pre, cot):
+def gelu_slope_twice(pre, cot):
     root = math.sqrt(2.0 / math.pi)
     p = (root * 0.044715) * (pre * pre) + root
     th = jnp.tanh(pre * p)
     q = 3.0 * p - 2.0 * root
-    return ((1.0 + th) * (1.0 + (pre * q) * (1.0 - th))) * (0.5 * cot)
+    return ((1.0 + th) * (1.0 + (pre * q) * (1.0 - th))) * cot
 
 
 def own_pair(kp, rows):
@@ -136,24 +137,26 @@
 
 
 def coeff_kernel(
-    in_ref, tab_ref, mix_ref, own_ref, send_ref, table, mixing, fields, scratch, sems
+    in_ref, tab_ref, mix_ref, own_ref, send_ref, table, mixing, fields, forward, inverse, scratch, sems
 ):
     copies = [
-        pltpu.make_async_copy(tab_ref, table, sems.at[3]),
-        pltpu.make_async_copy(mix_ref, mixing, sems.at[4]),
+        pltpu.make_async_copy(tab_ref, table, sems.at[len(PARTS)]),
+        pltpu.make_async_copy(mix_ref, mixing, sems.at[len(PARTS) + 1]),
     ]
-    for b in range(3):
-        part = pl.ds(8 * b, 8)
-        copies.append(pltpu.make_async_copy(in_ref.at[part], fields.at[part], sems.at[b]))
+    for p, (first, n) in enumerate(PARTS):
+        part = pl.ds(first, n)
+        copies.append(pltpu.make_async_copy(in_ref.at[part], fields.at[part], sems.at[p]))
     for copy in copies:
         copy.start()
+    forward[...] = forward_table()
+    inverse[...] = inverse_table()
     copies[0].wait()
-    for b in range(3):
-        copies[2 + b].wait()
-        coeffs = dot(table[...], fields[8 * b : 8 * b + 8].reshape(512, DURATION), NT) * SCALE
-        for i in range(8):
+    for p, (first, n) in enumerate(PARTS):
+        copies[2 + p].wait()
+        coeffs = dot(table[...], fields[first : first + n].reshape(n * 64, DURATION), NT) * SCALE
+        for i in range(n):
             cols = slice(i * 64, i * 64 + 64)
-            scratch[field_rows(8 * b + i), :] = jnp.concatenate([coeffs[:32, cols], coeffs[32:, cols]], axis=1)
+            scratch[field_rows(first + i), :] = jnp.concatenate([coeffs[:32, cols], coeffs[32:, cols]], axis=1)
     store_rows(scratch, own_ref, send_ref)
     copies[1].wait()
 
@@ -170,8 +173,8 @@
         o_ref[modes] = jnp.concatenate([scratch[modes, 0], scratch[modes, 1]], axis=2).astype(BF16)
 
 
-def spread_kernel(own_ref, other_ref, o_ref, scratch, *point, rows):
-    table = forward_table()
+def spread_kernel(own_ref, other_ref, tab_ref, o_ref, scratch, *point, rows):
+    table = tab_ref[...]
     both = jnp.concatenate([own_ref[:, :3].astype(F32), other_ref[:, :3].astype(F32)], axis=2).astype(BF16)
     both = both.reshape(PAIRS, 16, 128)
     for group in range(4):
@@ -241,8 +244,8 @@
     fact_ref[...] = jnp.broadcast_to(fact[...].astype(BF16)[None], (4, 160, 128))
 
 
-def gather_kernel(recv_ref, own_ref, send_ref, scratch, *, rows):
-    table = inverse_table()
+def gather_kernel(recv_ref, tab_ref, own_ref, send_ref, scratch, *, rows):
+    table = tab_ref[...]
     scratch[...] = recv_ref[...].astype(F32).reshape(32 * rows, 128)
     for group in range(4):
         cols = []
@@ -284,7 +287,7 @@
         for chunk in range(4):
             ts = slice(chunk * 256, chunk * 256 + 256)
             for i, f in enumerate(fields_of(g)):
-                slope = gelu_slope(pre[chunk][i * 64 : i * 64 + 64], cot_ref[f, :, ts].astype(F32))
+                slope = gelu_slope_twice(pre[chunk][i * 64 : i * 64 + 64], cot_ref[f, :, ts].astype(F32))
                 dpre[f, :, ts] = slope.astype(BF16)
         pre = following
         part = pl.ds(3 * g, 3)
@@ -296,8 +299,9 @@
             cols = slice(i * 64, i * 64 + 64)
             point = point + r[64 + i * 64 : 128 + i * 64, cols]
             drows = jnp.concatenate([r[:32, cols], r[32:64, cols]], axis=1)
-            scratch[field_rows(f), :] = drows * INV_SCALE
+            scratch[field_rows(f), :] = drows * (0.5 * INV_SCALE)
     store_rows(scratch, own_ref, send_ref)
+    point = 0.5 * point
     pair = split_pair(jnp.concatenate([point, point], axis=1))
     pair = jnp.concatenate([pair, jnp.zeros_like(pair)], axis=0).reshape(16, 8, 128).astype(BF16)
     own_ref[:, 3] = pair
@@ -314,7 +318,7 @@
 
 def grad_kernel(dpre_ref, got_ref, other_ref, tab_ref, w_ref, o_ref, rows, grad, sems):
     load_rows(got_ref, other_ref, rows)
-    mixing = w_ref[...]
+    mixing = (w_ref[...].astype(F32) * 0.5).astype(BF16)
     copies = []
     for g in range(GROUPS):
         fields = [3 * g + i for i in range(3)]
@@ -382,22 +386,22 @@
     return lax.ppermute(v, "core", [(0, 1), (1, 0)])
 
 
-def spread(own, other, rows):
+def spread(own, other, table, rows):
     scratch = [pltpu.VMEM((32 * rows, 128), F32)]
     if rows == ROWS:
         scratch.append(pltpu.VMEM((64, 128), F32))
     kernel = functools.partial(spread_kernel, rows=rows)
-    return call(kernel, shape(32, rows, 128), [FAST] * 2, FAST, scratch)(own, other)
-
-
-def gather(got, rows):
+    return call(kernel, shape(32, rows, 128), [FAST] * 3, FAST, scratch)(own, other, table)
+
+
+def gather(got, table, rows):
     return call(
         functools.partial(gather_kernel, rows=rows),
         (shape(16, 3, 8, 128),) * 2,
-        [FAST],
+        [FAST] * 2,
         (FAST, FAST),
         [pltpu.VMEM((32 * rows, 128), F32)],
-    )(got)
+    )(got, table)
 
 
 def local(inputs, cotangent, spec_weight, point_weight):
@@ -409,7 +413,7 @@
     whole_field = pltpu.VMEM((FIELDS, CHANNELS, DURATION), BF16)
     sems = pltpu.SemaphoreType.DMA((GROUPS,))
 
-    own, send, table, mixing, fields = call(
+    own, send, table, mixing, fields, forward, inverse = call(
         coeff_kernel,
         (
             pltpu.VMEM((16, 3, 8, 128), BF16),
@@ -417,10 +421,12 @@
             pltpu.VMEM((64, DURATION), BF16),
             pltpu.VMEM((CHANNELS, CHANNELS), BF16),
             pltpu.VMEM((FIELDS, CHANNELS, DURATION), BF16),
+            pltpu.VMEM((64, 32), BF16),
+            pltpu.VMEM((16, 128), BF16),
         ),
         [SLOW] * 3,
-        (FAST,) * 5,
-        [rows, pltpu.SemaphoreType.DMA((5,))],
+        (FAST,) * 7,
+        [rows, pltpu.SemaphoreType.DMA((len(PARTS) + 2,))],
         limit=56,
     )(*(pltpu.with_memory_space_constraint(v, pltpu.HBM) for v in (fields, tab, point_weight)))
     weights = call(
@@ -431,7 +437,7 @@
         [pltpu.VMEM((16, 2, CHANNELS, CHANNELS), F32), pltpu.SemaphoreType.DMA((4,))],
     )(pltpu.with_memory_space_constraint(spec_weight, pltpu.HBM))
     other, weights = lax.optimization_barrier((to_other_core(send), weights))
-    got = exchange(spread(own, other, PAIRS), CHIP)
+    got = exchange(spread(own, other, forward, PAIRS), CHIP)
     mixed, spectrum = call(
         mix_kernel,
         (shape(32, PAIRS, 128), shape(PAIRS, 128, dtype=F32)),
@@ -439,7 +445,7 @@
         (FAST,) * 2,
     )(got, weights)
     got = exchange(mixed, CHIP)
-    own, send = gather(got, PAIRS)
+    own, send = gather(got, inverse, PAIRS)
     dpre, own, send = call(
         field_kernel,
         (pltpu.HBM((FIELDS, CHANNELS, DURATION), BF16), part4, part4),
@@ -448,7 +454,7 @@
         [rows, rows, whole_field, sems],
         limit=16,
     )(pltpu.with_memory_space_constraint(fields, pltpu.VMEM), cots, own, to_other_core(send), table, mixing)
-    got = exchange(spread(own, to_other_core(send), ROWS), CHIP)
+    got = exchange(spread(own, to_other_core(send), forward, ROWS), CHIP)
     dmodes, dmixed = call(
         adjoint_kernel,
         (shape(32, ROWS, 128), shape(PAIRS, 128, dtype=F32)),
@@ -464,7 +470,7 @@
         [pltpu.VMEM((160, 128), F32)],
     )(got, spectrum, dmixed)
     factors = exchange(factors, "dp")
-    own, send = gather(got, ROWS)
+    own, send = gather(got, inverse, ROWS)
     dpre = call(
         fetch_kernel,
         pltpu.VMEM((FIELDS, CHANNELS, DURATION), BF16),

time: 96 us -> 95.7 us (level)
  no operation moved by 1% of the time
where the time goes in v6:
time: 95.7 us; the launch traced here: 95.3 us
  blocking collectives  61.1 us (64%)
  Pallas kernels  18.3 us (19%)
  starting transfers between devices  8.08 us (8%)
  waiting for transfers between devices  7.06 us (7%)
    all_to_all x4, blocking collectives, exchange(): return lax.all_to_all(v, axes, 0, 0, tiled=True)  61.1 us
    all_to_all x1, starting transfers between devices, exchange(): return lax.all_to_all(v, axes, 0, 0, tiled=True)  7.56 us
    pallas_call x1, Pallas kernels, local(): call(field_kernel, (pltpu.HBM((FIELDS, CHANNELS, DURATION), BF16), part4,...  5 us
    all_to_all x1, waiting for transfers between devices, exchange(): return lax.all_to_all(v, axes, 0, 0, tiled=True)  4.57 us
    pallas_call x1, Pallas kernels, local(): call(coeff_kernel, (pltpu.VMEM((16, 3, 8, 128), BF16), pltpu.VMEM((16, 3,...  3.11 us
    ppermute x4, waiting for transfers between devices, to_other_core(): return lax.ppermute(v, 'core', [(0, 1), (1, 0)])  2.48 us
    pallas_call x1, Pallas kernels, local(): call(grad_kernel, pltpu.HBM((FIELDS, CHANNELS, DURATION), BF16), [FAST] *...  2.14 us
  transfers between devices with their start and end apart: 5, of which 3 were waited for; matrix products, arithmetic and copies ran while one was open for 0% of the time, Pallas kernels for 6%

profile of v6, /device:TPU:32, one launch (start us, length us, event | category | flops | bytes accessed | tf_op | source)
XLA Modules:
  0.0 95.3 jit_solution(16036184827457901530)
XLA Ops:
  0.6 3.1 %shard_map.76 = (bf16[16,3,8,128]{3,2,1,0:T(8,128)(2,1)S(1)}, bf16[16,3,8,128]{3,2,1,0:T(8,128)(2,1)S(1)}, bf16[64,1024]{1,0:T(8,128)(2,1)S(1)}, bf16[64,64]{1,0...) custom-call(bf16[24,64,1024]{2,1,0:T(8,128)(2,1)} %bitcast.4, ...), custom_call_target="tpu_custom_call" | custom-call | tf_op jit(solution)/shard_map/pallas_call | solution.py:416
  3.9 1.3 %shard_map.77.w_ref = bf16[16,64,128]{2,1,0:T(8,128)(2,1)S(1)} custom-call(f32[16,2,64,64]{3,2,1,0:T(8,128)} %w_ref.1), custom_call_target="tpu_custom_call" | custom-call | tf_op jit(solution)/shard_map/pallas_call | solution.py:432
  5.2 0.5 shard_map.78
  5.8 18.3 %all_to_all.25.recv_ref = bf16[32,48,128]{2,1,0:T(8,128)(2,1)S(1)} all-to-all(bf16[32,48,128]{2,1,0:T(8,128)(2,1)S(1)} %shard_map.78), channel_id=1, replica_groups=mesh['dp'=4,'z'=2,'y'=4,'x'=4,'core'=2] {'z','y','x'}, dimensions={0} | all-to-all | bytes 786432 | tf_op jit(solution)/shard_map/all_to_all | solution.py:382
  24.1 0.4 shard_map.79
  24.5 13.7 %all_to_all.26.recv_ref = bf16[32,48,128]{2,1,0:T(8,128)(2,1)S(1)} all-to-all(bf16[32,48,128]{2,1,0:T(8,128)(2,1)S(1)} %get-tuple-element.33), channel_id=1, replica_groups=mesh['dp'=4,'z'=2,'y'=4,'x'=4,'core'=2] {'z','y','x'}, dimensions={0} | all-to-all | bytes 786432 | tf_op jit(solution)/shard_map/all_to_all | solution.py:382
  38.2 0.5 shard_map.80
  38.7 0.1 collective-permute-start.1
  38.8 1.3 %collective-permute-done.1.other_ref = bf16[16,3,8,128]{3,2,1,0:T(8,128)(2,1)S(1)} collective-permute-done((bf16[16,3,8,128]{3,2,1,0:T(8,128)(2,1)S(1)}, bf16[16,3,8,128]{3,2,1,0:T(8,128)(2,1)S(1)}, u32[]{:S(2)}, u32[]{:S(2)}) %collective-permute-start.1) | collective-permute-done | bytes 98336 | tf_op jit(solution)/shard_map/ppermute | solution.py:386
  40.1 5.0 %shard_map.81 = (bf16[24,64,1024]{2,1,0:T(8,128)(2,1)}, bf16[16,4,8,128]{3,2,1,0:T(8,128)(2,1)S(1)}, bf16[16,4,8,128]{3,2,1,0:T(8,128)(2,1)S(1)}) custom-call(bf16[24,64,1024]{2,1,0:T(8,128)(2,1)S(1)} %get-tuple-element.27.in_ref, bf16[24,64,1024]{2,1,0:T(8,128)(2,1)S(1)} %bitcast.3, bf16[16,3,8,128]{3,2,1,0:T(8,128)(2,1)S(1)} %get-tuple-element.35.got_ref, ...), custom_call_target="tpu_custom_call" | custom-call | tf_op jit(solution)/shard_map/pallas_call | solution.py:449
  45.1 0.2 collective-permute-start.2
  45.3 1.2 %collective-permute-done.2.other_ref = bf16[16,4,8,128]{3,2,1,0:T(8,128)(2,1)S(1)} collective-permute-done((bf16[16,4,8,128]{3,2,1,0:T(8,128)(2,1)S(1)}, bf16[16,4,8,128]{3,2,1,0:T(8,128)(2,1)S(1)}, u32[]{:S(2)}, u32[]{:S(2)}) %collective-permute-start.2) | collective-permute-done | bytes 131104 | tf_op jit(solution)/shard_map/ppermute | solution.py:386
  46.5 0.5 shard_map.82
  47.0 15.0 %all_to_all.27.recv_ref = bf16[32,56,128]{2,1,0:T(8,128)(2,1)S(1)} all-to-all(bf16[32,56,128]{2,1,0:T(8,128)(2,1)S(1)} %shard_map.82), channel_id=1, replica_groups=mesh['dp'=4,'z'=2,'y'=4,'x'=4,'core'=2] {'z','y','x'}, dimensions={0} | all-to-all | bytes 917504 | tf_op jit(solution)/shard_map/all_to_all | solution.py:382
  62.0 0.4 shard_map.83
  62.4 14.0 %all_to_all.28.recv_ref = bf16[32,56,128]{2,1,0:T(8,128)(2,1)S(1)} all-to-all(bf16[32,56,128]{2,1,0:T(8,128)(2,1)S(1)} %get-tuple-element.41), channel_id=1, replica_groups=mesh['dp'=4,'z'=2,'y'=4,'x'=4,'core'=2] {'z','y','x'}, dimensions={0} | all-to-all | bytes 917504 | tf_op jit(solution)/shard_map/all_to_all | solution.py:382
  76.4 0.7 shard_map.87
  77.1 7.6 %all-to-all-start.4 = ((bf16[4,160,128]{2,1,0:T(8,128)(2,1)}), bf16[4,160,128]{2,1,0:T(8,128)(2,1)S(1)}, u32[]{:S(2)}, u32[]{:S(2)}) async-start(bf16[4,160,128]{2,1,0:T(8,128)(2,1)} %shard_map.87), calls=%async_computation.4 | async-start | bytes 327680 | tf_op jit(solution)/shard_map/all_to_all | solution.py:382
  84.7 0.4 shard_map.84
  85.1 0.1 collective-permute-start.3
  85.2 1.9 %shard_map.85.dpre_ref = bf16[24,64,1024]{2,1,0:T(8,128)(2,1)S(1)} custom-call(bf16[24,64,1024]{2,1,0:T(8,128)(2,1)} %get-tuple-element.43.slow_ref), custom_call_target="tpu_custom_call" | custom-call | tf_op jit(solution)/shard_map/pallas_call | solution.py:474
  87.1 2.1 %shard_map.86 = bf16[24,64,1024]{2,1,0:T(8,128)(2,1)} custom-call(bf16[24,64,1024]{2,1,0:T(8,128)(2,1)S(1)} %shard_map.85.dpre_ref, bf16[16,3,8,128]{3,2,1,0:T(8,128)(2,1)S(1)} %get-tuple-element.45.got_ref, bf16[16,3,8,128]{3,2,1,0:T(8,128)(2,1)S(1)} %collective-permute-done.3.other_ref, bf16[64,1024]{1,0:T(8,128)(2,1)S(1)} %get-tuple-element.37.tab_ref, ...), custom_call_target="tpu_custom_call" | custom-call | tf_op jit(solution)/shard_map/pallas_call | solution.py:483
  89.2 4.6 %all-to-all-done.4.fact_ref = bf16[4,160,128]{2,1,0:T(8,128)(2,1)S(1)} async-done(((bf16[4,160,128]{2,1,0:T(8,128)(2,1)}), bf16[4,160,128]{2,1,0:T(8,128)(2,1)S(1)}, u32[]{:S(2)}, u32[]{:S(2)}) %all-to-all-start.4) | async-done | bytes 163872 | tf_op jit(solution)/shard_map/all_to_all | solution.py:382
  93.8 1.5 %shard_map.88 = (f32[16,2,64,64]{3,2,1,0:T(8,128)}, f32[64,64]{1,0:T(8,128)}) custom-call(bf16[4,160,128]{2,1,0:T(8,128)(2,1)S(1)} %all-to-all-done.4.fact_ref), custom_call_target="tpu_custom_call" | custom-call | tf_op jit(solution)/shard_map/pallas_call | solution.py:491
  (5 shorter events, 0.1 us)
Async XLA Ops:
  0.6 39.4 %copy-start = (bf16[3,8,64,1024]{3,2,1,0:T(8,128)(2,1)S(1)}, bf16[3,8,64,1024]{3,2,1,0:T(8,128)(2,1)}, u32[]{:S(2)}) copy-start(bf16[3,8,64,1024]{3,2,1,0:T(8,128)(2,1)} %param.6) | copy-start | bytes 9437188
  3.8 1.5 %collective-permute-start = (bf16[16,3,8,128]{3,2,1,0:T(8,128)(2,1)S(1)}, bf16[16,3,8,128]{3,2,1,0:T(8,128)(2,1)S(1)}, u32[]{:S(2)}, u32[]{:S(2)}) collective-permute-start(bf16[16,3,8,128]{3,2,1,0:T(8,128)(2,1)S(1)} %get-tuple-element.29), channel_id=1, source_target_pairs={{0,1},{1,0},{2,3},{3,2},{4,5},{5,4},{6,7},{7,6},{8,9},{9,8},{10,11... | collective-permute-start | bytes 294920 | tf_op jit(solution)/shard_map/ppermute | solution.py:386
  38.7 1.4 %collective-permute-start.1 = (bf16[16,3,8,128]{3,2,1,0:T(8,128)(2,1)S(1)}, bf16[16,3,8,128]{3,2,1,0:T(8,128)(2,1)S(1)}, u32[]{:S(2)}, u32[]{:S(2)}) collective-permute-start(bf16[16,3,8,128]{3,2,1,0:T(8,128)(2,1)S(1)} %get-tuple-element.36), channel_id=1, source_target_pairs={{0,1},{1,0},{2,3},{3,2},{4,5},{5,4},{6,7},{7,6},{8,9},{9,8},{10,11... | collective-permute-start | bytes 294920 | tf_op jit(solution)/shard_map/ppermute | solution.py:386
  45.1 1.4 %collective-permute-start.2 = (bf16[16,4,8,128]{3,2,1,0:T(8,128)(2,1)S(1)}, bf16[16,4,8,128]{3,2,1,0:T(8,128)(2,1)S(1)}, u32[]{:S(2)}, u32[]{:S(2)}) collective-permute-start(bf16[16,4,8,128]{3,2,1,0:T(8,128)(2,1)S(1)} %get-tuple-element.40), channel_id=1, source_target_pairs={{0,1},{1,0},{2,3},{3,2},{4,5},{5,4},{6,7},{7,6},{8,9},{9,8},{10,11... | collective-permute-start | bytes 393224 | tf_op jit(solution)/shard_map/ppermute | solution.py:386
  77.1 16.7 %all-to-all-start.4 = ((bf16[4,160,128]{2,1,0:T(8,128)(2,1)}), bf16[4,160,128]{2,1,0:T(8,128)(2,1)S(1)}, u32[]{:S(2)}, u32[]{:S(2)}) async-start(bf16[4,160,128]{2,1,0:T(8,128)(2,1)} %shard_map.87), calls=%async_computation.4 | async-start | bytes 327680 | tf_op jit(solution)/shard_map/all_to_all | solution.py:382
  85.1 2.0 %collective-permute-start.3 = (bf16[16,3,8,128]{3,2,1,0:T(8,128)(2,1)S(1)}, bf16[16,3,8,128]{3,2,1,0:T(8,128)(2,1)S(1)}, u32[]{:S(2)}, u32[]{:S(2)}) collective-permute-start(bf16[16,3,8,128]{3,2,1,0:T(8,128)(2,1)S(1)} %get-tuple-element.42), channel_id=1, source_target_pairs={{0,1},{1,0},{2,3},{3,2},{4,5},{5,4},{6,7},{7,6},{8,9},{9,8},{10,11... | collective-permute-start | bytes 294920 | tf_op jit(solution)/shard_map/ppermute | solution.py:386

commit v7 on v6

--- a/solution.py
+++ b/solution.py
@@ -29,7 +29,6 @@
 MIB = 1024 * 1024
 FIELDS = 24
 GROUPS = 8
-PARTS = ((0, 8), (8, 8), (16, 8))
 PAIRS = 48
 ROWS = 56
 
@@ -88,12 +87,11 @@
     return lax.dot_general(a, b, dims, preferred_element_type=F32)
 
 
-def store_rows(scratch, own_ref, send_ref):
+def store_rows(scratch, b, own_ref, send_ref):
     core = lax.axis_index("core")
-    for b in range(3):
-        for c, ref in ((core, own_ref), (1 - core, send_ref)):
-            rows = scratch[pl.ds(pl.multiple_of(b * 256 + c * 128, 128), 128), :]
-            ref[:, b] = rows.reshape(16, 8, 128).astype(BF16)
+    for c, ref in ((core, own_ref), (1 - core, send_ref)):
+        rows = scratch[pl.ds(pl.multiple_of(b * 256 + c * 128, 128), 128), :]
+        ref[:, b] = rows.reshape(16, 8, 128).astype(BF16)
 
 
 def load_rows(own_ref, other_ref, scratch):
@@ -140,24 +138,24 @@
     in_ref, tab_ref, mix_ref, own_ref, send_ref, table, mixing, fields, forward, inverse, scratch, sems
 ):
     copies = [
-        pltpu.make_async_copy(tab_ref, table, sems.at[len(PARTS)]),
-        pltpu.make_async_copy(mix_ref, mixing, sems.at[len(PARTS) + 1]),
+        pltpu.make_async_copy(tab_ref, table, sems.at[3]),
+        pltpu.make_async_copy(mix_ref, mixing, sems.at[4]),
     ]
-    for p, (first, n) in enumerate(PARTS):
-        part = pl.ds(first, n)
-        copies.append(pltpu.make_async_copy(in_ref.at[part], fields.at[part], sems.at[p]))
+    for b in range(3):
+        part = pl.ds(8 * b, 8)
+        copies.append(pltpu.make_async_copy(in_ref.at[part], fields.at[part], sems.at[b]))
     for copy in copies:
         copy.start()
     forward[...] = forward_table()
     inverse[...] = inverse_table()
     copies[0].wait()
-    for p, (first, n) in enumerate(PARTS):
-        copies[2 + p].wait()
-        coeffs = dot(table[...], fields[first : first + n].reshape(n * 64, DURATION), NT) * SCALE
-        for i in range(n):
+    for b in range(3):
+        copies[2 + b].wait()
+        coeffs = dot(table[...], fields[8 * b : 8 * b + 8].reshape(512, DURATION), NT) * SCALE
+        for i in range(8):
             cols = slice(i * 64, i * 64 + 64)
-            scratch[field_rows(first + i), :] = jnp.concatenate([coeffs[:32, cols], coeffs[32:, cols]], axis=1)
-    store_rows(scratch, own_ref, send_ref)
+            scratch[field_rows(8 * b + i), :] = jnp.concatenate([coeffs[:32, cols], coeffs[32:, cols]], axis=1)
+        store_rows(scratch, b, own_ref, send_ref)
     copies[1].wait()
 
 
@@ -187,12 +185,12 @@
     if point:
         (pairs,) = point
         total = own_ref[:8, 3].astype(F32).reshape(64, 128) + other_ref[:8, 3].astype(F32).reshape(64, 128)
-        pairs[...] = split_pair(total + swap(total))
+        pairs[:64] = split_pair(total + swap(total))
         for i in range(2):
             scratch[pl.ds(PAIRS + i, 32, stride=rows), :] = pairs[pl.ds(i, 32, stride=2), :]
         for i in range(2, 8):
             scratch[pl.ds(PAIRS + i, 32, stride=rows), :] = jnp.zeros((32, 128), F32)
-    o_ref[...] = scratch[...].reshape(32, rows, 128).astype(BF16)
+    o_ref[...] = scratch[: 32 * rows].reshape(32, rows, 128).astype(BF16)
 
 
 def mix_kernel(recv_ref, w_ref, o_ref, spec_ref):
@@ -246,7 +244,7 @@
 
 def gather_kernel(recv_ref, tab_ref, own_ref, send_ref, scratch, *, rows):
     table = tab_ref[...]
-    scratch[...] = recv_ref[...].astype(F32).reshape(32 * rows, 128)
+    scratch[: 32 * rows] = recv_ref[...].astype(F32).reshape(32 * rows, 128)
     for group in range(4):
         cols = []
         for i in range(12):
@@ -300,7 +298,8 @@
             point = point + r[64 + i * 64 : 128 + i * 64, cols]
             drows = jnp.concatenate([r[:32, cols], r[32:64, cols]], axis=1)
             scratch[field_rows(f), :] = drows * (0.5 * INV_SCALE)
-    store_rows(scratch, own_ref, send_ref)
+            if f % 8 == 7:
+                store_rows(scratch, f // 8, own_ref, send_ref)
     point = 0.5 * point
     pair = split_pair(jnp.concatenate([point, point], axis=1))
     pair = jnp.concatenate([pair, jnp.zeros_like(pair)], axis=0).reshape(16, 8, 128).astype(BF16)
@@ -346,10 +345,10 @@
         rows = slice(half * 24, half * 24 + 24)
         s = jnp.concatenate([fact[:, rows].reshape(96, 128), empty], axis=0).T
         d = jnp.concatenate([fact[:, 48:96][:, rows].reshape(96, 128), empty], axis=0)
-        left = jnp.concatenate([s[:64], s[64:]], axis=1)
+        left = jnp.concatenate([s[:64], s[64:]], axis=1) * (1.0 / math.sqrt(BATCH * DEPTH))
         right = jnp.concatenate([d, turn(d, 1.0)], axis=0).astype(BF16)
         parts = [jnp.where(mode == m, left, 0.0).astype(BF16) for m in range(8)]
-        g = dot(jnp.concatenate(parts, axis=0), right) * (1.0 / math.sqrt(BATCH * DEPTH))
+        g = dot(jnp.concatenate(parts, axis=0), right)
         g = g.reshape(8, 64, 128)
         modes = slice(half * 8, half * 8 + 8)
         spec_ref[modes, 0] = g[:, :, :64]
@@ -387,9 +386,9 @@
 
 
 def spread(own, other, table, rows):
-    scratch = [pltpu.VMEM((32 * rows, 128), F32)]
+    scratch = [pltpu.VMEM((33 * rows, 128), F32)]
     if rows == ROWS:
-        scratch.append(pltpu.VMEM((64, 128), F32))
+        scratch.append(pltpu.VMEM((72, 128), F32))
     kernel = functools.partial(spread_kernel, rows=rows)
     return call(kernel, shape(32, rows, 128), [FAST] * 3, FAST, scratch)(own, other, table)
 
@@ -400,7 +399,7 @@
         (shape(16, 3, 8, 128),) * 2,
         [FAST] * 2,
         (FAST, FAST),
-        [pltpu.VMEM((32 * rows, 128), F32)],
+        [pltpu.VMEM((33 * rows, 128), F32)],
     )(got, table)
 
 
@@ -409,7 +408,7 @@
     fields = inputs.reshape(FIELDS, CHANNELS, DURATION)
     cots = cotangent.reshape(FIELDS, CHANNELS, DURATION)
     part4 = shape(16, 4, 8, 128)
-    rows = pltpu.VMEM((FIELDS * 32, 128), F32)
+    rows = pltpu.VMEM((FIELDS * 32 + 8, 128), F32)
     whole_field = pltpu.VMEM((FIELDS, CHANNELS, DURATION), BF16)
     sems = pltpu.SemaphoreType.DMA((GROUPS,))
 
@@ -426,7 +425,7 @@
         ),
         [SLOW] * 3,
         (FAST,) * 7,
-        [rows, pltpu.SemaphoreType.DMA((len(PARTS) + 2,))],
+        [rows, pltpu.SemaphoreType.DMA((5,))],
         limit=56,
     )(*(pltpu.with_memory_space_constraint(v, pltpu.HBM) for v in (fields, tab, point_weight)))
     weights = call(

time: 95.7 us -> 95.6 us (level)
  no operation moved by 1% of the time
where the time goes in v7:
time: 95.6 us; the launch traced here: 95.2 us
  blocking collectives  61.1 us (64%)
  Pallas kernels  18.3 us (19%)
  starting transfers between devices  8.07 us (8%)
  waiting for transfers between devices  7.06 us (7%)
    all_to_all x4, blocking collectives, exchange(): return lax.all_to_all(v, axes, 0, 0, tiled=True)  61.1 us
    all_to_all x1, starting transfers between devices, exchange(): return lax.all_to_all(v, axes, 0, 0, tiled=True)  7.55 us
    pallas_call x1, Pallas kernels, local(): call(field_kernel, (pltpu.HBM((FIELDS, CHANNELS, DURATION), BF16), part4,...  4.94 us
    all_to_all x1, waiting for transfers between devices, exchange(): return lax.all_to_all(v, axes, 0, 0, tiled=True)  4.57 us
    pallas_call x1, Pallas kernels, local(): call(coeff_kernel, (pltpu.VMEM((16, 3, 8, 128), BF16), pltpu.VMEM((16, 3,...  3.14 us
    ppermute x4, waiting for transfers between devices, to_other_core(): return lax.ppermute(v, 'core', [(0, 1), (1, 0)])  2.49 us
    pallas_call x1, Pallas kernels, local(): call(grad_kernel, pltpu.HBM((FIELDS, CHANNELS, DURATION), BF16), [FAST] *...  2.14 us
  transfers between devices with their start and end apart: 5, of which 3 were waited for; matrix products, arithmetic and copies ran while one was open for 0% of the time, Pallas kernels for 6%

profile of v7, /device:TPU:32, one launch (start us, length us, event | category | flops | bytes accessed | tf_op | source)
XLA Modules:
  0.0 95.2 jit_solution(8081782945817042877)
XLA Ops:
  0.6 3.1 %shard_map.76 = (bf16[16,3,8,128]{3,2,1,0:T(8,128)(2,1)S(1)}, bf16[16,3,8,128]{3,2,1,0:T(8,128)(2,1)S(1)}, bf16[64,1024]{1,0:T(8,128)(2,1)S(1)}, bf16[64,64]{1,0...) custom-call(bf16[24,64,1024]{2,1,0:T(8,128)(2,1)} %bitcast.4, ...), custom_call_target="tpu_custom_call" | custom-call | tf_op jit(solution)/shard_map/pallas_call | solution.py:415
  3.8 0.1 collective-permute-start
  3.9 1.3 %shard_map.77.w_ref = bf16[16,64,128]{2,1,0:T(8,128)(2,1)S(1)} custom-call(f32[16,2,64,64]{3,2,1,0:T(8,128)} %w_ref.1), custom_call_target="tpu_custom_call" | custom-call | tf_op jit(solution)/shard_map/pallas_call | solution.py:431
  5.2 0.5 shard_map.78
  5.8 18.3 %all_to_all.25.recv_ref = bf16[32,48,128]{2,1,0:T(8,128)(2,1)S(1)} all-to-all(bf16[32,48,128]{2,1,0:T(8,128)(2,1)S(1)} %shard_map.78), channel_id=1, replica_groups=mesh['dp'=4,'z'=2,'y'=4,'x'=4,'core'=2] {'z','y','x'}, dimensions={0} | all-to-all | bytes 786432 | tf_op jit(solution)/shard_map/all_to_all | solution.py:381
  24.1 0.4 shard_map.79
  24.5 13.7 %all_to_all.26.recv_ref = bf16[32,48,128]{2,1,0:T(8,128)(2,1)S(1)} all-to-all(bf16[32,48,128]{2,1,0:T(8,128)(2,1)S(1)} %get-tuple-element.33), channel_id=1, replica_groups=mesh['dp'=4,'z'=2,'y'=4,'x'=4,'core'=2] {'z','y','x'}, dimensions={0} | all-to-all | bytes 786432 | tf_op jit(solution)/shard_map/all_to_all | solution.py:381
  38.3 0.5 shard_map.80
  38.7 0.1 collective-permute-start.1
  38.8 1.3 %collective-permute-done.1.other_ref = bf16[16,3,8,128]{3,2,1,0:T(8,128)(2,1)S(1)} collective-permute-done((bf16[16,3,8,128]{3,2,1,0:T(8,128)(2,1)S(1)}, bf16[16,3,8,128]{3,2,1,0:T(8,128)(2,1)S(1)}, u32[]{:S(2)}, u32[]{:S(2)}) %collective-permute-start.1) | collective-permute-done | bytes 98336 | tf_op jit(solution)/shard_map/ppermute | solution.py:385
  40.1 4.9 %shard_map.81 = (bf16[24,64,1024]{2,1,0:T(8,128)(2,1)}, bf16[16,4,8,128]{3,2,1,0:T(8,128)(2,1)S(1)}, bf16[16,4,8,128]{3,2,1,0:T(8,128)(2,1)S(1)}) custom-call(bf16[24,64,1024]{2,1,0:T(8,128)(2,1)S(1)} %get-tuple-element.27.in_ref, bf16[24,64,1024]{2,1,0:T(8,128)(2,1)S(1)} %bitcast.3, bf16[16,3,8,128]{3,2,1,0:T(8,128)(2,1)S(1)} %get-tuple-element.35.got_ref, ...), custom_call_target="tpu_custom_call" | custom-call | tf_op jit(solution)/shard_map/pallas_call | solution.py:448
  45.1 0.2 collective-permute-start.2
  45.3 1.2 %collective-permute-done.2.other_ref = bf16[16,4,8,128]{3,2,1,0:T(8,128)(2,1)S(1)} collective-permute-done((bf16[16,4,8,128]{3,2,1,0:T(8,128)(2,1)S(1)}, bf16[16,4,8,128]{3,2,1,0:T(8,128)(2,1)S(1)}, u32[]{:S(2)}, u32[]{:S(2)}) %collective-permute-start.2) | collective-permute-done | bytes 131104 | tf_op jit(solution)/shard_map/ppermute | solution.py:385
  46.5 0.5 shard_map.82
  47.0 15.0 %all_to_all.27.recv_ref = bf16[32,56,128]{2,1,0:T(8,128)(2,1)S(1)} all-to-all(bf16[32,56,128]{2,1,0:T(8,128)(2,1)S(1)} %shard_map.82), channel_id=1, replica_groups=mesh['dp'=4,'z'=2,'y'=4,'x'=4,'core'=2] {'z','y','x'}, dimensions={0} | all-to-all | bytes 917504 | tf_op jit(solution)/shard_map/all_to_all | solution.py:381
  62.0 0.4 shard_map.83
  62.4 14.0 %all_to_all.28.recv_ref = bf16[32,56,128]{2,1,0:T(8,128)(2,1)S(1)} all-to-all(bf16[32,56,128]{2,1,0:T(8,128)(2,1)S(1)} %get-tuple-element.41), channel_id=1, replica_groups=mesh['dp'=4,'z'=2,'y'=4,'x'=4,'core'=2] {'z','y','x'}, dimensions={0} | all-to-all | bytes 917504 | tf_op jit(solution)/shard_map/all_to_all | solution.py:381
  76.4 0.7 shard_map.87
  77.1 7.6 %all-to-all-start.4 = ((bf16[4,160,128]{2,1,0:T(8,128)(2,1)}), bf16[4,160,128]{2,1,0:T(8,128)(2,1)S(1)}, u32[]{:S(2)}, u32[]{:S(2)}) async-start(bf16[4,160,128]{2,1,0:T(8,128)(2,1)} %shard_map.87), calls=%async_computation.4 | async-start | bytes 327680 | tf_op jit(solution)/shard_map/all_to_all | solution.py:381
  84.6 0.4 shard_map.84
  85.2 1.9 %shard_map.85.dpre_ref = bf16[24,64,1024]{2,1,0:T(8,128)(2,1)S(1)} custom-call(bf16[24,64,1024]{2,1,0:T(8,128)(2,1)} %get-tuple-element.43.slow_ref), custom_call_target="tpu_custom_call" | custom-call | tf_op jit(solution)/shard_map/pallas_call | solution.py:473
  87.1 2.1 %shard_map.86 = bf16[24,64,1024]{2,1,0:T(8,128)(2,1)} custom-call(bf16[24,64,1024]{2,1,0:T(8,128)(2,1)S(1)} %shard_map.85.dpre_ref, bf16[16,3,8,128]{3,2,1,0:T(8,128)(2,1)S(1)} %get-tuple-element.45.got_ref, bf16[16,3,8,128]{3,2,1,0:T(8,128)(2,1)S(1)} %collective-permute-done.3.other_ref, bf16[64,1024]{1,0:T(8,128)(2,1)S(1)} %get-tuple-element.37.tab_ref, ...), custom_call_target="tpu_custom_call" | custom-call | tf_op jit(solution)/shard_map/pallas_call | solution.py:482
  89.2 4.6 %all-to-all-done.4.fact_ref = bf16[4,160,128]{2,1,0:T(8,128)(2,1)S(1)} async-done(((bf16[4,160,128]{2,1,0:T(8,128)(2,1)}), bf16[4,160,128]{2,1,0:T(8,128)(2,1)S(1)}, u32[]{:S(2)}, u32[]{:S(2)}) %all-to-all-start.4) | async-done | bytes 163872 | tf_op jit(solution)/shard_map/all_to_all | solution.py:381
  93.8 1.5 %shard_map.88 = (f32[16,2,64,64]{3,2,1,0:T(8,128)}, f32[64,64]{1,0:T(8,128)}) custom-call(bf16[4,160,128]{2,1,0:T(8,128)(2,1)S(1)} %all-to-all-done.4.fact_ref), custom_call_target="tpu_custom_call" | custom-call | tf_op jit(solution)/shard_map/pallas_call | solution.py:490
  (5 shorter events, 0.1 us)
Async XLA Ops:
  0.6 39.5 %copy-start = (bf16[3,8,64,1024]{3,2,1,0:T(8,128)(2,1)S(1)}, bf16[3,8,64,1024]{3,2,1,0:T(8,128)(2,1)}, u32[]{:S(2)}) copy-start(bf16[3,8,64,1024]{3,2,1,0:T(8,128)(2,1)} %param.6) | copy-start | bytes 9437188
  3.8 1.5 %collective-permute-start = (bf16[16,3,8,128]{3,2,1,0:T(8,128)(2,1)S(1)}, bf16[16,3,8,128]{3,2,1,0:T(8,128)(2,1)S(1)}, u32[]{:S(2)}, u32[]{:S(2)}) collective-permute-start(bf16[16,3,8,128]{3,2,1,0:T(8,128)(2,1)S(1)} %get-tuple-element.29), channel_id=1, source_target_pairs={{0,1},{1,0},{2,3},{3,2},{4,5},{5,4},{6,7},{7,6},{8,9},{9,8},{10,11... | collective-permute-start | bytes 294920 | tf_op jit(solution)/shard_map/ppermute | solution.py:385
  38.7 1.4 %collective-permute-start.1 = (bf16[16,3,8,128]{3,2,1,0:T(8,128)(2,1)S(1)}, bf16[16,3,8,128]{3,2,1,0:T(8,128)(2,1)S(1)}, u32[]{:S(2)}, u32[]{:S(2)}) collective-permute-start(bf16[16,3,8,128]{3,2,1,0:T(8,128)(2,1)S(1)} %get-tuple-element.36), channel_id=1, source_target_pairs={{0,1},{1,0},{2,3},{3,2},{4,5},{5,4},{6,7},{7,6},{8,9},{9,8},{10,11... | collective-permute-start | bytes 294920 | tf_op jit(solution)/shard_map/ppermute | solution.py:385
  45.1 1.4 %collective-permute-start.2 = (bf16[16,4,8,128]{3,2,1,0:T(8,128)(2,1)S(1)}, bf16[16,4,8,128]{3,2,1,0:T(8,128)(2,1)S(1)}, u32[]{:S(2)}, u32[]{:S(2)}) collective-permute-start(bf16[16,4,8,128]{3,2,1,0:T(8,128)(2,1)S(1)} %get-tuple-element.40), channel_id=1, source_target_pairs={{0,1},{1,0},{2,3},{3,2},{4,5},{5,4},{6,7},{7,6},{8,9},{9,8},{10,11... | collective-permute-start | bytes 393224 | tf_op jit(solution)/shard_map/ppermute | solution.py:385
  77.1 16.7 %all-to-all-start.4 = ((bf16[4,160,128]{2,1,0:T(8,128)(2,1)}), bf16[4,160,128]{2,1,0:T(8,128)(2,1)S(1)}, u32[]{:S(2)}, u32[]{:S(2)}) async-start(bf16[4,160,128]{2,1,0:T(8,128)(2,1)} %shard_map.87), calls=%async_computation.4 | async-start | bytes 327680 | tf_op jit(solution)/shard_map/all_to_all | solution.py:381
  85.1 2.0 %collective-permute-start.3 = (bf16[16,3,8,128]{3,2,1,0:T(8,128)(2,1)S(1)}, bf16[16,3,8,128]{3,2,1,0:T(8,128)(2,1)S(1)}, u32[]{:S(2)}, u32[]{:S(2)}) collective-permute-start(bf16[16,3,8,128]{3,2,1,0:T(8,128)(2,1)S(1)} %get-tuple-element.42), channel_id=1, source_target_pairs={{0,1},{1,0},{2,3},{3,2},{4,5},{5,4},{6,7},{7,6},{8,9},{9,8},{10,11... | collective-permute-start | bytes 294920 | tf_op jit(solution)/shard_map/ppermute | solution.py:385

commit v8 on v7

--- a/solution.py
+++ b/solution.py
@@ -345,10 +345,10 @@
         rows = slice(half * 24, half * 24 + 24)
         s = jnp.concatenate([fact[:, rows].reshape(96, 128), empty], axis=0).T
         d = jnp.concatenate([fact[:, 48:96][:, rows].reshape(96, 128), empty], axis=0)
-        left = jnp.concatenate([s[:64], s[64:]], axis=1) * (1.0 / math.sqrt(BATCH * DEPTH))
+        left = jnp.concatenate([s[:64], s[64:]], axis=1)
         right = jnp.concatenate([d, turn(d, 1.0)], axis=0).astype(BF16)
         parts = [jnp.where(mode == m, left, 0.0).astype(BF16) for m in range(8)]
-        g = dot(jnp.concatenate(parts, axis=0), right)
+        g = dot(jnp.concatenate(parts, axis=0), right) * (1.0 / math.sqrt(BATCH * DEPTH))
         g = g.reshape(8, 64, 128)
         modes = slice(half * 8, half * 8 + 8)
         spec_ref[modes, 0] = g[:, :, :64]

time: 95.6 us -> 95.6 us (level)
  no operation moved by 1% of the time
where the time goes in v8:
time: 95.6 us; the launch traced here: 95.2 us
  blocking collectives  61.1 us (64%)
  Pallas kernels  18.3 us (19%)
  starting transfers between devices  8.07 us (8%)
  waiting for transfers between devices  7.06 us (7%)
    all_to_all x4, blocking collectives, exchange(): return lax.all_to_all(v, axes, 0, 0, tiled=True)  61.1 us
    all_to_all x1, starting transfers between devices, exchange(): return lax.all_to_all(v, axes, 0, 0, tiled=True)  7.55 us
    pallas_call x1, Pallas kernels, local(): call(field_kernel, (pltpu.HBM((FIELDS, CHANNELS, DURATION), BF16), part4,...  4.94 us
    all_to_all x1, waiting for transfers between devices, exchange(): return lax.all_to_all(v, axes, 0, 0, tiled=True)  4.57 us
    pallas_call x1, Pallas kernels, local(): call(coeff_kernel, (pltpu.VMEM((16, 3, 8, 128), BF16), pltpu.VMEM((16, 3,...  3.14 us
    ppermute x4, waiting for transfers between devices, to_other_core(): return lax.ppermute(v, 'core', [(0, 1), (1, 0)])  2.49 us
    pallas_call x1, Pallas kernels, local(): call(grad_kernel, pltpu.HBM((FIELDS, CHANNELS, DURATION), BF16), [FAST] *...  2.14 us
  transfers between devices with their start and end apart: 5, of which 3 were waited for; matrix products, arithmetic and copies ran while one was open for 0% of the time, Pallas kernels for 6%

profile of v8, /device:TPU:32, one launch (start us, length us, event | category | flops | bytes accessed | tf_op | source)
XLA Modules:
  0.0 95.2 jit_solution(10026608911372970511)
XLA Ops:
  0.6 3.1 %shard_map.76 = (bf16[16,3,8,128]{3,2,1,0:T(8,128)(2,1)S(1)}, bf16[16,3,8,128]{3,2,1,0:T(8,128)(2,1)S(1)}, bf16[64,1024]{1,0:T(8,128)(2,1)S(1)}, bf16[64,64]{1,0...) custom-call(bf16[24,64,1024]{2,1,0:T(8,128)(2,1)} %bitcast.4, ...), custom_call_target="tpu_custom_call" | custom-call | tf_op jit(solution)/shard_map/pallas_call | solution.py:415
  3.8 0.1 collective-permute-start
  3.9 1.3 %shard_map.77.w_ref = bf16[16,64,128]{2,1,0:T(8,128)(2,1)S(1)} custom-call(f32[16,2,64,64]{3,2,1,0:T(8,128)} %w_ref.1), custom_call_target="tpu_custom_call" | custom-call | tf_op jit(solution)/shard_map/pallas_call | solution.py:431
  5.2 0.5 shard_map.78
  5.8 18.3 %all_to_all.25.recv_ref = bf16[32,48,128]{2,1,0:T(8,128)(2,1)S(1)} all-to-all(bf16[32,48,128]{2,1,0:T(8,128)(2,1)S(1)} %shard_map.78), channel_id=1, replica_groups=mesh['dp'=4,'z'=2,'y'=4,'x'=4,'core'=2] {'z','y','x'}, dimensions={0} | all-to-all | bytes 786432 | tf_op jit(solution)/shard_map/all_to_all | solution.py:381
  24.1 0.4 shard_map.79
  24.5 13.7 %all_to_all.26.recv_ref = bf16[32,48,128]{2,1,0:T(8,128)(2,1)S(1)} all-to-all(bf16[32,48,128]{2,1,0:T(8,128)(2,1)S(1)} %get-tuple-element.33), channel_id=1, replica_groups=mesh['dp'=4,'z'=2,'y'=4,'x'=4,'core'=2] {'z','y','x'}, dimensions={0} | all-to-all | bytes 786432 | tf_op jit(solution)/shard_map/all_to_all | solution.py:381
  38.3 0.5 shard_map.80
  38.8 1.3 %collective-permute-done.1.other_ref = bf16[16,3,8,128]{3,2,1,0:T(8,128)(2,1)S(1)} collective-permute-done((bf16[16,3,8,128]{3,2,1,0:T(8,128)(2,1)S(1)}, bf16[16,3,8,128]{3,2,1,0:T(8,128)(2,1)S(1)}, u32[]{:S(2)}, u32[]{:S(2)}) %collective-permute-start.1) | collective-permute-done | bytes 98336 | tf_op jit(solution)/shard_map/ppermute | solution.py:385
  40.1 4.9 %shard_map.81 = (bf16[24,64,1024]{2,1,0:T(8,128)(2,1)}, bf16[16,4,8,128]{3,2,1,0:T(8,128)(2,1)S(1)}, bf16[16,4,8,128]{3,2,1,0:T(8,128)(2,1)S(1)}) custom-call(bf16[24,64,1024]{2,1,0:T(8,128)(2,1)S(1)} %get-tuple-element.27.in_ref, bf16[24,64,1024]{2,1,0:T(8,128)(2,1)S(1)} %bitcast.3, bf16[16,3,8,128]{3,2,1,0:T(8,128)(2,1)S(1)} %get-tuple-element.35.got_ref, ...), custom_call_target="tpu_custom_call" | custom-call | tf_op jit(solution)/shard_map/pallas_call | solution.py:448
  45.1 0.2 collective-permute-start.2
  45.3 1.2 %collective-permute-done.2.other_ref = bf16[16,4,8,128]{3,2,1,0:T(8,128)(2,1)S(1)} collective-permute-done((bf16[16,4,8,128]{3,2,1,0:T(8,128)(2,1)S(1)}, bf16[16,4,8,128]{3,2,1,0:T(8,128)(2,1)S(1)}, u32[]{:S(2)}, u32[]{:S(2)}) %collective-permute-start.2) | collective-permute-done | bytes 131104 | tf_op jit(solution)/shard_map/ppermute | solution.py:385
  46.5 0.5 shard_map.82
  47.0 15.0 %all_to_all.27.recv_ref = bf16[32,56,128]{2,1,0:T(8,128)(2,1)S(1)} all-to-all(bf16[32,56,128]{2,1,0:T(8,128)(2,1)S(1)} %shard_map.82), channel_id=1, replica_groups=mesh['dp'=4,'z'=2,'y'=4,'x'=4,'core'=2] {'z','y','x'}, dimensions={0} | all-to-all | bytes 917504 | tf_op jit(solution)/shard_map/all_to_all | solution.py:381
  62.0 0.4 shard_map.83
  62.4 14.0 %all_to_all.28.recv_ref = bf16[32,56,128]{2,1,0:T(8,128)(2,1)S(1)} all-to-all(bf16[32,56,128]{2,1,0:T(8,128)(2,1)S(1)} %get-tuple-element.41), channel_id=1, replica_groups=mesh['dp'=4,'z'=2,'y'=4,'x'=4,'core'=2] {'z','y','x'}, dimensions={0} | all-to-all | bytes 917504 | tf_op jit(solution)/shard_map/all_to_all | solution.py:381
  76.4 0.7 shard_map.87
  77.1 7.6 %all-to-all-start.4 = ((bf16[4,160,128]{2,1,0:T(8,128)(2,1)}), bf16[4,160,128]{2,1,0:T(8,128)(2,1)S(1)}, u32[]{:S(2)}, u32[]{:S(2)}) async-start(bf16[4,160,128]{2,1,0:T(8,128)(2,1)} %shard_map.87), calls=%async_computation.4 | async-start | bytes 327680 | tf_op jit(solution)/shard_map/all_to_all | solution.py:381
  84.6 0.4 shard_map.84
  85.1 0.1 collective-permute-start.3
  85.2 1.9 %shard_map.85.dpre_ref = bf16[24,64,1024]{2,1,0:T(8,128)(2,1)S(1)} custom-call(bf16[24,64,1024]{2,1,0:T(8,128)(2,1)} %get-tuple-element.43.slow_ref), custom_call_target="tpu_custom_call" | custom-call | tf_op jit(solution)/shard_map/pallas_call | solution.py:473
  87.1 2.1 %shard_map.86 = bf16[24,64,1024]{2,1,0:T(8,128)(2,1)} custom-call(bf16[24,64,1024]{2,1,0:T(8,128)(2,1)S(1)} %shard_map.85.dpre_ref, bf16[16,3,8,128]{3,2,1,0:T(8,128)(2,1)S(1)} %get-tuple-element.45.got_ref, bf16[16,3,8,128]{3,2,1,0:T(8,128)(2,1)S(1)} %collective-permute-done.3.other_ref, bf16[64,1024]{1,0:T(8,128)(2,1)S(1)} %get-tuple-element.37.tab_ref, ...), custom_call_target="tpu_custom_call" | custom-call | tf_op jit(solution)/shard_map/pallas_call | solution.py:482
  89.2 4.6 %all-to-all-done.4.fact_ref = bf16[4,160,128]{2,1,0:T(8,128)(2,1)S(1)} async-done(((bf16[4,160,128]{2,1,0:T(8,128)(2,1)}), bf16[4,160,128]{2,1,0:T(8,128)(2,1)S(1)}, u32[]{:S(2)}, u32[]{:S(2)}) %all-to-all-start.4) | async-done | bytes 163872 | tf_op jit(solution)/shard_map/all_to_all | solution.py:381
  93.8 1.5 %shard_map.88 = (f32[16,2,64,64]{3,2,1,0:T(8,128)}, f32[64,64]{1,0:T(8,128)}) custom-call(bf16[4,160,128]{2,1,0:T(8,128)(2,1)S(1)} %all-to-all-done.4.fact_ref), custom_call_target="tpu_custom_call" | custom-call | tf_op jit(solution)/shard_map/pallas_call | solution.py:490
  (5 shorter events, 0.1 us)
Async XLA Ops:
  0.6 39.5 %copy-start = (bf16[3,8,64,1024]{3,2,1,0:T(8,128)(2,1)S(1)}, bf16[3,8,64,1024]{3,2,1,0:T(8,128)(2,1)}, u32[]{:S(2)}) copy-start(bf16[3,8,64,1024]{3,2,1,0:T(8,128)(2,1)} %param.6) | copy-start | bytes 9437188
  3.8 1.5 %collective-permute-start = (bf16[16,3,8,128]{3,2,1,0:T(8,128)(2,1)S(1)}, bf16[16,3,8,128]{3,2,1,0:T(8,128)(2,1)S(1)}, u32[]{:S(2)}, u32[]{:S(2)}) collective-permute-start(bf16[16,3,8,128]{3,2,1,0:T(8,128)(2,1)S(1)} %get-tuple-element.29), channel_id=1, source_target_pairs={{0,1},{1,0},{2,3},{3,2},{4,5},{5,4},{6,7},{7,6},{8,9},{9,8},{10,11... | collective-permute-start | bytes 294920 | tf_op jit(solution)/shard_map/ppermute | solution.py:385
  38.7 1.4 %collective-permute-start.1 = (bf16[16,3,8,128]{3,2,1,0:T(8,128)(2,1)S(1)}, bf16[16,3,8,128]{3,2,1,0:T(8,128)(2,1)S(1)}, u32[]{:S(2)}, u32[]{:S(2)}) collective-permute-start(bf16[16,3,8,128]{3,2,1,0:T(8,128)(2,1)S(1)} %get-tuple-element.36), channel_id=1, source_target_pairs={{0,1},{1,0},{2,3},{3,2},{4,5},{5,4},{6,7},{7,6},{8,9},{9,8},{10,11... | collective-permute-start | bytes 294920 | tf_op jit(solution)/shard_map/ppermute | solution.py:385
  45.1 1.4 %collective-permute-start.2 = (bf16[16,4,8,128]{3,2,1,0:T(8,128)(2,1)S(1)}, bf16[16,4,8,128]{3,2,1,0:T(8,128)(2,1)S(1)}, u32[]{:S(2)}, u32[]{:S(2)}) collective-permute-start(bf16[16,4,8,128]{3,2,1,0:T(8,128)(2,1)S(1)} %get-tuple-element.40), channel_id=1, source_target_pairs={{0,1},{1,0},{2,3},{3,2},{4,5},{5,4},{6,7},{7,6},{8,9},{9,8},{10,11... | collective-permute-start | bytes 393224 | tf_op jit(solution)/shard_map/ppermute | solution.py:385
  77.1 16.7 %all-to-all-start.4 = ((bf16[4,160,128]{2,1,0:T(8,128)(2,1)}), bf16[4,160,128]{2,1,0:T(8,128)(2,1)S(1)}, u32[]{:S(2)}, u32[]{:S(2)}) async-start(bf16[4,160,128]{2,1,0:T(8,128)(2,1)} %shard_map.87), calls=%async_computation.4 | async-start | bytes 327680 | tf_op jit(solution)/shard_map/all_to_all | solution.py:381
  85.1 2.0 %collective-permute-start.3 = (bf16[16,3,8,128]{3,2,1,0:T(8,128)(2,1)S(1)}, bf16[16,3,8,128]{3,2,1,0:T(8,128)(2,1)S(1)}, u32[]{:S(2)}, u32[]{:S(2)}) collective-permute-start(bf16[16,3,8,128]{3,2,1,0:T(8,128)(2,1)S(1)} %get-tuple-element.42), channel_id=1, source_target_pairs={{0,1},{1,0},{2,3},{3,2},{4,5},{5,4},{6,7},{7,6},{8,9},{9,8},{10,11... | collective-permute-start | bytes 294920 | tf_op jit(solution)/shard_map/ppermute | solution.py:385

commit v9 on v8

--- a/solution.py
+++ b/solution.py
@@ -233,13 +233,14 @@
     o_ref[...] = jnp.broadcast_to(message[None], (32, ROWS, 128))
 
 
-def factor_kernel(recv_ref, spec_ref, dmix_ref, fact_ref, fact):
+def factor_kernel(recv_ref, spec_ref, dmix_ref, fact_ref, fact, tiles):
     fact[:PAIRS] = spec_ref[...]
     fact[PAIRS : 2 * PAIRS] = dmix_ref[...]
-    point = recv_ref[:, PAIRS:].astype(F32)
-    for k in range(32):
-        fact[2 * PAIRS + 2 * k : 2 * PAIRS + 2 * k + 2, :] = point[k, :2]
-    fact_ref[...] = jnp.broadcast_to(fact[...].astype(BF16)[None], (4, 160, 128))
+    tiles[:256] = recv_ref[:, PAIRS:].astype(F32).reshape(256, 128)
+    first, second = (tiles[pl.ds(i, 32, stride=8), :] for i in range(2))
+    both = jnp.where(lanes((32, 128)) < 64, first + swap(first), second + swap(second))
+    fact[2 * PAIRS :] = both
+    fact_ref[...] = jnp.broadcast_to(fact[...].astype(BF16)[None], (4, 128, 128))
 
 
 def gather_kernel(recv_ref, tab_ref, own_ref, send_ref, scratch, *, rows):
@@ -335,7 +336,7 @@
         copy.wait()
 
 
-def weight_grad_kernel(fact_ref, spec_ref, point_ref):
+def weight_grad_kernel(fact_ref, spec_ref, point_ref, whole_point):
     fact = fact_ref[...].astype(F32)
     place = lanes((1, 256)) & 127
     place = place - 24 * ((place * 171) >> 12)
@@ -354,8 +355,10 @@
         spec_ref[modes, 0] = g[:, :, :64]
         spec_ref[modes, 1] = g[:, :, 64:]
     point = fact[0, 96:] + fact[1, 96:] + fact[2, 96:] + fact[3, 96:]
-    point = (point + swap(point)) * (1.0 / math.sqrt(BATCH * DEPTH * DURATION))
-    point_ref[...] = point[:, :64]
+    point = point * (1.0 / math.sqrt(BATCH * DEPTH * DURATION))
+    whole_point[pl.ds(0, 32, stride=2), :] = point
+    whole_point[pl.ds(1, 32, stride=2), :] = swap(point)
+    point_ref[...] = whole_point[:64, :64]
 
 
 FAST = pl.BlockSpec(memory_space=pltpu.VMEM)
@@ -463,10 +466,10 @@
     got = exchange(dmodes, CHIP)
     factors = call(
         factor_kernel,
-        pltpu.HBM((4, 160, 128), BF16),
+        pltpu.HBM((4, 128, 128), BF16),
         [FAST] * 3,
         FAST,
-        [pltpu.VMEM((160, 128), F32)],
+        [pltpu.VMEM((128, 128), F32), pltpu.VMEM((264, 128), F32)],
     )(got, spectrum, dmixed)
     factors = exchange(factors, "dp")
     own, send = gather(got, inverse, ROWS)
@@ -492,6 +495,7 @@
         (shape(16, 2, 64, 64, dtype=F32), shape(64, 64, dtype=F32)),
         [FAST],
         (FAST, FAST),
+        [pltpu.VMEM((72, 128), F32)],
     )(factors)
     return (input_grad.reshape(inputs.shape), spec_grad, point_grad)
 

time: 95.6 us -> 95.4 us (level)
  no operation moved by 1% of the time
where the time goes in v9:
time: 95.4 us; the launch traced here: 94.7 us
  blocking collectives  61.1 us (64%)
  Pallas kernels  18.3 us (19%)
  starting transfers between devices  8.07 us (8%)
  waiting for transfers between devices  6.43 us (7%)
    all_to_all x4, blocking collectives, exchange(): return lax.all_to_all(v, axes, 0, 0, tiled=True)  61.1 us
    all_to_all x1, starting transfers between devices, exchange(): return lax.all_to_all(v, axes, 0, 0, tiled=True)  7.55 us
    pallas_call x1, Pallas kernels, local(): call(field_kernel, (pltpu.HBM((FIELDS, CHANNELS, DURATION), BF16), part4,...  4.94 us
    all_to_all x1, waiting for transfers between devices, exchange(): return lax.all_to_all(v, axes, 0, 0, tiled=True)  3.94 us
    pallas_call x1, Pallas kernels, local(): call(coeff_kernel, (pltpu.VMEM((16, 3, 8, 128), BF16), pltpu.VMEM((16, 3,...  3.14 us
    ppermute x4, waiting for transfers between devices, to_other_core(): return lax.ppermute(v, 'core', [(0, 1), (1, 0)])  2.49 us
    pallas_call x1, Pallas kernels, local(): call(grad_kernel, pltpu.HBM((FIELDS, CHANNELS, DURATION), BF16), [FAST] *...  2.14 us
  transfers between devices with their start and end apart: 5, of which 3 were waited for; matrix products, arithmetic and copies ran while one was open for 0% of the time, Pallas kernels for 6%

profile of v9, /device:TPU:32, one launch (start us, length us, event | category | flops | bytes accessed | tf_op | source)
XLA Modules:
  0.0 94.7 jit_solution(15619502280751536210)
XLA Ops:
  0.6 3.1 %shard_map.76 = (bf16[16,3,8,128]{3,2,1,0:T(8,128)(2,1)S(1)}, bf16[16,3,8,128]{3,2,1,0:T(8,128)(2,1)S(1)}, bf16[64,1024]{1,0:T(8,128)(2,1)S(1)}, bf16[64,64]{1,0...) custom-call(bf16[24,64,1024]{2,1,0:T(8,128)(2,1)} %bitcast.4, ...), custom_call_target="tpu_custom_call" | custom-call | tf_op jit(solution)/shard_map/pallas_call | solution.py:418
  3.9 1.3 %shard_map.77.w_ref = bf16[16,64,128]{2,1,0:T(8,128)(2,1)S(1)} custom-call(f32[16,2,64,64]{3,2,1,0:T(8,128)} %w_ref.1), custom_call_target="tpu_custom_call" | custom-call | tf_op jit(solution)/shard_map/pallas_call | solution.py:434
  5.2 0.5 shard_map.78
  5.8 18.3 %all_to_all.25.recv_ref = bf16[32,48,128]{2,1,0:T(8,128)(2,1)S(1)} all-to-all(bf16[32,48,128]{2,1,0:T(8,128)(2,1)S(1)} %shard_map.78), channel_id=1, replica_groups=mesh['dp'=4,'z'=2,'y'=4,'x'=4,'core'=2] {'z','y','x'}, dimensions={0} | all-to-all | bytes 786432 | tf_op jit(solution)/shard_map/all_to_all | solution.py:384
  24.1 0.4 shard_map.79
  24.5 13.7 %all_to_all.26.recv_ref = bf16[32,48,128]{2,1,0:T(8,128)(2,1)S(1)} all-to-all(bf16[32,48,128]{2,1,0:T(8,128)(2,1)S(1)} %get-tuple-element.33), channel_id=1, replica_groups=mesh['dp'=4,'z'=2,'y'=4,'x'=4,'core'=2] {'z','y','x'}, dimensions={0} | all-to-all | bytes 786432 | tf_op jit(solution)/shard_map/all_to_all | solution.py:384
  38.3 0.5 shard_map.80
  38.7 0.1 collective-permute-start.1
  38.8 1.3 %collective-permute-done.1.other_ref = bf16[16,3,8,128]{3,2,1,0:T(8,128)(2,1)S(1)} collective-permute-done((bf16[16,3,8,128]{3,2,1,0:T(8,128)(2,1)S(1)}, bf16[16,3,8,128]{3,2,1,0:T(8,128)(2,1)S(1)}, u32[]{:S(2)}, u32[]{:S(2)}) %collective-permute-start.1) | collective-permute-done | bytes 98336 | tf_op jit(solution)/shard_map/ppermute | solution.py:388
  40.1 4.9 %shard_map.81 = (bf16[24,64,1024]{2,1,0:T(8,128)(2,1)}, bf16[16,4,8,128]{3,2,1,0:T(8,128)(2,1)S(1)}, bf16[16,4,8,128]{3,2,1,0:T(8,128)(2,1)S(1)}) custom-call(bf16[24,64,1024]{2,1,0:T(8,128)(2,1)S(1)} %get-tuple-element.27.in_ref, bf16[24,64,1024]{2,1,0:T(8,128)(2,1)S(1)} %bitcast.3, bf16[16,3,8,128]{3,2,1,0:T(8,128)(2,1)S(1)} %get-tuple-element.35.got_ref, ...), custom_call_target="tpu_custom_call" | custom-call | tf_op jit(solution)/shard_map/pallas_call | solution.py:451
  45.1 0.2 collective-permute-start.2
  45.3 1.2 %collective-permute-done.2.other_ref = bf16[16,4,8,128]{3,2,1,0:T(8,128)(2,1)S(1)} collective-permute-done((bf16[16,4,8,128]{3,2,1,0:T(8,128)(2,1)S(1)}, bf16[16,4,8,128]{3,2,1,0:T(8,128)(2,1)S(1)}, u32[]{:S(2)}, u32[]{:S(2)}) %collective-permute-start.2) | collective-permute-done | bytes 131104 | tf_op jit(solution)/shard_map/ppermute | solution.py:388
  46.5 0.5 shard_map.82
  47.0 15.0 %all_to_all.27.recv_ref = bf16[32,56,128]{2,1,0:T(8,128)(2,1)S(1)} all-to-all(bf16[32,56,128]{2,1,0:T(8,128)(2,1)S(1)} %shard_map.82), channel_id=1, replica_groups=mesh['dp'=4,'z'=2,'y'=4,'x'=4,'core'=2] {'z','y','x'}, dimensions={0} | all-to-all | bytes 917504 | tf_op jit(solution)/shard_map/all_to_all | solution.py:384
  62.0 0.4 shard_map.83
  62.4 14.0 %all_to_all.28.recv_ref = bf16[32,56,128]{2,1,0:T(8,128)(2,1)S(1)} all-to-all(bf16[32,56,128]{2,1,0:T(8,128)(2,1)S(1)} %get-tuple-element.41), channel_id=1, replica_groups=mesh['dp'=4,'z'=2,'y'=4,'x'=4,'core'=2] {'z','y','x'}, dimensions={0} | all-to-all | bytes 917504 | tf_op jit(solution)/shard_map/all_to_all | solution.py:384
  76.4 0.8 shard_map.87
  77.1 7.6 %all-to-all-start.4 = ((bf16[4,128,128]{2,1,0:T(8,128)(2,1)}), bf16[4,128,128]{2,1,0:T(8,128)(2,1)S(1)}, u32[]{:S(2)}, u32[]{:S(2)}) async-start(bf16[4,128,128]{2,1,0:T(8,128)(2,1)} %shard_map.87), calls=%async_computation.4 | async-start | bytes 262144 | tf_op jit(solution)/shard_map/all_to_all | solution.py:384
  84.7 0.4 shard_map.84
  85.1 0.1 collective-permute-start.3
  85.2 1.9 %shard_map.85.dpre_ref = bf16[24,64,1024]{2,1,0:T(8,128)(2,1)S(1)} custom-call(bf16[24,64,1024]{2,1,0:T(8,128)(2,1)} %get-tuple-element.43.slow_ref), custom_call_target="tpu_custom_call" | custom-call | tf_op jit(solution)/shard_map/pallas_call | solution.py:476
  87.1 2.1 %shard_map.86 = bf16[24,64,1024]{2,1,0:T(8,128)(2,1)} custom-call(bf16[24,64,1024]{2,1,0:T(8,128)(2,1)S(1)} %shard_map.85.dpre_ref, bf16[16,3,8,128]{3,2,1,0:T(8,128)(2,1)S(1)} %get-tuple-element.45.got_ref, bf16[16,3,8,128]{3,2,1,0:T(8,128)(2,1)S(1)} %collective-permute-done.3.other_ref, bf16[64,1024]{1,0:T(8,128)(2,1)S(1)} %get-tuple-element.37.tab_ref, ...), custom_call_target="tpu_custom_call" | custom-call | tf_op jit(solution)/shard_map/pallas_call | solution.py:485
  89.3 3.9 %all-to-all-done.4.fact_ref = bf16[4,128,128]{2,1,0:T(8,128)(2,1)S(1)} async-done(((bf16[4,128,128]{2,1,0:T(8,128)(2,1)}), bf16[4,128,128]{2,1,0:T(8,128)(2,1)S(1)}, u32[]{:S(2)}, u32[]{:S(2)}) %all-to-all-start.4) | async-done | bytes 131104 | tf_op jit(solution)/shard_map/all_to_all | solution.py:384
  93.2 1.5 %shard_map.88 = (f32[16,2,64,64]{3,2,1,0:T(8,128)}, f32[64,64]{1,0:T(8,128)}) custom-call(bf16[4,128,128]{2,1,0:T(8,128)(2,1)S(1)} %all-to-all-done.4.fact_ref), custom_call_target="tpu_custom_call" | custom-call | tf_op jit(solution)/shard_map/pallas_call | solution.py:493
  (5 shorter events, 0.1 us)
Async XLA Ops:
  0.6 39.5 %copy-start = (bf16[3,8,64,1024]{3,2,1,0:T(8,128)(2,1)S(1)}, bf16[3,8,64,1024]{3,2,1,0:T(8,128)(2,1)}, u32[]{:S(2)}) copy-start(bf16[3,8,64,1024]{3,2,1,0:T(8,128)(2,1)} %param.6) | copy-start | bytes 9437188
  3.8 1.5 %collective-permute-start = (bf16[16,3,8,128]{3,2,1,0:T(8,128)(2,1)S(1)}, bf16[16,3,8,128]{3,2,1,0:T(8,128)(2,1)S(1)}, u32[]{:S(2)}, u32[]{:S(2)}) collective-permute-start(bf16[16,3,8,128]{3,2,1,0:T(8,128)(2,1)S(1)} %get-tuple-element.29), channel_id=1, source_target_pairs={{0,1},{1,0},{2,3},{3,2},{4,5},{5,4},{6,7},{7,6},{8,9},{9,8},{10,11... | collective-permute-start | bytes 294920 | tf_op jit(solution)/shard_map/ppermute | solution.py:388
  38.7 1.4 %collective-permute-start.1 = (bf16[16,3,8,128]{3,2,1,0:T(8,128)(2,1)S(1)}, bf16[16,3,8,128]{3,2,1,0:T(8,128)(2,1)S(1)}, u32[]{:S(2)}, u32[]{:S(2)}) collective-permute-start(bf16[16,3,8,128]{3,2,1,0:T(8,128)(2,1)S(1)} %get-tuple-element.36), channel_id=1, source_target_pairs={{0,1},{1,0},{2,3},{3,2},{4,5},{5,4},{6,7},{7,6},{8,9},{9,8},{10,11... | collective-permute-start | bytes 294920 | tf_op jit(solution)/shard_map/ppermute | solution.py:388
  45.1 1.4 %collective-permute-start.2 = (bf16[16,4,8,128]{3,2,1,0:T(8,128)(2,1)S(1)}, bf16[16,4,8,128]{3,2,1,0:T(8,128)(2,1)S(1)}, u32[]{:S(2)}, u32[]{:S(2)}) collective-permute-start(bf16[16,4,8,128]{3,2,1,0:T(8,128)(2,1)S(1)} %get-tuple-element.40), channel_id=1, source_target_pairs={{0,1},{1,0},{2,3},{3,2},{4,5},{5,4},{6,7},{7,6},{8,9},{9,8},{10,11... | collective-permute-start | bytes 393224 | tf_op jit(solution)/shard_map/ppermute | solution.py:388
  77.1 16.1 %all-to-all-start.4 = ((bf16[4,128,128]{2,1,0:T(8,128)(2,1)}), bf16[4,128,128]{2,1,0:T(8,128)(2,1)S(1)}, u32[]{:S(2)}, u32[]{:S(2)}) async-start(bf16[4,128,128]{2,1,0:T(8,128)(2,1)} %shard_map.87), calls=%async_computation.4 | async-start | bytes 262144 | tf_op jit(solution)/shard_map/all_to_all | solution.py:384
  85.1 2.0 %collective-permute-start.3 = (bf16[16,3,8,128]{3,2,1,0:T(8,128)(2,1)S(1)}, bf16[16,3,8,128]{3,2,1,0:T(8,128)(2,1)S(1)}, u32[]{:S(2)}, u32[]{:S(2)}) collective-permute-start(bf16[16,3,8,128]{3,2,1,0:T(8,128)(2,1)S(1)} %get-tuple-element.42), channel_id=1, source_target_pairs={{0,1},{1,0},{2,3},{3,2},{4,5},{5,4},{6,7},{7,6},{8,9},{9,8},{10,11... | collective-permute-start | bytes 294920 | tf_op jit(solution)/shard_map/ppermute | solution.py:388

commit v10 on v9

--- a/solution.py
+++ b/solution.py
@@ -159,16 +159,8 @@
     copies[1].wait()
 
 
-def weight_kernel(w_ref, o_ref, scratch, sems):
-    copies = []
-    for part in range(4):
-        modes = pl.ds(4 * part, 4)
-        copies.append(pltpu.make_async_copy(w_ref.at[modes], scratch.at[modes], sems.at[part]))
-        copies[part].start()
-    for part in range(4):
-        copies[part].wait()
-        modes = slice(4 * part, 4 * part + 4)
-        o_ref[modes] = jnp.concatenate([scratch[modes, 0], scratch[modes, 1]], axis=2).astype(BF16)
+def weight_kernel(w_ref, o_ref):
+    o_ref[...] = jnp.concatenate([w_ref[:, 0], w_ref[:, 1]], axis=2).astype(BF16)
 
 
 def spread_kernel(own_ref, other_ref, tab_ref, o_ref, scratch, *point, rows):
@@ -431,13 +423,7 @@
         [rows, pltpu.SemaphoreType.DMA((5,))],
         limit=56,
     )(*(pltpu.with_memory_space_constraint(v, pltpu.HBM) for v in (fields, tab, point_weight)))
-    weights = call(
-        weight_kernel,
-        shape(16, 64, 128),
-        [SLOW],
-        FAST,
-        [pltpu.VMEM((16, 2, CHANNELS, CHANNELS), F32), pltpu.SemaphoreType.DMA((4,))],
-    )(pltpu.with_memory_space_constraint(spec_weight, pltpu.HBM))
+    weights = call(weight_kernel, shape(16, CHANNELS, 128), [FAST], FAST)(spec_weight)
     other, weights = lax.optimization_barrier((to_other_core(send), weights))
     got = exchange(spread(own, other, forward, PAIRS), CHIP)
     mixed, spectrum = call(

time: 95.4 us -> 94.6 us (level)
  Pallas kernels: 18.3 us -> 17.1 us
  waiting for transfers between devices: 6.43 us -> 7.56 us
    pallas_call x1, Pallas kernels: 1.34 us -> 0.14 us  [local(): call(weight_kernel, shape(16, CHANNELS, 128), [FAST], FAST)(spec_weight)]
    ppermute x4, waiting for transfers between devices: 2.49 us -> 3.62 us  [to_other_core(): return lax.ppermute(v, 'core', [(0, 1), (1, 0)])]
  transfers between devices with their start and end apart: 5 -> 5, of which waited for: 3 -> 4; matrix products, arithmetic and copies ran while one was open for 0% -> 0% of each run, Pallas kernels for 6% -> 5%
where the time goes in v10:
time: 94.6 us; the launch traced here: 93.9 us
  blocking collectives  60.4 us (64%)
  Pallas kernels  17.1 us (18%)
  starting transfers between devices  8.08 us (9%)
  waiting for transfers between devices  7.56 us (8%)
    all_to_all x4, blocking collectives, exchange(): return lax.all_to_all(v, axes, 0, 0, tiled=True)  60.4 us
    all_to_all x1, starting transfers between devices, exchange(): return lax.all_to_all(v, axes, 0, 0, tiled=True)  7.56 us
    pallas_call x1, Pallas kernels, local(): call(field_kernel, (pltpu.HBM((FIELDS, CHANNELS, DURATION), BF16), part4,...  4.94 us
    all_to_all x1, waiting for transfers between devices, exchange(): return lax.all_to_all(v, axes, 0, 0, tiled=True)  3.94 us
    ppermute x4, waiting for transfers between devices, to_other_core(): return lax.ppermute(v, 'core', [(0, 1), (1, 0)])  3.62 us
    pallas_call x1, Pallas kernels, local(): call(coeff_kernel, (pltpu.VMEM((16, 3, 8, 128), BF16), pltpu.VMEM((16, 3,...  3.15 us
    pallas_call x1, Pallas kernels, local(): call(grad_kernel, pltpu.HBM((FIELDS, CHANNELS, DURATION), BF16), [FAST] *...  2.14 us
    pallas_call x1, Pallas kernels, local(): call(fetch_kernel, pltpu.VMEM((FIELDS, CHANNELS, DURATION), BF16), [SLOW]...  1.9 us
  transfers between devices with their start and end apart: 5, of which 4 were waited for; matrix products, arithmetic and copies ran while one was open for 0% of the time, Pallas kernels for 5%

profile of v10, /device:TPU:32, one launch (start us, length us, event | category | flops | bytes accessed | tf_op | source)
XLA Modules:
  0.0 93.9 jit_solution(13842485418635119511)
XLA Ops:
  0.7 3.1 %shard_map.76 = (bf16[16,3,8,128]{3,2,1,0:T(8,128)(2,1)S(1)}, bf16[16,3,8,128]{3,2,1,0:T(8,128)(2,1)S(1)}, bf16[64,1024]{1,0:T(8,128)(2,1)S(1)}, bf16[64,64]{1,0...) custom-call(bf16[24,64,1024]{2,1,0:T(8,128)(2,1)} %bitcast.4, ...), custom_call_target="tpu_custom_call" | custom-call | tf_op jit(solution)/shard_map/pallas_call | solution.py:410
  3.8 0.1 collective-permute-start
  3.9 0.1 shard_map.77.w_ref
  4.1 1.1 %collective-permute-done.other_ref = bf16[16,3,8,128]{3,2,1,0:T(8,128)(2,1)S(1)} collective-permute-done((bf16[16,3,8,128]{3,2,1,0:T(8,128)(2,1)S(1)}, bf16[16,3,8,128]{3,2,1,0:T(8,128)(2,1)S(1)}, u32[]{:S(2)}, u32[]{:S(2)}) %collective-permute-start) | collective-permute-done | bytes 98336 | tf_op jit(solution)/shard_map/ppermute | solution.py:380
  5.2 0.5 shard_map.78
  5.7 18.0 %all_to_all.25.recv_ref = bf16[32,48,128]{2,1,0:T(8,128)(2,1)S(1)} all-to-all(bf16[32,48,128]{2,1,0:T(8,128)(2,1)S(1)} %shard_map.78), channel_id=1, replica_groups=mesh['dp'=4,'z'=2,'y'=4,'x'=4,'core'=2] {'z','y','x'}, dimensions={0} | all-to-all | bytes 786432 | tf_op jit(solution)/shard_map/all_to_all | solution.py:376
  23.7 0.4 shard_map.79
  24.1 13.6 %all_to_all.26.recv_ref = bf16[32,48,128]{2,1,0:T(8,128)(2,1)S(1)} all-to-all(bf16[32,48,128]{2,1,0:T(8,128)(2,1)S(1)} %get-tuple-element.33), channel_id=1, replica_groups=mesh['dp'=4,'z'=2,'y'=4,'x'=4,'core'=2] {'z','y','x'}, dimensions={0} | all-to-all | bytes 786432 | tf_op jit(solution)/shard_map/all_to_all | solution.py:376
  37.7 0.5 shard_map.80
  38.3 1.3 %collective-permute-done.1.other_ref = bf16[16,3,8,128]{3,2,1,0:T(8,128)(2,1)S(1)} collective-permute-done((bf16[16,3,8,128]{3,2,1,0:T(8,128)(2,1)S(1)}, bf16[16,3,8,128]{3,2,1,0:T(8,128)(2,1)S(1)}, u32[]{:S(2)}, u32[]{:S(2)}) %collective-permute-start.1) | collective-permute-done | bytes 98336 | tf_op jit(solution)/shard_map/ppermute | solution.py:380
  39.6 4.9 %shard_map.81 = (bf16[24,64,1024]{2,1,0:T(8,128)(2,1)}, bf16[16,4,8,128]{3,2,1,0:T(8,128)(2,1)S(1)}, bf16[16,4,8,128]{3,2,1,0:T(8,128)(2,1)S(1)}) custom-call(bf16[24,64,1024]{2,1,0:T(8,128)(2,1)S(1)} %get-tuple-element.27.in_ref, bf16[24,64,1024]{2,1,0:T(8,128)(2,1)S(1)} %bitcast.3, bf16[16,3,8,128]{3,2,1,0:T(8,128)(2,1)S(1)} %get-tuple-element.35.got_ref, ...), custom_call_target="tpu_custom_call" | custom-call | tf_op jit(solution)/shard_map/pallas_call | solution.py:437
  44.5 0.2 collective-permute-start.2
  44.8 1.2 %collective-permute-done.2.other_ref = bf16[16,4,8,128]{3,2,1,0:T(8,128)(2,1)S(1)} collective-permute-done((bf16[16,4,8,128]{3,2,1,0:T(8,128)(2,1)S(1)}, bf16[16,4,8,128]{3,2,1,0:T(8,128)(2,1)S(1)}, u32[]{:S(2)}, u32[]{:S(2)}) %collective-permute-start.2) | collective-permute-done | bytes 131104 | tf_op jit(solution)/shard_map/ppermute | solution.py:380
  46.0 0.5 shard_map.82
  46.4 14.8 %all_to_all.27.recv_ref = bf16[32,56,128]{2,1,0:T(8,128)(2,1)S(1)} all-to-all(bf16[32,56,128]{2,1,0:T(8,128)(2,1)S(1)} %shard_map.82), channel_id=1, replica_groups=mesh['dp'=4,'z'=2,'y'=4,'x'=4,'core'=2] {'z','y','x'}, dimensions={0} | all-to-all | bytes 917504 | tf_op jit(solution)/shard_map/all_to_all | solution.py:376
  61.2 0.4 shard_map.83
  61.6 14.0 %all_to_all.28.recv_ref = bf16[32,56,128]{2,1,0:T(8,128)(2,1)S(1)} all-to-all(bf16[32,56,128]{2,1,0:T(8,128)(2,1)S(1)} %get-tuple-element.41), channel_id=1, replica_groups=mesh['dp'=4,'z'=2,'y'=4,'x'=4,'core'=2] {'z','y','x'}, dimensions={0} | all-to-all | bytes 917504 | tf_op jit(solution)/shard_map/all_to_all | solution.py:376
  75.6 0.8 shard_map.87
  76.4 7.6 %all-to-all-start.4 = ((bf16[4,128,128]{2,1,0:T(8,128)(2,1)}), bf16[4,128,128]{2,1,0:T(8,128)(2,1)S(1)}, u32[]{:S(2)}, u32[]{:S(2)}) async-start(bf16[4,128,128]{2,1,0:T(8,128)(2,1)} %shard_map.87), calls=%async_computation.4 | async-start | bytes 262144 | tf_op jit(solution)/shard_map/all_to_all | solution.py:376
  83.9 0.4 shard_map.84
  84.4 1.9 %shard_map.85.dpre_ref = bf16[24,64,1024]{2,1,0:T(8,128)(2,1)S(1)} custom-call(bf16[24,64,1024]{2,1,0:T(8,128)(2,1)} %get-tuple-element.43.slow_ref), custom_call_target="tpu_custom_call" | custom-call | tf_op jit(solution)/shard_map/pallas_call | solution.py:462
  86.4 2.1 %shard_map.86 = bf16[24,64,1024]{2,1,0:T(8,128)(2,1)} custom-call(bf16[24,64,1024]{2,1,0:T(8,128)(2,1)S(1)} %shard_map.85.dpre_ref, bf16[16,3,8,128]{3,2,1,0:T(8,128)(2,1)S(1)} %get-tuple-element.45.got_ref, bf16[16,3,8,128]{3,2,1,0:T(8,128)(2,1)S(1)} %collective-permute-done.3.other_ref, bf16[64,1024]{1,0:T(8,128)(2,1)S(1)} %get-tuple-element.37.tab_ref, ...), custom_call_target="tpu_custom_call" | custom-call | tf_op jit(solution)/shard_map/pallas_call | solution.py:471
  88.5 3.9 %all-to-all-done.4.fact_ref = bf16[4,128,128]{2,1,0:T(8,128)(2,1)S(1)} async-done(((bf16[4,128,128]{2,1,0:T(8,128)(2,1)}), bf16[4,128,128]{2,1,0:T(8,128)(2,1)S(1)}, u32[]{:S(2)}, u32[]{:S(2)}) %all-to-all-start.4) | async-done | bytes 131104 | tf_op jit(solution)/shard_map/all_to_all | solution.py:376
  92.4 1.5 %shard_map.88 = (f32[16,2,64,64]{3,2,1,0:T(8,128)}, f32[64,64]{1,0:T(8,128)}) custom-call(bf16[4,128,128]{2,1,0:T(8,128)(2,1)S(1)} %all-to-all-done.4.fact_ref), custom_call_target="tpu_custom_call" | custom-call | tf_op jit(solution)/shard_map/pallas_call | solution.py:479
  (7 shorter events, 0.2 us)
Async XLA Ops:
  0.6 3.3 %copy-start.1 = (f32[16,2,64,64]{3,2,1,0:T(8,128)S(1)}, f32[16,2,64,64]{3,2,1,0:T(8,128)}, u32[]{:S(2)}) copy-start(f32[16,2,64,64]{3,2,1,0:T(8,128)} %w_ref.1) | copy-start | bytes 1572868
  0.6 38.9 %copy-start = (bf16[3,8,64,1024]{3,2,1,0:T(8,128)(2,1)S(1)}, bf16[3,8,64,1024]{3,2,1,0:T(8,128)(2,1)}, u32[]{:S(2)}) copy-start(bf16[3,8,64,1024]{3,2,1,0:T(8,128)(2,1)} %param.6) | copy-start | bytes 9437188
  3.8 1.4 %collective-permute-start = (bf16[16,3,8,128]{3,2,1,0:T(8,128)(2,1)S(1)}, bf16[16,3,8,128]{3,2,1,0:T(8,128)(2,1)S(1)}, u32[]{:S(2)}, u32[]{:S(2)}) collective-permute-start(bf16[16,3,8,128]{3,2,1,0:T(8,128)(2,1)S(1)} %get-tuple-element.29), channel_id=1, source_target_pairs={{0,1},{1,0},{2,3},{3,2},{4,5},{5,4},{6,7},{7,6},{8,9},{9,8},{10,11... | collective-permute-start | bytes 294920 | tf_op jit(solution)/shard_map/ppermute | solution.py:380
  38.2 1.4 %collective-permute-start.1 = (bf16[16,3,8,128]{3,2,1,0:T(8,128)(2,1)S(1)}, bf16[16,3,8,128]{3,2,1,0:T(8,128)(2,1)S(1)}, u32[]{:S(2)}, u32[]{:S(2)}) collective-permute-start(bf16[16,3,8,128]{3,2,1,0:T(8,128)(2,1)S(1)} %get-tuple-element.36), channel_id=1, source_target_pairs={{0,1},{1,0},{2,3},{3,2},{4,5},{5,4},{6,7},{7,6},{8,9},{9,8},{10,11... | collective-permute-start | bytes 294920 | tf_op jit(solution)/shard_map/ppermute | solution.py:380
  44.5 1.4 %collective-permute-start.2 = (bf16[16,4,8,128]{3,2,1,0:T(8,128)(2,1)S(1)}, bf16[16,4,8,128]{3,2,1,0:T(8,128)(2,1)S(1)}, u32[]{:S(2)}, u32[]{:S(2)}) collective-permute-start(bf16[16,4,8,128]{3,2,1,0:T(8,128)(2,1)S(1)} %get-tuple-element.40), channel_id=1, source_target_pairs={{0,1},{1,0},{2,3},{3,2},{4,5},{5,4},{6,7},{7,6},{8,9},{9,8},{10,11... | collective-permute-start | bytes 393224 | tf_op jit(solution)/shard_map/ppermute | solution.py:380
  76.4 16.1 %all-to-all-start.4 = ((bf16[4,128,128]{2,1,0:T(8,128)(2,1)}), bf16[4,128,128]{2,1,0:T(8,128)(2,1)S(1)}, u32[]{:S(2)}, u32[]{:S(2)}) async-start(bf16[4,128,128]{2,1,0:T(8,128)(2,1)} %shard_map.87), calls=%async_computation.4 | async-start | bytes 262144 | tf_op jit(solution)/shard_map/all_to_all | solution.py:376
  84.3 2.0 %collective-permute-start.3 = (bf16[16,3,8,128]{3,2,1,0:T(8,128)(2,1)S(1)}, bf16[16,3,8,128]{3,2,1,0:T(8,128)(2,1)S(1)}, u32[]{:S(2)}, u32[]{:S(2)}) collective-permute-start(bf16[16,3,8,128]{3,2,1,0:T(8,128)(2,1)S(1)} %get-tuple-element.42), channel_id=1, source_target_pairs={{0,1},{1,0},{2,3},{3,2},{4,5},{5,4},{6,7},{7,6},{8,9},{9,8},{10,11... | collective-permute-start | bytes 294920 | tf_op jit(solution)/shard_map/ppermute | solution.py:380
